TPU v7x, 128 devices: a whole 4x4x4 slice. The times are simulated.
128 devices in a mesh: tm: 8 (over x_hi, y), space: 16 (over z, x_lo, core).
Axes of the slice: x: 4 (x_hi: 2, x_lo: 2; x = x_hi * 2 + x_lo), y: 4, z: 4, core: 2. Of those that a mesh axis runs over, the one named last changes fastest.
Arguments:
- initial: float32 [32, 256, 512], P('space'), may hold values from -6 to 6
- c_values: float32 [16, 32, 256, 512], P('tm', 'space'), may hold values from -6 to 6
- forcing: float32 [32, 256, 512], P('space'), may hold values from -0.6 to 0.6
- classes: int32 [32, 256, 512], P('space'), may hold values from 0 to 7
- diffusion: float32 [8], replicated, may hold values from 0.01 to 0.04
- drift: float32 [3, 8], replicated, may hold values from -1 to 1
Outputs:
- updated: float32 [16, 32, 256, 512], P('tm', 'space')
- residual: float32 [16, 32, 256, 512], P('tm', 'space')
All inputs are finite; a program needn't handle non-finite values.
Results may differ from a plain program's by a relative error of at most 0.00002.
Values sent between devices are 32-bit elements; how exact they have to be, the bound alone decides.
No kernel may reach another device: no remote copies, remote signals or barrier semaphores. Data moves between devices by JAX's collectives and lax.ppermute only.
A program may use at most 192 MiB of HBM per device.

v0:
```python
import functools

import jax
import jax.numpy as jnp
import numpy as np
from jax import lax
from jax.experimental import pallas as pl
from jax.experimental.pallas import tpu as pltpu
from jax.sharding import Mesh, PartitionSpec as P

COARSEN = 4
XH, Y, SPACE = 2, 4, 16
XC = 4
ROWS = 4
HALO = 3
GROUP = Y * SPACE
TIMES = 2 * Y
ROW = (2, XC, SPACE, 128)


def rho(y, s):
    z, x, core = s >> 2, (s >> 1) & 1, s & 1
    chip = 4 * z + (y if z % 2 == 0 else 3 - y)
    return 2 * (chip if x == 0 else 31 - chip) + core


BLOCK_OF = [rho(j // SPACE, j % SPACE) for j in range(GROUP)]
DEVICE_AT = [BLOCK_OF.index(p) for p in range(GROUP)]
UP = [(DEVICE_AT[p], DEVICE_AT[(p + 1) % GROUP]) for p in range(GROUP)]
DOWN = [(j, i) for i, j in UP]
TM = ("xh", "y")
RING = ("y", "space")
VMEM = pl.BlockSpec(memory_space=pltpu.VMEM)
SMEM = pl.BlockSpec(memory_space=pltpu.SMEM)


def f32(*shape):
    return jax.ShapeDtypeStruct(shape, jnp.float32)


def call(kernel, outs, *args, flops=0, scalars=0):
    single = not isinstance(outs, (list, tuple))
    out_list = [outs] if single else list(outs)
    size = sum(int(np.prod(a.shape)) * 4 for a in list(args) + out_list)
    return pl.pallas_call(
        kernel,
        out_shape=outs,
        in_specs=[SMEM] * scalars + [VMEM] * (len(args) - scalars),
        out_specs=VMEM if single else [VMEM] * len(out_list),
        compiler_params=pltpu.CompilerParams(vmem_limit_bytes=24 << 20),
        cost_estimate=pl.CostEstimate(flops=flops, bytes_accessed=size, transcendentals=0),
    )(*args)


def lanes(c):
    return slice(c * 128, (c + 1) * 128)


def pack_kernel(field, send):
    for j in range(GROUP):
        top = ROWS * BLOCK_OF[j]
        for tt in range(2):
            for z in range(2):
                for c in range(XC):
                    send[j, tt, c, pl.ds(z, ROWS, stride=2), :] = field[tt, z, top : top + ROWS, lanes(c)]


def pack_shared_kernel(y_ref, initial, forcing, classes, send):
    for y in range(Y):

        @pl.when(y_ref[0] == y)
        def _():
            for s in range(SPACE):
                top = ROWS * rho(y, s)
                for n, ref in enumerate((initial, forcing, classes)):
                    for z in range(2):
                        for c in range(XC):
                            send[s, n, c, pl.ds(z, ROWS, stride=2), :] = ref[z, top : top + ROWS, lanes(c)].astype(jnp.float32)


def unpack_shared_kernel(recv, initial, forcing, classes, low, high):
    flat = recv.reshape(SPACE * 3 * XC * 8, 128)
    for row in range(ROWS):
        for par in range(2):
            for c in range(XC):
                for n, ref in enumerate((initial, forcing, classes)):
                    part = flat[pl.ds((n * XC + c) * 8 + row * 2 + par, SPACE, stride=3 * XC * 8), :]
                    ref[row, par, c] = part
                    if n > 0 and row < HALO:
                        low[n - 1, row, par, c] = part
                    if n > 0 and row >= ROWS - HALO:
                        high[n - 1, row - ROWS + HALO, par, c] = part


def unpack_kernel(recv, own, early, late, last):
    flat = recv.reshape(GROUP * 2 * XC * 8, 128)
    for y in range(Y):
        for tt in range(2):
            k = 2 * y + tt
            copy, at = (early, k) if k < 3 else (late, k - 3) if k < 7 else (last, 0)
            for row in range(ROWS):
                for par in range(2):
                    for c in range(XC):
                        first = ((y * SPACE * 2 + tt) * XC + c) * 8 + row * 2 + par
                        part = flat[pl.ds(first, SPACE, stride=2 * XC * 8), :]
                        own[k, row, par, c] = part
                        copy[at, row, par, c] = part


def return_pack_kernel(early, late, send):
    flat = send.reshape(GROUP * 2 * XC * 8, 128)
    for y in range(Y):
        for tt in range(2):
            k = 2 * y + tt
            for row in range(ROWS):
                for par in range(2):
                    for c in range(XC):
                        first = ((y * SPACE * 2 + tt) * XC + c) * 8 + row * 2 + par
                        flat[pl.ds(first, SPACE, stride=2 * XC * 8), :] = (early if k < 4 else late)[k % 4, row, par, c]


def return_kernel(recv, *refs):
    out = refs[-1]
    for j in range(GROUP):
        top = ROWS * BLOCK_OF[j]
        for tt in range(2):
            for z in range(2):
                for c in range(XC):
                    here = (tt, z, slice(top, top + ROWS), lanes(c))
                    part = recv[j, tt, c, pl.ds(z, ROWS, stride=2), :]
                    out[here] = part if len(refs) == 1 else refs[0][here] + part


def coefficient_kernel(tables, own, below, above, coef):
    for i in range(ROWS + 2 * HALO):
        ref, n, at = (below, 1, i) if i < HALO else (above, 1, i - HALO - ROWS) if i >= HALO + ROWS else (own, None, i - HALO)
        for par in range(2):
            for c in range(XC):
                piece = ref[at, par, c] if n is None else ref[n, at, par, c]
                label = piece.astype(jnp.int32)
                for t in range(8):
                    table = jnp.broadcast_to(tables[t : t + 1, :], label.shape)
                    coef[t, i, par, c] = jnp.take_along_axis(table, label, axis=1, mode="promise_in_bounds")


def x_shifts(v):
    lane = lax.broadcasted_iota(jnp.int32, v.shape, 2)
    before = pltpu.roll(v, 1, 2)
    after = pltpu.roll(v, 127, 2)
    before = jnp.where(lane == 0, jnp.concatenate([before[-1:], before[:-1]], 0), before)
    after = jnp.where(lane == 127, jnp.concatenate([after[1:], after[:1]], 0), after)
    return before, after


def sweep_row(coef, row, v, up, down, extra, coarse):
    at = HALO + row
    result = []
    for p in range(2):
        if p == 0:
            z_above, z_below = v[1], pltpu.roll(v[1], 1, 1)
        else:
            z_above, z_below = pltpu.roll(v[0], SPACE - 1, 1), v[0]
        before, after = x_shifts(v[p])
        total = coef[1, at, p] * z_above + coef[2, at, p] * z_below
        if up is not None:
            total = total + coef[3, at, p] * up[p]
        if down is not None:
            total = total + coef[4, at, p] * down[p]
        total = total + coef[5, at, p] * after + coef[6, at, p] * before
        if coarse:
            total = coef[7, at, p] * v[p] + COARSEN * total
        else:
            total = coef[0, at, p] * v[p] + total
        if extra is not None:
            total = total + extra[p]
        result.append(total)
    return result


def pair(ref, *at):
    return [ref[(*at, 0)], ref[(*at, 1)]]


def put(ref, at, value):
    for p in range(2):
        ref[(*at, p)] = value[p]


def fine_time(coef, force, own, below, above, target, out):
    rows = {i: pair(*own, i) for i in range(ROWS)}
    rows |= {i - ROWS: pair(*below, i) for i in range(ROWS)}
    rows |= {i + ROWS: pair(*above, i) for i in range(ROWS)}
    for step in range(COARSEN):
        reach = COARSEN - 1 - step
        rows = {
            i: sweep_row(coef, i, rows[i], rows[i + 1], rows[i - 1], force(i), False) for i in range(-reach, ROWS + reach)
        }
    for i in range(ROWS):
        goal = pair(*target, i)
        put(out[0], (*out[1:], i), [rows[i][p] - goal[p] for p in range(2)])


def forcing_rows(own, below, above):
    def at(i):
        return pair(below, 0, i + HALO) if i < 0 else pair(above, 0, i - ROWS) if i >= ROWS else pair(own, i)

    return at


def fine_early_kernel(coef, f, f_below, f_above, start, own, start_below, start_above, below, above, out):
    force = forcing_rows(f, f_below, f_above)
    fine_time(coef, force, (start,), (start_below,), (start_above,), (own, 0), (out, 0))

    @pl.loop(1, 4)
    def _(k):
        fine_time(coef, force, (own, k - 1), (below, k - 1), (above, k - 1), (own, k), (out, k))


def fine_late_kernel(coef, f, f_below, f_above, own, below, above, out):
    force = forcing_rows(f, f_below, f_above)

    @pl.loop(0, 4)
    def _(k):
        fine_time(coef, force, (own, k + 3), (below, k), (above, k), (own, k + 4), (out, k))


def trajectory(coef, r, first, width, start, low, high):
    rows = start
    for j in range(width):
        put(low, (j,), rows[0])
        put(high, (j,), rows[-1])
        if j + 1 < width:
            rows = [
                sweep_row(
                    coef, i, rows[i], rows[i + 1] if i + 1 < ROWS else None, rows[i - 1] if i else None,
                    pair(r, first + j, i), True,
                )
                for i in range(ROWS)
            ]


def advance(coef, r, first, width, start, below, above, store):
    rows = start
    dev_low, dev_high = {}, {}
    for j in range(width):
        under, over = pair(below, j), pair(above, j)
        if 1 in dev_low:
            under = [a + b for a, b in zip(under, dev_low[1])]
            over = [a + b for a, b in zip(over, dev_high[1])]
        padded = [under] + rows + [over]
        new_low, new_high = {}, {}
        for i in range(1, min(j + 1, width - j - 1) + 1):
            source_low = rows[0] if i == 1 else dev_low[i - 1]
            source_high = rows[-1] if i == 1 else dev_high[i - 1]
            if i <= j:
                new_low[i] = sweep_row(coef, -i, dev_low[i], source_low, dev_low.get(i + 1), None, True)
                new_high[i] = sweep_row(coef, ROWS - 1 + i, dev_high[i], dev_high.get(i + 1), source_high, None, True)
            else:
                new_low[i] = [COARSEN * coef[3, HALO - i, p] * source_low[p] for p in range(2)]
                new_high[i] = [COARSEN * coef[4, HALO + ROWS - 1 + i, p] * source_high[p] for p in range(2)]
        rows = [sweep_row(coef, i, padded[i + 1], padded[i + 2], padded[i], pair(r, first + j, i), True) for i in range(ROWS)]
        dev_low, dev_high = new_low, new_high
        for i in range(ROWS):
            put(store, (j, i), rows[i])
    return rows


def block(ref, *at):
    return [pair(ref, *at, i) for i in range(ROWS)]


def start_kernel(first, width, coef, r, start, low, high):
    trajectory(coef, r, first, width, block(start), low, high)


def middle_kernel(first, width, then, coef, r, r_next, start, below, above, errors, low, high):
    rows = advance(coef, r, first, width, block(start), below, above, errors)
    trajectory(coef, r_next, 0, then, rows, low, high)


def end_kernel(width, coef, r, start, below, above, errors):
    advance(coef, r, 0, width, block(start), below, above, errors)


def exchange(low, high):
    return lax.ppermute(high, RING, UP), lax.ppermute(low, RING, DOWN)


def coarse(coef, r_early, r_late, start, first):
    a, b = 4 - first, 4
    low, high = call(functools.partial(start_kernel, first, a), [f32(a, *ROW)] * 2, coef, r_early, start, flops=1 << 24)
    below, above = exchange(low, high)
    early, low, high = call(
        functools.partial(middle_kernel, first, a, b), [f32(a, ROWS, *ROW)] + [f32(b, *ROW)] * 2,
        coef, r_early, r_late, start, below, above, flops=1 << 25,
    )
    below, above = exchange(low, high)
    late = call(functools.partial(end_kernel, b), f32(b, ROWS, *ROW), coef, r_late, early[a - 1], below, above, flops=1 << 24)
    return early, late


def class_tables(diffusion, drift):
    a = diffusion
    bz, by, bx = a * drift[0], a * drift[1], a * drift[2]
    scale = jnp.float32(COARSEN)
    tables = jnp.stack([1.0 - 6.0 * a, a - bz, a + bz, a - by, a + by, a - bx, a + bx, 1.0 - 6.0 * (a * scale)])
    return jnp.pad(tables, ((0, 0), (0, 128 - tables.shape[1])))


def shards(initial, c_values, forcing, classes, diffusion, drift):
    xh, y = lax.axis_index("xh"), lax.axis_index("y")
    parcel = (2, XC, 8, 128)

    shared = call(pack_shared_kernel, f32(SPACE, 3, XC, 8, 128), y.reshape(1), initial, forcing, classes, scalars=1)
    shared = lax.all_to_all(shared, "space", 0, 0, tiled=True)
    send = call(pack_kernel, f32(GROUP, *parcel), c_values)
    recv = lax.all_to_all(send, RING, 0, 0, tiled=True)

    start, f, label, low, high = call(
        unpack_shared_kernel, [f32(ROWS, *ROW)] * 3 + [f32(2, HALO, *ROW)] * 2, shared
    )
    f_below, f_above = exchange(low, high)
    coef = call(coefficient_kernel, f32(8, ROWS + 2 * HALO, *ROW), class_tables(diffusion, drift), label, f_below, f_above)

    own, c_early, c_late, c_last = call(
        unpack_kernel, [f32(TIMES, ROWS, *ROW), f32(3, ROWS, *ROW), f32(4, ROWS, *ROW), f32(1, ROWS, *ROW)], recv
    )
    before = lax.ppermute(c_last, "xh", [(0, 1)])
    below_early, above_early = exchange(c_early, c_early)
    start = jnp.where(xh == 0, start, before[0])
    start_below, start_above = exchange(start, start)
    below_late, above_late = exchange(c_late, c_late)
    r_early = call(
        fine_early_kernel, f32(4, ROWS, *ROW),
        coef, f, f_below, f_above, start, own, start_below, start_above, below_early, above_early, flops=1 << 27,
    )
    r_late = call(
        fine_late_kernel, f32(4, ROWS, *ROW), coef, f, f_below, f_above, own, below_late, above_late, flops=1 << 27
    )

    early, late = coarse(coef, r_early, r_late, r_early[0], 1)
    carried = lax.ppermute(late[3], "xh", [(0, 1)])
    back = call(return_pack_kernel, f32(GROUP, *parcel), r_early, r_late)
    got = lax.all_to_all(back, RING, 0, 0, tiled=True)
    residual = call(return_kernel, f32(*c_values.shape), got)

    early, late = coarse(coef, r_early, r_late, carried, 0)
    back = call(return_pack_kernel, f32(GROUP, *parcel), early, late)
    got = lax.all_to_all(back, RING, 0, 0, tiled=True)
    updated = call(return_kernel, f32(*c_values.shape), got, c_values)
    return updated, residual


def solution(mesh):
    split = Mesh(np.asarray(mesh.devices).reshape(XH, Y, SPACE), ("xh", "y", "space"))
    return jax.shard_map(
        shards,
        mesh=split,
        in_specs=(P("space"), P(TM, "space"), P("space"), P("space"), P(), P()),
        out_specs=(P(TM, "space"), P(TM, "space")),
        check_vma=False,
    )
```

profile of v0, /device:TPU:5, one launch (start us, length us, event | category | flops | bytes accessed | tf_op | source)
XLA Modules:
  0.0 230.7 jit_solution(3208019738810593985)
XLA Ops:
  5.4 6.6 %all-to-all-start = ((f32[16,3,4,8,128]{4,3,2,1,0:T(8,128)}), f32[16,3,4,8,128]{4,3,2,1,0:T(8,128)S(1)}, u32[]{:S(2)}, u32[]{:S(2)}) async-start(f32[16,3,4,8,128]{4,3,2,1,0:T(8,128)} %copy-done.8), calls=%async_computation | async-start | bytes 1572864 | tf_op jit(solution)/shard_map/all_to_all | solution.py:315
  13.9 11.1 %all-to-all-done.recv = f32[16,3,4,8,128]{4,3,2,1,0:T(8,128)S(1)} async-done(((f32[16,3,4,8,128]{4,3,2,1,0:T(8,128)}), f32[16,3,4,8,128]{4,3,2,1,0:T(8,128)S(1)}, u32[]{:S(2)}, u32[]{:S(2)}) %all-to-all-start) | async-done | bytes 786464 | tf_op jit(solution)/shard_map/all_to_all | solution.py:315
  25.0 6.2 %all-to-all-start.1 = ((f32[64,2,4,8,128]{4,3,2,1,0:T(8,128)}), f32[64,2,4,8,128]{4,3,2,1,0:T(8,128)S(1)}, u32[]{:S(2)}, u32[]{:S(2)}) async-start(f32[64,2,4,8,128]{4,3,2,1,0:T(8,128)} %copy-done.5), calls=%async_computation.1 | async-start | bytes 4194304 | tf_op jit(solution)/shard_map/all_to_all | solution.py:317
  33.4 1.6 collective-permute-start
  35.0 25.7 %all-to-all-done.1.recv = f32[64,2,4,8,128]{4,3,2,1,0:T(8,128)S(1)} async-done(((f32[64,2,4,8,128]{4,3,2,1,0:T(8,128)}), f32[64,2,4,8,128]{4,3,2,1,0:T(8,128)S(1)}, u32[]{:S(2)}, u32[]{:S(2)}) %all-to-all-start.1) | async-done | bytes 2097184 | tf_op jit(solution)/shard_map/all_to_all | solution.py:317
  60.7 2.4 %shard_map.81 = (f32[8,4,2,4,16,128]{5,4,3,2,1,0:T(8,128)S(1)}, f32[3,4,2,4,16,128]{5,4,3,2,1,0:T(8,128)}, f32[4,4,2,4,16,128]{5,4,3,2,1,0:T(8,128)}, f32[1,4,2,4,16,128]{5,4,3,2,1,0:T(8,128)S(1)}) custom-call(f32[64,2,4,8,128]{4,3,2,1,0:T(8,128)S(1)} %all-to-all-done.1.recv), custom_call_target="tpu_custom_call" | custom-call | bytes 6291456 | tf_op jit(solution)/shard_map/pallas_call | solution.py:45
  66.3 1.7 collective-permute-start.1
  68.1 7.2 %collective-permute-done.2 = f32[1,4,2,4,16,128]{5,4,3,2,1,0:T(8,128)S(1)} collective-permute-done((f32[1,4,2,4,16,128]{5,4,3,2,1,0:T(8,128)S(1)}, f32[1,4,2,4,16,128]{5,4,3,2,1,0:T(8,128)S(1)}, u32[]{:S(2)}, u32[]{:S(2)}) %collective-permute-start.2) | collective-permute-done | bytes 262176 | tf_op jit(solution)/shard_map/ppermute | solution.py:328
  76.6 8.2 %collective-permute-done.1.above.f_above = f32[2,3,2,4,16,128]{5,4,3,2,1,0:T(8,128)S(1)} collective-permute-done((f32[2,3,2,4,16,128]{5,4,3,2,1,0:T(8,128)}, f32[2,3,2,4,16,128]{5,4,3,2,1,0:T(8,128)S(1)}, u32[]{:S(2)}, u32[]{:S(2)}) %collective-permute-start.1) | collective-permute-done | bytes 393248 | tf_op jit(solution)/shard_map/ppermute | solution.py:286
  84.9 4.2 %collective-permute-done.3.start_below = f32[4,2,4,16,128]{4,3,2,1,0:T(8,128)S(1)} collective-permute-done((f32[4,2,4,16,128]{4,3,2,1,0:T(8,128)S(1)}, f32[4,2,4,16,128]{4,3,2,1,0:T(8,128)S(1)}, u32[]{:S(2)}, u32[]{:S(2)}) %collective-permute-start.3) | collective-permute-done | bytes 262176 | tf_op jit(solution)/shard_map/ppermute | solution.py:286
  89.0 2.9 %collective-permute-start.4 = (f32[4,2,4,16,128]{4,3,2,1,0:T(8,128)S(1)}, f32[4,2,4,16,128]{4,3,2,1,0:T(8,128)S(1)}, u32[]{:S(2)}, u32[]{:S(2)}) collective-permute-start(f32[4,2,4,16,128]{4,3,2,1,0:T(8,128)S(1)} %bitcast_select_fusion.start), channel_id=1, source_target_pairs={{1,0},{16,1},{17,16},{32,17},{33,32},{48,33},{49,48},{52,49},{53,5... | collective-permute-start | bytes 786440 | tf_op jit(solution)/shard_map/ppermute | solution.py:286
  92.9 2.9 %shard_map.79.coef = f32[8,10,2,4,16,128]{5,4,3,2,1,0:T(8,128)S(1)} custom-call(f32[8,128]{1,0:T(8,128)S(1)} %pad.4.tables, f32[4,2,4,16,128]{4,3,2,1,0:T(8,128)S(1)} %copy-done.17, f32[2,3,2,4,16,128]{5,4,3,2,1,0:T(8,128)S(1)} %collective-permute-done.below.f_below, f32[2,3,2,4,16,128]{5,4,3,2,1,0:T(8,128)S(1)} %collective-permute-done.1.above.f_above), custom_call_target="tpu_custom_call" | custom-call | bytes 6295552 | tf_op jit(solution)/shard_map/pallas_call | solution.py:45
  100.0 6.0 %shard_map.82.r.early = f32[4,4,2,4,16,128]{5,4,3,2,1,0:T(8,128)S(1)} custom-call(f32[8,10,2,4,16,128]{5,4,3,2,1,0:T(8,128)S(1)} %shard_map.79.coef, f32[4,2,4,16,128]{4,3,2,1,0:T(8,128)S(1)} %get-tuple-element.24.f, f32[2,3,2,4,16,128]{5,4,3,2,1,0:T(8,128)S(1)} %collective-permute-done.below.f_below, ...), custom_call_target="tpu_custom_call" | custom-call | flops 134217728 | bytes 11796480 | tf_op jit(solution)/shard_map/pallas_call | solution.py:45
  106.0 6.4 %shard_map.83.r_next.r.late = f32[4,4,2,4,16,128]{5,4,3,2,1,0:T(8,128)S(1)} custom-call(f32[8,10,2,4,16,128]{5,4,3,2,1,0:T(8,128)S(1)} %shard_map.79.coef, f32[4,2,4,16,128]{4,3,2,1,0:T(8,128)S(1)} %get-tuple-element.24.f, f32[2,3,2,4,16,128]{5,4,3,2,1,0:T(8,128)S(1)} %collective-permute-done.below.f_below, ...), custom_call_target="tpu_custom_call" | custom-call | flops 134217728 | bytes 11534336 | tf_op jit(solution)/shard_map/pallas_call | solution.py:45
  112.5 1.7 shard_map.92
  115.5 5.6 %all-to-all-start.3 = ((f32[64,2,4,8,128]{4,3,2,1,0:T(8,128)}), f32[64,2,4,8,128]{4,3,2,1,0:T(8,128)}, u32[]{:S(2)}, u32[]{:S(2)}) async-start(f32[64,2,4,8,128]{4,3,2,1,0:T(8,128)} %copy-done.4), calls=%async_computation.3 | async-start | bytes 4194304 | tf_op jit(solution)/shard_map/all_to_all | solution.py:344
  121.1 2.5 %copy-done.1 = f32[8,10,2,4,16,128]{5,4,3,2,1,0:T(8,128)S(1)} copy-done((f32[8,10,2,4,16,128]{5,4,3,2,1,0:T(8,128)S(1)}, f32[8,10,2,4,16,128]{5,4,3,2,1,0:T(8,128)}, u32[]{:S(2)}) %copy-start.1) | copy-done | bytes 5242904
  123.9 1.7 collective-permute-start.9
  125.6 20.2 %collective-permute-done.9.below = f32[3,2,4,16,128]{4,3,2,1,0:T(8,128)S(1)} collective-permute-done((f32[3,2,4,16,128]{4,3,2,1,0:T(8,128)S(1)}, f32[3,2,4,16,128]{4,3,2,1,0:T(8,128)S(1)}, u32[]{:S(2)}, u32[]{:S(2)}) %collective-permute-start.9) | collective-permute-done | bytes 196640 | tf_op jit(solution)/shard_map/ppermute | solution.py:286
  145.8 2.2 collective-permute-done.10.above
  149.7 3.0 %collective-permute-done.11.below = f32[4,2,4,16,128]{4,3,2,1,0:T(8,128)S(1)} collective-permute-done((f32[4,2,4,16,128]{4,3,2,1,0:T(8,128)S(1)}, f32[4,2,4,16,128]{4,3,2,1,0:T(8,128)S(1)}, u32[]{:S(2)}, u32[]{:S(2)}) %collective-permute-start.11) | collective-permute-done | bytes 262176 | tf_op jit(solution)/shard_map/ppermute | solution.py:286
  152.8 2.5 %collective-permute-done.12.above = f32[4,2,4,16,128]{4,3,2,1,0:T(8,128)S(1)} collective-permute-done((f32[4,2,4,16,128]{4,3,2,1,0:T(8,128)S(1)}, f32[4,2,4,16,128]{4,3,2,1,0:T(8,128)S(1)}, u32[]{:S(2)}, u32[]{:S(2)}) %collective-permute-start.12) | collective-permute-done | bytes 262176 | tf_op jit(solution)/shard_map/ppermute | solution.py:286
  157.7 12.6 %collective-permute-done.13.start = f32[4,2,4,16,128]{4,3,2,1,0:T(8,128)S(1)} collective-permute-done((f32[4,2,4,16,128]{4,3,2,1,0:T(8,128)S(1)}, f32[4,2,4,16,128]{4,3,2,1,0:T(8,128)S(1)}, u32[]{:S(2)}, u32[]{:S(2)}) %collective-permute-start.13) | collective-permute-done | bytes 262176 | tf_op jit(solution)/shard_map/ppermute | solution.py:342
  171.5 2.6 %collective-permute-done.14.below = f32[4,2,4,16,128]{4,3,2,1,0:T(8,128)S(1)} collective-permute-done((f32[4,2,4,16,128]{4,3,2,1,0:T(8,128)S(1)}, f32[4,2,4,16,128]{4,3,2,1,0:T(8,128)S(1)}, u32[]{:S(2)}, u32[]{:S(2)}) %collective-permute-start.14) | collective-permute-done | bytes 262176 | tf_op jit(solution)/shard_map/ppermute | solution.py:286
  174.2 2.7 %collective-permute-done.15.above = f32[4,2,4,16,128]{4,3,2,1,0:T(8,128)S(1)} collective-permute-done((f32[4,2,4,16,128]{4,3,2,1,0:T(8,128)S(1)}, f32[4,2,4,16,128]{4,3,2,1,0:T(8,128)S(1)}, u32[]{:S(2)}, u32[]{:S(2)}) %collective-permute-start.15) | collective-permute-done | bytes 262176 | tf_op jit(solution)/shard_map/ppermute | solution.py:286
  178.8 2.8 %collective-permute-done.16.below = f32[4,2,4,16,128]{4,3,2,1,0:T(8,128)S(1)} collective-permute-done((f32[4,2,4,16,128]{4,3,2,1,0:T(8,128)S(1)}, f32[4,2,4,16,128]{4,3,2,1,0:T(8,128)S(1)}, u32[]{:S(2)}, u32[]{:S(2)}) %collective-permute-start.16) | collective-permute-done | bytes 262176 | tf_op jit(solution)/shard_map/ppermute | solution.py:286
  181.6 2.7 %collective-permute-done.17.above = f32[4,2,4,16,128]{4,3,2,1,0:T(8,128)S(1)} collective-permute-done((f32[4,2,4,16,128]{4,3,2,1,0:T(8,128)S(1)}, f32[4,2,4,16,128]{4,3,2,1,0:T(8,128)S(1)}, u32[]{:S(2)}, u32[]{:S(2)}) %collective-permute-start.17) | collective-permute-done | bytes 262176 | tf_op jit(solution)/shard_map/ppermute | solution.py:286
  185.2 3.0 %shard_map.90 = f32[64,2,4,8,128]{4,3,2,1,0:T(8,128)} custom-call(f32[4,4,2,4,16,128]{5,4,3,2,1,0:T(8,128)S(1)} %get-tuple-element.37.early, f32[4,4,2,4,16,128]{5,4,3,2,1,0:T(8,128)S(1)} %shard_map.89.late), custom_call_target="tpu_custom_call" | custom-call | bytes 4194304 | tf_op jit(solution)/shard_map/pallas_call | solution.py:45
  188.2 9.5 %all-to-all-start.2 = ((f32[64,2,4,8,128]{4,3,2,1,0:T(8,128)}), f32[64,2,4,8,128]{4,3,2,1,0:T(8,128)}, u32[]{:S(2)}, u32[]{:S(2)}) async-start(f32[64,2,4,8,128]{4,3,2,1,0:T(8,128)} %shard_map.90), calls=%async_computation.2 | async-start | bytes 4194304 | tf_op jit(solution)/shard_map/all_to_all | solution.py:349
  197.7 3.6 %shard_map.93 = f32[2,2,256,512]{3,2,1,0:T(8,128)} custom-call(f32[64,2,4,8,128]{4,3,2,1,0:T(8,128)} %all-to-all-done.3.recv), custom_call_target="tpu_custom_call" | custom-call | bytes 4194304 | tf_op jit(solution)/shard_map/pallas_call | solution.py:45
  201.3 25.7 %all-to-all-done.2.recv = f32[64,2,4,8,128]{4,3,2,1,0:T(8,128)} async-done(((f32[64,2,4,8,128]{4,3,2,1,0:T(8,128)}), f32[64,2,4,8,128]{4,3,2,1,0:T(8,128)}, u32[]{:S(2)}, u32[]{:S(2)}) %all-to-all-start.2) | async-done | bytes 2097184 | tf_op jit(solution)/shard_map/all_to_all | solution.py:349
  227.1 3.7 %shard_map.91 = f32[2,2,256,512]{3,2,1,0:T(8,128)} custom-call(f32[64,2,4,8,128]{4,3,2,1,0:T(8,128)} %all-to-all-done.2.recv, f32[2,2,256,512]{3,2,1,0:T(8,128)S(1)} %copy-done.3), custom_call_target="tpu_custom_call" | custom-call | bytes 6291456 | tf_op jit(solution)/shard_map/pallas_call | solution.py:45
  (77 shorter events, 28.1 us)
Async XLA Ops:
  4.3 7.7 %copy-start.2 = (f32[2,2,256,512]{3,2,1,0:T(8,128)S(1)}, f32[2,2,256,512]{3,2,1,0:T(8,128)}, u32[]{:S(2)}) copy-start(f32[2,2,256,512]{3,2,1,0:T(8,128)} %refs_0_.1) | copy-start | bytes 6291460
  5.4 19.6 %all-to-all-start = ((f32[16,3,4,8,128]{4,3,2,1,0:T(8,128)}), f32[16,3,4,8,128]{4,3,2,1,0:T(8,128)S(1)}, u32[]{:S(2)}, u32[]{:S(2)}) async-start(f32[16,3,4,8,128]{4,3,2,1,0:T(8,128)} %copy-done.8), calls=%async_computation | async-start | bytes 1572864 | tf_op jit(solution)/shard_map/all_to_all | solution.py:315
  12.6 1.3 copy-start.5
  25.0 35.7 %all-to-all-start.1 = ((f32[64,2,4,8,128]{4,3,2,1,0:T(8,128)}), f32[64,2,4,8,128]{4,3,2,1,0:T(8,128)S(1)}, u32[]{:S(2)}, u32[]{:S(2)}) async-start(f32[64,2,4,8,128]{4,3,2,1,0:T(8,128)} %copy-done.5), calls=%async_computation.1 | async-start | bytes 4194304 | tf_op jit(solution)/shard_map/all_to_all | solution.py:317
  31.3 60.6 %copy-start.18 = (f32[3,8]{1,0:T(4,128)S(1)}, f32[3,8]{1,0:T(4,128)}, u32[]{:S(2)}) copy-start(f32[3,8]{1,0:T(4,128)} %param.11) | copy-start | bytes 292
  31.3 60.6 %copy-start.19 = (f32[8]{0:T(128)S(1)}, f32[8]{0:T(128)}, u32[]{:S(2)}) copy-start(f32[8]{0:T(128)} %param.10) | copy-start | bytes 100
  33.4 34.6 %collective-permute-start = (f32[2,3,2,4,16,128]{5,4,3,2,1,0:T(8,128)}, f32[2,3,2,4,16,128]{5,4,3,2,1,0:T(8,128)S(1)}, u32[]{:S(2)}, u32[]{:S(2)}) collective-permute-start(f32[2,3,2,4,16,128]{5,4,3,2,1,0:T(8,128)} %get-tuple-element.22), channel_id=1, source_target_pairs={{0,1},{1,16},{16,17},{17,32},{32,33},{33,48},{48,49},{49,52},{52,5... | collective-permute-start | bytes 1179656 | tf_op jit(solution)/shard_map/ppermute | solution.py:286
  64.5 10.9 %collective-permute-start.2 = (f32[1,4,2,4,16,128]{5,4,3,2,1,0:T(8,128)S(1)}, f32[1,4,2,4,16,128]{5,4,3,2,1,0:T(8,128)S(1)}, u32[]{:S(2)}, u32[]{:S(2)}) collective-permute-start(f32[1,4,2,4,16,128]{5,4,3,2,1,0:T(8,128)S(1)} %get-tuple-element.26), channel_id=1, source_target_pairs={{0,64},{1,65},{2,66},{3,67},{4,68},{5,69},{6,70},{7,71},{8,72},{9,... | collective-permute-start | bytes 786440 | tf_op jit(solution)/shard_map/ppermute | solution.py:328
  65.8 40.2 %collective-permute-start.7 = (f32[4,4,2,4,16,128]{5,4,3,2,1,0:T(8,128)}, f32[4,4,2,4,16,128]{5,4,3,2,1,0:T(8,128)}, u32[]{:S(2)}, u32[]{:S(2)}) collective-permute-start(f32[4,4,2,4,16,128]{5,4,3,2,1,0:T(8,128)} %get-tuple-element.29), channel_id=1, source_target_pairs={{0,1},{1,16},{16,17},{17,32},{32,33},{33,48},{48,49},{49,52},{52,5... | collective-permute-start | bytes 3145736 | tf_op jit(solution)/shard_map/ppermute | solution.py:286
  65.8 40.2 %collective-permute-start.8 = (f32[4,4,2,4,16,128]{5,4,3,2,1,0:T(8,128)}, f32[4,4,2,4,16,128]{5,4,3,2,1,0:T(8,128)}, u32[]{:S(2)}, u32[]{:S(2)}) collective-permute-start(f32[4,4,2,4,16,128]{5,4,3,2,1,0:T(8,128)} %get-tuple-element.29), channel_id=1, source_target_pairs={{1,0},{16,1},{17,16},{32,17},{33,32},{48,33},{49,48},{52,49},{53,5... | collective-permute-start | bytes 3145736 | tf_op jit(solution)/shard_map/ppermute | solution.py:286
  66.3 18.5 %collective-permute-start.1 = (f32[2,3,2,4,16,128]{5,4,3,2,1,0:T(8,128)}, f32[2,3,2,4,16,128]{5,4,3,2,1,0:T(8,128)S(1)}, u32[]{:S(2)}, u32[]{:S(2)}) collective-permute-start(f32[2,3,2,4,16,128]{5,4,3,2,1,0:T(8,128)} %get-tuple-element.23), channel_id=1, source_target_pairs={{1,0},{16,1},{17,16},{32,17},{33,32},{48,33},{49,48},{52,49},{53,5... | collective-permute-start | bytes 1179656 | tf_op jit(solution)/shard_map/ppermute | solution.py:286
  68.0 28.5 %collective-permute-start.5 = (f32[3,4,2,4,16,128]{5,4,3,2,1,0:T(8,128)}, f32[3,4,2,4,16,128]{5,4,3,2,1,0:T(8,128)S(1)}, u32[]{:S(2)}, u32[]{:S(2)}) collective-permute-start(f32[3,4,2,4,16,128]{5,4,3,2,1,0:T(8,128)} %get-tuple-element.28), channel_id=1, source_target_pairs={{0,1},{1,16},{16,17},{17,32},{32,33},{33,48},{48,49},{49,52},{52,5... | collective-permute-start | bytes 2359304 | tf_op jit(solution)/shard_map/ppermute | solution.py:286
  75.3 22.5 %collective-permute-start.6 = (f32[3,4,2,4,16,128]{5,4,3,2,1,0:T(8,128)}, f32[3,4,2,4,16,128]{5,4,3,2,1,0:T(8,128)}, u32[]{:S(2)}, u32[]{:S(2)}) collective-permute-start(f32[3,4,2,4,16,128]{5,4,3,2,1,0:T(8,128)} %get-tuple-element.28), channel_id=1, source_target_pairs={{1,0},{16,1},{17,16},{32,17},{33,32},{48,33},{49,48},{52,49},{53,5... | collective-permute-start | bytes 2359304 | tf_op jit(solution)/shard_map/ppermute | solution.py:286
  84.9 4.2 %collective-permute-start.3 = (f32[4,2,4,16,128]{4,3,2,1,0:T(8,128)S(1)}, f32[4,2,4,16,128]{4,3,2,1,0:T(8,128)S(1)}, u32[]{:S(2)}, u32[]{:S(2)}) collective-permute-start(f32[4,2,4,16,128]{4,3,2,1,0:T(8,128)S(1)} %bitcast_select_fusion.start), channel_id=1, source_target_pairs={{0,1},{1,16},{16,17},{17,32},{32,33},{33,48},{48,49},{49,52},{52,5... | collective-permute-start | bytes 786440 | tf_op jit(solution)/shard_map/ppermute | solution.py:286
  89.0 6.8 %collective-permute-start.4 = (f32[4,2,4,16,128]{4,3,2,1,0:T(8,128)S(1)}, f32[4,2,4,16,128]{4,3,2,1,0:T(8,128)S(1)}, u32[]{:S(2)}, u32[]{:S(2)}) collective-permute-start(f32[4,2,4,16,128]{4,3,2,1,0:T(8,128)S(1)} %bitcast_select_fusion.start), channel_id=1, source_target_pairs={{1,0},{16,1},{17,16},{32,17},{33,32},{48,33},{49,48},{52,49},{53,5... | collective-permute-start | bytes 786440 | tf_op jit(solution)/shard_map/ppermute | solution.py:286
  92.9 5.0 %copy-start.7 = (f32[8,4,2,4,16,128]{5,4,3,2,1,0:T(8,128)S(1)}, f32[8,4,2,4,16,128]{5,4,3,2,1,0:T(8,128)}, u32[]{:S(2)}) copy-start(f32[8,4,2,4,16,128]{5,4,3,2,1,0:T(8,128)} %copy-done.6) | copy-start | bytes 6291460
  95.8 10.2 %copy-start = (f32[8,10,2,4,16,128]{5,4,3,2,1,0:T(8,128)}, f32[8,10,2,4,16,128]{5,4,3,2,1,0:T(8,128)S(1)}, u32[]{:S(2)}) copy-start(f32[8,10,2,4,16,128]{5,4,3,2,1,0:T(8,128)S(1)} %shard_map.79.coef) | copy-start | bytes 15728644
  96.5 1.3 copy-start.12
  114.2 1.3 copy-start.4
  115.5 72.7 %all-to-all-start.3 = ((f32[64,2,4,8,128]{4,3,2,1,0:T(8,128)}), f32[64,2,4,8,128]{4,3,2,1,0:T(8,128)}, u32[]{:S(2)}, u32[]{:S(2)}) async-start(f32[64,2,4,8,128]{4,3,2,1,0:T(8,128)} %copy-done.4), calls=%async_computation.3 | async-start | bytes 4194304 | tf_op jit(solution)/shard_map/all_to_all | solution.py:344
  121.1 2.5 %copy-start.1 = (f32[8,10,2,4,16,128]{5,4,3,2,1,0:T(8,128)S(1)}, f32[8,10,2,4,16,128]{5,4,3,2,1,0:T(8,128)}, u32[]{:S(2)}) copy-start(f32[8,10,2,4,16,128]{5,4,3,2,1,0:T(8,128)} %copy-done) | copy-start | bytes 15728644
  123.9 21.9 %collective-permute-start.9 = (f32[3,2,4,16,128]{4,3,2,1,0:T(8,128)S(1)}, f32[3,2,4,16,128]{4,3,2,1,0:T(8,128)S(1)}, u32[]{:S(2)}, u32[]{:S(2)}) collective-permute-start(f32[3,2,4,16,128]{4,3,2,1,0:T(8,128)S(1)} %get-tuple-element.30), channel_id=1, source_target_pairs={{0,1},{1,16},{16,17},{17,32},{32,33},{33,48},{48,49},{49,52},{52,5... | collective-permute-start | bytes 589832 | tf_op jit(solution)/shard_map/ppermute | solution.py:286
  125.6 22.4 %collective-permute-start.10 = (f32[3,2,4,16,128]{4,3,2,1,0:T(8,128)S(1)}, f32[3,2,4,16,128]{4,3,2,1,0:T(8,128)S(1)}, u32[]{:S(2)}, u32[]{:S(2)}) collective-permute-start(f32[3,2,4,16,128]{4,3,2,1,0:T(8,128)S(1)} %get-tuple-element.31), channel_id=1, source_target_pairs={{1,0},{16,1},{17,16},{32,17},{33,32},{48,33},{49,48},{52,49},{53,5... | collective-permute-start | bytes 589832 | tf_op jit(solution)/shard_map/ppermute | solution.py:286
  149.1 3.6 %collective-permute-start.11 = (f32[4,2,4,16,128]{4,3,2,1,0:T(8,128)S(1)}, f32[4,2,4,16,128]{4,3,2,1,0:T(8,128)S(1)}, u32[]{:S(2)}, u32[]{:S(2)}) collective-permute-start(f32[4,2,4,16,128]{4,3,2,1,0:T(8,128)S(1)} %get-tuple-element.33), channel_id=1, source_target_pairs={{0,1},{1,16},{16,17},{17,32},{32,33},{33,48},{48,49},{49,52},{52,5... | collective-permute-start | bytes 786440 | tf_op jit(solution)/shard_map/ppermute | solution.py:286
  149.4 5.8 %collective-permute-start.12 = (f32[4,2,4,16,128]{4,3,2,1,0:T(8,128)S(1)}, f32[4,2,4,16,128]{4,3,2,1,0:T(8,128)S(1)}, u32[]{:S(2)}, u32[]{:S(2)}) collective-permute-start(f32[4,2,4,16,128]{4,3,2,1,0:T(8,128)S(1)} %get-tuple-element.34), channel_id=1, source_target_pairs={{1,0},{16,1},{17,16},{32,17},{33,32},{48,33},{49,48},{52,49},{53,5... | collective-permute-start | bytes 786440 | tf_op jit(solution)/shard_map/ppermute | solution.py:286
  156.2 14.1 %collective-permute-start.13 = (f32[4,2,4,16,128]{4,3,2,1,0:T(8,128)S(1)}, f32[4,2,4,16,128]{4,3,2,1,0:T(8,128)S(1)}, u32[]{:S(2)}, u32[]{:S(2)}) collective-permute-start(f32[4,2,4,16,128]{4,3,2,1,0:T(8,128)S(1)} %slice_bitcast_fusion), channel_id=1, source_target_pairs={{0,64},{1,65},{2,66},{3,67},{4,68},{5,69},{6,70},{7,71},{8,72},{9,... | collective-permute-start | bytes 786440 | tf_op jit(solution)/shard_map/ppermute | solution.py:342
  170.8 3.4 %collective-permute-start.14 = (f32[4,2,4,16,128]{4,3,2,1,0:T(8,128)S(1)}, f32[4,2,4,16,128]{4,3,2,1,0:T(8,128)S(1)}, u32[]{:S(2)}, u32[]{:S(2)}) collective-permute-start(f32[4,2,4,16,128]{4,3,2,1,0:T(8,128)S(1)} %get-tuple-element.35), channel_id=1, source_target_pairs={{0,1},{1,16},{16,17},{17,32},{32,33},{33,48},{48,49},{49,52},{52,5... | collective-permute-start | bytes 786440 | tf_op jit(solution)/shard_map/ppermute | solution.py:286
  170.8 6.0 %collective-permute-start.15 = (f32[4,2,4,16,128]{4,3,2,1,0:T(8,128)S(1)}, f32[4,2,4,16,128]{4,3,2,1,0:T(8,128)S(1)}, u32[]{:S(2)}, u32[]{:S(2)}) collective-permute-start(f32[4,2,4,16,128]{4,3,2,1,0:T(8,128)S(1)} %get-tuple-element.36), channel_id=1, source_target_pairs={{1,0},{16,1},{17,16},{32,17},{33,32},{48,33},{49,48},{52,49},{53,5... | collective-permute-start | bytes 786440 | tf_op jit(solution)/shard_map/ppermute | solution.py:286
  178.2 3.4 %collective-permute-start.16 = (f32[4,2,4,16,128]{4,3,2,1,0:T(8,128)S(1)}, f32[4,2,4,16,128]{4,3,2,1,0:T(8,128)S(1)}, u32[]{:S(2)}, u32[]{:S(2)}) collective-permute-start(f32[4,2,4,16,128]{4,3,2,1,0:T(8,128)S(1)} %get-tuple-element.38), channel_id=1, source_target_pairs={{0,1},{1,16},{16,17},{17,32},{32,33},{33,48},{48,49},{49,52},{52,5... | collective-permute-start | bytes 786440 | tf_op jit(solution)/shard_map/ppermute | solution.py:286
  178.2 6.0 %collective-permute-start.17 = (f32[4,2,4,16,128]{4,3,2,1,0:T(8,128)S(1)}, f32[4,2,4,16,128]{4,3,2,1,0:T(8,128)S(1)}, u32[]{:S(2)}, u32[]{:S(2)}) collective-permute-start(f32[4,2,4,16,128]{4,3,2,1,0:T(8,128)S(1)} %get-tuple-element.39), channel_id=1, source_target_pairs={{1,0},{16,1},{17,16},{32,17},{33,32},{48,33},{49,48},{52,49},{53,5... | collective-permute-start | bytes 786440 | tf_op jit(solution)/shard_map/ppermute | solution.py:286
  188.2 38.9 %all-to-all-start.2 = ((f32[64,2,4,8,128]{4,3,2,1,0:T(8,128)}), f32[64,2,4,8,128]{4,3,2,1,0:T(8,128)}, u32[]{:S(2)}, u32[]{:S(2)}) async-start(f32[64,2,4,8,128]{4,3,2,1,0:T(8,128)} %shard_map.90), calls=%async_computation.2 | async-start | bytes 4194304 | tf_op jit(solution)/shard_map/all_to_all | solution.py:349
  197.7 29.4 %copy-start.3 = (f32[2,2,256,512]{3,2,1,0:T(8,128)S(1)}, f32[2,2,256,512]{3,2,1,0:T(8,128)}, u32[]{:S(2)}) copy-start(f32[2,2,256,512]{3,2,1,0:T(8,128)} %refs_0_.1) | copy-start | bytes 6291460
  (10 other events, 10.4 us)
where the time goes:
time: 232 us; the launch traced here: 231 us
  waiting for transfers between devices  134 us (58%)
  starting transfers between devices  42.5 us (18%)
  Pallas kernels  36.8 us (16%)
  local copies, waits for them, and re-layouts  16.9 us (7%)
    ppermute x16, waiting for transfers between devices, exchange(): return (lax.ppermute(high, RING, UP), lax.ppermute(low, RING, DOWN))  51.2 us
    pallas_call x17, Pallas kernels, call(): pl.pallas_call(kernel, out_shape=outs, in_specs=[SMEM] * scalars + [VMEM]...  36.8 us
    all_to_all x2, waiting for transfers between devices, shards(): got = lax.all_to_all(back, RING, 0, 0, tiled=True)  25.7 us
    all_to_all x1, waiting for transfers between devices, shards(): recv = lax.all_to_all(send, RING, 0, 0, tiled=True)  25.7 us
    unnamed x40, local copies, waits for them, and re-layouts  16.8 us
    all_to_all x2, starting transfers between devices, shards(): got = lax.all_to_all(back, RING, 0, 0, tiled=True)  15.1 us
    ppermute x1, waiting for transfers between devices, shards(): carried = lax.ppermute(late[3], 'xh', [(0, 1)])  12.6 us
    ppermute x16, starting transfers between devices, exchange(): return (lax.ppermute(high, RING, UP), lax.ppermute(low, RING, DOWN))  11.7 us
  transfers between devices with their start and end apart: 22, of which 15 were waited for; matrix products, arithmetic and copies ran while one was open for 0% of the time, Pallas kernels for 11%

commit v1 on v0

v1 whole, which is shorter than its diff:
```python
import functools

import jax
import jax.numpy as jnp
import numpy as np
from jax import lax
from jax.experimental import pallas as pl
from jax.experimental.pallas import tpu as pltpu
from jax.sharding import Mesh, PartitionSpec as P

COARSEN = 4
XH, Y, SPACE = 2, 4, 16
XC = 4
ROWS = 4
HALO = 3
GROUP = Y * SPACE
TIMES = 2 * Y
ROW = (2, XC, SPACE, 128)


def rho(y, s):
    z, x, core = s >> 2, (s >> 1) & 1, s & 1
    chip = 4 * z + (y if z % 2 == 0 else 3 - y)
    return 2 * (chip if x == 0 else 31 - chip) + core


BLOCK_OF = [rho(j // SPACE, j % SPACE) for j in range(GROUP)]
DEVICE_AT = [BLOCK_OF.index(p) for p in range(GROUP)]
RING = ("y", "space")
ALL = ("xh", "y", "space")
UP = [(DEVICE_AT[p], DEVICE_AT[(p + 1) % GROUP]) for p in range(GROUP)]
UP += [(GROUP + (i ^ 2), GROUP + (j ^ 2)) for i, j in UP]
DOWN = [(j, i) for i, j in UP]
ACROSS = [(j, GROUP + (j ^ 2)) for j in range(GROUP)]
TM = ("xh", "y")
VMEM = pl.BlockSpec(memory_space=pltpu.VMEM)
SMEM = pl.BlockSpec(memory_space=pltpu.SMEM)


def f32(*shape):
    return jax.ShapeDtypeStruct(shape, jnp.float32)


def call(kernel, outs, *args, flops=0, scalars=0):
    single = not isinstance(outs, (list, tuple))
    out_list = [outs] if single else list(outs)
    size = sum(int(np.prod(a.shape)) * 4 for a in list(args) + out_list)
    return pl.pallas_call(
        kernel,
        out_shape=outs,
        in_specs=[SMEM] * scalars + [VMEM] * (len(args) - scalars),
        out_specs=VMEM if single else [VMEM] * len(out_list),
        compiler_params=pltpu.CompilerParams(vmem_limit_bytes=16 << 20),
        cost_estimate=pl.CostEstimate(flops=flops, bytes_accessed=size, transcendentals=0),
    )(*args)


def lanes(c):
    return slice(c * 128, (c + 1) * 128)


PARCEL = 2 * XC + 3


def mirrored(xh, j):
    return jnp.where(xh == 0, j, j ^ 2)


def pack_kernel(at_ref, *refs):
    inputs, send, held, done = refs[:4], refs[4], refs[5:9], refs[9]
    planes = [(0, (tt, z)) for z in range(2) for tt in range(2)] + [(n, (z,)) for z in range(2) for n in range(1, 4)]
    copies = [pltpu.make_async_copy(inputs[n].at[i], held[n].at[i], done.at[m]) for m, (n, i) in enumerate(planes)]
    for copy in copies:
        copy.start()
    mine = pl.ds(pl.multiple_of(at_ref[1] * 128, 128), 128)
    for copy, (n, i) in zip(copies, planes):
        copy.wait()
        spread = pl.ds(i[-1], ROWS, stride=2)
        for j in range(GROUP):
            rows = slice(ROWS * BLOCK_OF[j], ROWS * BLOCK_OF[j] + ROWS)
            to = mirrored(at_ref[0], j)
            if n == 0:
                for c in range(XC):
                    send[to, i[0] * XC + c, spread, :] = held[0][(*i, rows, lanes(c))]
            else:
                send[to, 2 * XC + n - 1, spread, :] = held[n][(*i, rows, mine)].astype(jnp.float32)


EARLY, LATE = 5, 4
EDGE = EARLY * ROWS


def unpack_kernel(recv, up, down, second, label, force):
    flat = recv.reshape(GROUP * PARCEL * 8, 128)

    def piece(y, n, row, par):
        return flat[pl.ds((y * SPACE * PARCEL + n) * 8 + row * 2 + par, SPACE, stride=PARCEL * 8), :]

    for y in range(Y):
        for row in range(ROWS):
            for par in range(2):
                for tt in range(2):
                    k = 2 * y + tt
                    for c in range(XC):
                        part = piece(y, tt * XC + c, row, par)
                        if k < EARLY - 1:
                            up[(k + 1) * ROWS + row, par, c] = part
                            down[(k + 1) * ROWS + row, par, c] = part
                        else:
                            second[k - EARLY + 1, row, par, c] = part
                part = piece(y, 2 * XC, row, par)
                up[row, par, y] = part
                down[row, par, y] = part
                for n, ref in enumerate((force, label)):
                    part = piece(y, 2 * XC + 1 + n, row, par)
                    ref[row, par, y] = part
                    first = EDGE + (1 - n) * HALO
                    if row < HALO:
                        down[first + row, par, y] = part
                    if row >= ROWS - HALO:
                        up[first + row - ROWS + HALO, par, y] = part


def return_pack_kernel(early, late, first, r_early, r_late, send):
    flat = send.reshape(GROUP * 4 * XC * 8, 128)
    r = residual_rows(first, r_early, r_late)
    for y in range(Y):
        for tt in range(2):
            k = 2 * y + tt
            for row in range(ROWS):
                for n, rows in enumerate((pair((early, late)[k // 4], k % 4, row), r(k, row))):
                    for par in range(2):
                        for c in range(XC):
                            at = ((y * SPACE * 2 + n) * 2 + tt) * XC + c
                            flat[pl.ds(at * 8 + row * 2 + par, SPACE, stride=4 * XC * 8), :] = rows[par][c]


def return_kernel(at_ref, recv, field, updated, residual, new, rest, done):
    copies = []
    for tt in range(2):
        for z in range(2):
            spread = pl.ds(z, ROWS, stride=2)
            for n in range(GROUP):
                rows = slice(ROWS * BLOCK_OF[n], ROWS * BLOCK_OF[n] + ROWS)
                j = mirrored(at_ref[0], n)
                for c in range(XC):
                    here = (tt, z, rows, lanes(c))
                    new[here] = field[here] + recv[j, tt * XC + c, spread, :]
                    rest[here] = recv[j, (2 + tt) * XC + c, spread, :]
            for held, out in ((new, updated), (rest, residual)):
                copies.append(pltpu.make_async_copy(held.at[tt, z], out.at[tt, z], done.at[len(copies)]))
                copies[-1].start()
    for copy in copies:
        copy.wait()


def fill_coefficients(diffusion, drift, label, below, above, coef):
    lane = lax.broadcasted_iota(jnp.int32, (SPACE, 128), 1)
    tables = [jnp.zeros((SPACE, 128), jnp.float32)] * 8
    for n in range(diffusion.shape[0]):
        a = diffusion[n]
        bz, by, bx = a * drift[0, n], a * drift[1, n], a * drift[2, n]
        values = [1.0 - 6.0 * a, a - bz, a + bz, a - by, a + by, a - bx, a + bx, 1.0 - 6.0 * (a * COARSEN)]
        tables = [jnp.where(lane == n, value, table) for value, table in zip(values, tables)]
    for i in range(-HALO, ROWS + HALO):
        ref, at = (below, EDGE + HALO + i) if i < 0 else (above, EDGE + i - ROWS) if i >= ROWS else (label, i)
        for par in range(2):
            for c in range(XC):
                index = ref[at, par, c].astype(jnp.int32)
                for t in range(8):
                    coef[t, HALO + i, par, c] = jnp.take_along_axis(tables[t], index, axis=1, mode="promise_in_bounds")


def x_shifts(v):
    lane = lax.broadcasted_iota(jnp.int32, v.shape, 2)
    before = pltpu.roll(v, 1, 2)
    after = pltpu.roll(v, 127, 2)
    before = jnp.where(lane == 0, jnp.concatenate([before[-1:], before[:-1]], 0), before)
    after = jnp.where(lane == 127, jnp.concatenate([after[1:], after[:1]], 0), after)
    return before, after


def sweep_row(coef, row, v, up, down, extra, coarse):
    at = HALO + row
    result = []
    for p in range(2):
        if p == 0:
            z_above, z_below = v[1], pltpu.roll(v[1], 1, 1)
        else:
            z_above, z_below = pltpu.roll(v[0], SPACE - 1, 1), v[0]
        before, after = x_shifts(v[p])
        total = coef[1, at, p] * z_above + coef[2, at, p] * z_below
        if up is not None:
            total = total + coef[3, at, p] * up[p]
        if down is not None:
            total = total + coef[4, at, p] * down[p]
        total = total + coef[5, at, p] * after + coef[6, at, p] * before
        if coarse:
            total = coef[7, at, p] * v[p] + COARSEN * total
        else:
            total = coef[0, at, p] * v[p] + total
        if extra is not None:
            total = total + extra[p]
        result.append(total)
    return result


def pair(ref, *at):
    return [ref[(*at, 0)], ref[(*at, 1)]]


def put(ref, at, value):
    for p in range(2):
        ref[(*at, p)] = value[p]


def fine_times(coef, force, starts):
    all_rows = []
    for own, below, above in starts:
        rows = {i: own(i) for i in range(ROWS)}
        rows |= {i - ROWS: below(i) for i in range(ROWS)}
        rows |= {i + ROWS: above(i) for i in range(ROWS)}
        all_rows.append(rows)
    for step in range(COARSEN):
        reach = COARSEN - 1 - step
        new = [{} for _ in starts]
        for i in range(-reach, ROWS + reach):
            for rows, out in zip(all_rows, new):
                out[i] = sweep_row(coef, i, rows[i], rows[i + 1], rows[i - 1], force(i), False)
        all_rows = new
    return [[rows[i] for i in range(ROWS)] for rows in all_rows]


def forcing_rows(own, below, above):
    first = EDGE + HALO

    def at(i):
        return pair(below, first + HALO + i) if i < 0 else pair(above, first + i - ROWS) if i >= ROWS else pair(own, i)

    return at


def minus(a, b):
    return [x - y for x, y in zip(a, b)]


def fine_early_kernel(diffusion, drift, label, force, up, below, above, second, coef, r, first):
    fill_coefficients(diffusion, drift, label, below, above, coef)
    extra = forcing_rows(force, below, above)

    def results(*times):
        return fine_times(coef, extra, [[lambda i, ref=ref, k=k: pair(ref, k * ROWS + i) for ref in (up, below, above)] for k in times])

    @pl.loop(0, EARLY // 2)
    def _(n):
        for k, rows in zip((2 * n, 2 * n + 1), results(2 * n, 2 * n + 1)):
            for i in range(ROWS):
                put(r, (k, i), minus(rows[i], pair(up, (k + 1) * ROWS + i)))

    for i in range(ROWS):
        put(first, (i,), pair(r, 0, i))
    (rows,) = results(EARLY - 1)
    for i in range(ROWS):
        put(r, (EARLY - 1, i), minus(rows[i], pair(second, 0, i)))


def fine_late_kernel(coef, force, edge_below, edge_above, second, below, above, order, r, beyond):
    extra = forcing_rows(force, edge_below, edge_above)

    def results(*times):
        return fine_times(coef, extra, [[lambda i, ref=ref, k=k: pair(ref, k, i) for ref in (second, below, above)] for k in times])

    @pl.loop(0, LATE // 2)
    def _(n):
        even, odd = results(2 * n, 2 * n + 1)
        for i in range(ROWS):
            put(r, (2 * n, i), minus(even[i], pair(second, 2 * n + 1, i)))

            @pl.when(n == 0)
            def _():
                put(r, (1, i), minus(odd[i], pair(second, 2, i)))

            @pl.when(n == 1)
            def _():
                put(beyond, (i,), odd[i])


def residual_rows(first, early, late):
    def at(k, i):
        return pair(first, i) if k == 0 else pair(early, k, i) if k < EARLY else pair(late, k - EARLY, i)

    return at


def trajectory(coef, r, first, width, start, low, high):
    rows = start
    for j in range(width):
        put(low, (j,), rows[0])
        put(high, (j,), rows[-1])
        if j + 1 < width:
            rows = [
                sweep_row(
                    coef, i, rows[i], rows[i + 1] if i + 1 < ROWS else None, rows[i - 1] if i else None,
                    r(first + j, i), True,
                )
                for i in range(ROWS)
            ]


def advance(coef, r, first, width, start, below, above, store):
    rows = start
    dev_low, dev_high = {}, {}
    for j in range(width):
        under, over = pair(below, j), pair(above, j)
        if 1 in dev_low:
            under = [a + b for a, b in zip(under, dev_low[1])]
            over = [a + b for a, b in zip(over, dev_high[1])]
        padded = [under] + rows + [over]
        new_low, new_high = {}, {}
        for i in range(1, min(j + 1, width - j - 1) + 1):
            source_low = rows[0] if i == 1 else dev_low[i - 1]
            source_high = rows[-1] if i == 1 else dev_high[i - 1]
            if i <= j:
                new_low[i] = sweep_row(coef, -i, dev_low[i], source_low, dev_low.get(i + 1), None, True)
                new_high[i] = sweep_row(coef, ROWS - 1 + i, dev_high[i], dev_high.get(i + 1), source_high, None, True)
            else:
                new_low[i] = [COARSEN * coef[3, HALO - i, p] * source_low[p] for p in range(2)]
                new_high[i] = [COARSEN * coef[4, HALO + ROWS - 1 + i, p] * source_high[p] for p in range(2)]
        rows = [sweep_row(coef, i, padded[i + 1], padded[i + 2], padded[i], r(first + j, i), True) for i in range(ROWS)]
        dev_low, dev_high = new_low, new_high
        for i in range(ROWS):
            put(store, (j, i), rows[i])
    return rows


def block(ref, *at):
    return [pair(ref, *at, i) for i in range(ROWS)]


def start_kernel(time, width, coef, first, r_early, start, low, high):
    r = residual_rows(first, r_early, None)
    trajectory(coef, r, time, width, block(start), low, high)


def middle_kernel(time, width, then, coef, first, r_early, r_late, start, below, above, errors, low, high):
    r = residual_rows(first, r_early, r_late)
    rows = advance(coef, r, time, width, block(start), below, above, errors)
    trajectory(coef, r, time + width, then, rows, low, high)


def end_kernel(time, width, coef, first, r_early, r_late, start, below, above, errors, last):
    r = residual_rows(first, r_early, r_late)
    rows = advance(coef, r, time, width, block(start, start.shape[0] - 1), below, above, errors)
    for i in range(ROWS):
        put(last, (i,), rows[i])


def exchange(low, high):
    return lax.ppermute(high, ALL, UP), lax.ppermute(low, ALL, DOWN)


def coarse(coef, first, r_early, r_late, start, time):
    a, b = 4 - time, 4
    low, high = call(
        functools.partial(start_kernel, time, a), [f32(a, *ROW)] * 2, coef, first, r_early, start, flops=500_000_000
    )
    below, above = exchange(low, high)
    if callable(r_late):
        r_late = r_late(low)
    given = coef, first, r_early, r_late
    early, low, high = call(
        functools.partial(middle_kernel, time, a, b), [f32(a, ROWS, *ROW)] + [f32(b, *ROW)] * 2,
        *given, start, below, above, flops=1_000_000_000,
    )
    below, above = exchange(low, high)
    late, last = call(
        functools.partial(end_kernel, 4, b), [f32(b, ROWS, *ROW), f32(ROWS, *ROW)],
        *given, early, below, above, flops=500_000_000,
    )
    return early, late, last


def choose_kernel(at_ref, first, beyond, up, out):
    @pl.when(at_ref[0] == 0)
    def _():
        out[...] = first[...]

    @pl.when(at_ref[0] == 1)
    def _():
        out[...] = beyond[...] - up[ROWS : 2 * ROWS]


def shards(initial, c_values, forcing, classes, diffusion, drift):
    xh = lax.axis_index("xh")
    at = jnp.stack([xh, lax.axis_index("y")])
    one = f32(ROWS, *ROW)

    inputs = (c_values, initial, forcing, classes)
    send = pl.pallas_call(
        pack_kernel,
        out_shape=f32(GROUP, PARCEL, 8, 128),
        in_specs=[SMEM] + [pl.BlockSpec(memory_space=pl.ANY)] * 4,
        out_specs=VMEM,
        scratch_shapes=[pltpu.VMEM(a.shape, a.dtype) for a in inputs] + [pltpu.SemaphoreType.DMA((10,))],
        compiler_params=pltpu.CompilerParams(vmem_limit_bytes=56 << 20),
    )(at, *inputs)
    recv = lax.all_to_all(send, RING, 0, 0, tiled=True)
    message = f32(EDGE + 2 * HALO, *ROW)
    up, down, second, label, force = call(unpack_kernel, [message, message, f32(LATE, ROWS, *ROW), one, one], recv)
    edge_below, edge_above = exchange(down, up)
    below, above = exchange(second, second)
    coef, r_early, first = call(
        fine_early_kernel, [f32(8, ROWS + 2 * HALO, *ROW), f32(EARLY, ROWS, *ROW), one],
        diffusion, drift, label, force, up, edge_below, edge_above, second, flops=10_000_000_000, scalars=2,
    )
    made = []

    def make_late(order):
        made.extend(
            call(
                fine_late_kernel, [f32(LATE - 1, ROWS, *ROW), one],
                coef, force, edge_below, edge_above, second, below, above, order, flops=5_000_000_000,
            )
        )
        return made[0]

    early, late, last = coarse(coef, first, r_early, make_late, first, 1)
    r_late, beyond = made
    beyond = lax.ppermute(beyond, ALL, ACROSS)
    start = lax.ppermute(last, ALL, ACROSS)
    first = call(choose_kernel, one, at, first, beyond, up, scalars=1)
    early, late, last = coarse(coef, first, r_early, r_late, start, 0)
    back = call(return_pack_kernel, f32(GROUP, 4 * XC, 8, 128), early, late, first, r_early, r_late)
    got = lax.all_to_all(back, RING, 0, 0, tiled=True)
    return tuple(
        pl.pallas_call(
            return_kernel,
            out_shape=[f32(*c_values.shape)] * 2,
            in_specs=[SMEM, VMEM, VMEM],
            out_specs=[pl.BlockSpec(memory_space=pl.ANY)] * 2,
            scratch_shapes=[pltpu.VMEM(c_values.shape, jnp.float32)] * 2 + [pltpu.SemaphoreType.DMA((8,))],
            compiler_params=pltpu.CompilerParams(vmem_limit_bytes=16 << 20),
        )(at, got, c_values)
    )


def solution(mesh):
    split = Mesh(np.asarray(mesh.devices).reshape(XH, Y, SPACE), ("xh", "y", "space"))
    return jax.shard_map(
        shards,
        mesh=split,
        in_specs=(P("space"), P(TM, "space"), P("space"), P("space"), P(), P()),
        out_specs=(P(TM, "space"), P(TM, "space")),
        check_vma=False,
    )
```

time: 232 us -> 198 us (0.85)
  blocking collectives: 0 us -> 105 us
  waiting for transfers between devices: 134 us -> 41.3 us
  starting transfers between devices: 42.5 us -> 12.4 us
  local copies, waits for them, and re-layouts: 16.9 us -> 0.02 us
    all_to_all x0 -> x2, blocking collectives: none -> 105 us  [the longest x1 56.8 us: shards(): got = lax.all_to_all(back, RING, 0, 0, tiled=True)]
    all_to_all x4 -> x0, waiting for transfers between devices: 62.6 us -> none  [the longest x2 25.7 us: shards(): got = lax.all_to_all(back, RING, 0, 0, tiled=True)]
    ppermute x18 -> x14, waiting for transfers between devices: 71 us -> 41.3 us  [the longest x12 34.2 us: exchange(): return (lax.ppermute(high, ALL, UP), lax.ppermute(low, ALL, DOWN))]
    all_to_all x4 -> x0, starting transfers between devices: 28 us -> none  [the longest x2 15.1 us: shards(): got = lax.all_to_all(back, RING, 0, 0, tiled=True)]
    unnamed x40 -> x8, local copies, waits for them, and re-layouts: 16.8 us -> 0.02 us
    pallas_call x0 -> x2, Pallas kernels: none -> 7.72 us  [the longest x1 4.86 us: shards(): pl.pallas_call(pack_kernel, out_shape=f32(GROUP, PARCEL, 8, 128), in_spec...]
    pallas_call x17 -> x11, Pallas kernels: 36.8 us -> 30 us  [call(): pl.pallas_call(kernel, out_shape=outs, in_specs=[SMEM] * scalars + [VMEM]...]
    ppermute x18 -> x14, starting transfers between devices: 14.5 us -> 12.4 us  [the longest x12 9.86 us: exchange(): return (lax.ppermute(high, ALL, UP), lax.ppermute(low, ALL, DOWN))]
  transfers between devices with their start and end apart: 22 -> 14, of which waited for: 15 -> 8; matrix products, arithmetic and copies ran while one was open for 0% -> 0% of each run, Pallas kernels for 11% -> 10%
where the time goes in v1:
time: 198 us
  blocking collectives  105 us (53%)
  waiting for transfers between devices  41.3 us (21%)
  Pallas kernels  37.7 us (19%)
  starting transfers between devices  12.4 us (6%)
    all_to_all x1, blocking collectives, shards(): got = lax.all_to_all(back, RING, 0, 0, tiled=True)  56.8 us
    all_to_all x1, blocking collectives, shards(): recv = lax.all_to_all(send, RING, 0, 0, tiled=True)  47.8 us
    ppermute x12, waiting for transfers between devices, exchange(): return (lax.ppermute(high, ALL, UP), lax.ppermute(low, ALL, DOWN))  34.2 us
    pallas_call x11, Pallas kernels, call(): pl.pallas_call(kernel, out_shape=outs, in_specs=[SMEM] * scalars + [VMEM]...  30 us
    ppermute x12, starting transfers between devices, exchange(): return (lax.ppermute(high, ALL, UP), lax.ppermute(low, ALL, DOWN))  9.86 us
    ppermute x1, waiting for transfers between devices, shards(): start = lax.ppermute(last, ALL, ACROSS)  7.03 us
    pallas_call x1, Pallas kernels, shards(): pl.pallas_call(pack_kernel, out_shape=f32(GROUP, PARCEL, 8, 128), in_spec...  4.86 us
  transfers between devices with their start and end apart: 14, of which 8 were waited for; matrix products, arithmetic and copies ran while one was open for 0% of the time, Pallas kernels for 10%

profile of v1, /device:TPU:5, one launch (start us, length us, event | category | flops | bytes accessed | tf_op | source)
XLA Modules:
  0.0 197.7 jit_solution(4047829255672917196)
XLA Ops:
  0.6 0.6 pad_add_fusion.at_ref
  1.2 4.9 %shard_map.77 = f32[64,11,8,128]{3,2,1,0:T(8,128)} custom-call(s32[2]{0:T(128)} %pad_add_fusion.at_ref, f32[2,2,256,512]{3,2,1,0:T(8,128)} %field.1, f32[2,256,512]{2,1,0:T(8,128)} %refs_1_.1, f32[2,256,512]{2,1,0:T(8,128)} %refs_2_.1, s32[2,256,512]{2,1,0:T(8,128)} %refs_3_.1), custom_call_target="tpu_custom_call" | custom-call | tf_op jit(solution)/shard_map/pallas_call | solution.py:399
  6.1 47.8 %all_to_all.10.recv = f32[64,11,8,128]{3,2,1,0:T(8,128)S(1)} all-to-all(f32[64,11,8,128]{3,2,1,0:T(8,128)} %shard_map.77), channel_id=1, replica_groups=mesh['xh'=2,'y'=4,'space'=16] {'y','space'}, dimensions={0} | all-to-all | bytes 5767168 | tf_op jit(solution)/shard_map/all_to_all | solution.py:407
  53.9 0.6 shard_map.78
  54.5 0.6 collective-permute-start.1
  55.1 1.2 collective-permute-start
  56.3 1.7 collective-permute-start.2
  58.1 18.0 %collective-permute-done.1.above.edge_above = f32[26,2,4,16,128]{4,3,2,1,0:T(8,128)S(1)} collective-permute-done((f32[26,2,4,16,128]{4,3,2,1,0:T(8,128)S(1)}, f32[26,2,4,16,128]{4,3,2,1,0:T(8,128)S(1)}, u32[]{:S(2)}, u32[]{:S(2)}) %collective-permute-start.1) | collective-permute-done | bytes 1703968 | tf_op jit(solution)/shard_map/ppermute | solution.py:359
  76.1 11.1 %shard_map.79 = (f32[8,10,2,4,16,128]{5,4,3,2,1,0:T(8,128)S(1)}, f32[5,4,2,4,16,128]{5,4,3,2,1,0:T(8,128)S(1)}, f32[4,2,4,16,128]{4,3,2,1,0:T(8,128)S(1)}) custom-call(f32[8]{0:T(128)S(1)} %copy-done.3, f32[3,8]{1,0:T(4,128)S(1)} %copy-done.2, f32[4,2,4,16,128]{4,3,2,1,0:T(8,128)S(1)} %get-tuple-element.24.label, ...), custom_call_target="tpu_custom_call" | custom-call | flops 10000000000 | bytes 13500544 | tf_op jit(solution)/shard_map/pallas_call | solution.py:48
  87.7 1.5 collective-permute-start.5
  89.2 6.2 %shard_map.81 = (f32[3,4,2,4,16,128]{5,4,3,2,1,0:T(8,128)S(1)}, f32[4,2,4,16,128]{4,3,2,1,0:T(8,128)S(1)}) custom-call(f32[8,10,2,4,16,128]{5,4,3,2,1,0:T(8,128)S(1)} %get-tuple-element.29.coef, f32[4,2,4,16,128]{4,3,2,1,0:T(8,128)S(1)} %get-tuple-element.25.force, f32[26,2,4,16,128]{4,3,2,1,0:T(8,128)S(1)} %collective-permute-done.below.edge_below, ...), custom_call_target="tpu_custom_call" | custom-call | flops 5000000000 | bytes 13303808 | tf_op jit(solution)/shard_map/pallas_call | solution.py:48
  95.4 1.4 shard_map.83
  96.8 1.8 collective-permute-start.7
  98.6 1.3 collective-permute-start.4
  99.9 2.0 %collective-permute-done.7.below = f32[4,2,4,16,128]{4,3,2,1,0:T(8,128)S(1)} collective-permute-done((f32[4,2,4,16,128]{4,3,2,1,0:T(8,128)S(1)}, f32[4,2,4,16,128]{4,3,2,1,0:T(8,128)S(1)}, u32[]{:S(2)}, u32[]{:S(2)}) %collective-permute-start.7) | collective-permute-done | bytes 262176 | tf_op jit(solution)/shard_map/ppermute | solution.py:359
  101.9 2.8 %collective-permute-done.8.above = f32[4,2,4,16,128]{4,3,2,1,0:T(8,128)S(1)} collective-permute-done((f32[4,2,4,16,128]{4,3,2,1,0:T(8,128)S(1)}, f32[4,2,4,16,128]{4,3,2,1,0:T(8,128)S(1)}, u32[]{:S(2)}, u32[]{:S(2)}) %collective-permute-start.8) | collective-permute-done | bytes 262176 | tf_op jit(solution)/shard_map/ppermute | solution.py:359
  104.7 2.1 %shard_map.84 = (f32[4,4,2,4,16,128]{5,4,3,2,1,0:T(8,128)}, f32[4,2,4,16,128]{4,3,2,1,0:T(8,128)S(1)}) custom-call(f32[8,10,2,4,16,128]{5,4,3,2,1,0:T(8,128)S(1)} %get-tuple-element.29.coef, f32[4,2,4,16,128]{4,3,2,1,0:T(8,128)S(1)} %get-tuple-element.30.first.start, f32[5,4,2,4,16,128]{5,4,3,2,1,0:T(8,128)S(1)} %get-tuple-element.31.r_early, ...), custom_call_target="tpu_custom_call" | custom-call | flops 500000000 | bytes 10223616 | tf_op jit(solution)/shard_map/pallas_call | solution.py:48
  106.8 1.3 collective-permute-start.9
  108.1 0.6 shard_map.82.first
  108.7 7.0 %collective-permute-done.9.start = f32[4,2,4,16,128]{4,3,2,1,0:T(8,128)S(1)} collective-permute-done((f32[4,2,4,16,128]{4,3,2,1,0:T(8,128)S(1)}, f32[4,2,4,16,128]{4,3,2,1,0:T(8,128)S(1)}, u32[]{:S(2)}, u32[]{:S(2)}) %collective-permute-start.9) | collective-permute-done | bytes 262176 | tf_op jit(solution)/shard_map/ppermute | solution.py:430
  115.8 0.6 shard_map.85
  116.3 2.4 %collective-permute-start.10 = (f32[4,2,4,16,128]{4,3,2,1,0:T(8,128)S(1)}, f32[4,2,4,16,128]{4,3,2,1,0:T(8,128)S(1)}, u32[]{:S(2)}, u32[]{:S(2)}) collective-permute-start(f32[4,2,4,16,128]{4,3,2,1,0:T(8,128)S(1)} %get-tuple-element.40), channel_id=1, source_target_pairs={{0,1},{1,16},{16,17},{17,32},{32,33},{33,48},{48,49},{49,52},{52,5... | collective-permute-start | bytes 786440 | tf_op jit(solution)/shard_map/ppermute | solution.py:359
  118.8 3.3 %collective-permute-done.10.below = f32[4,2,4,16,128]{4,3,2,1,0:T(8,128)S(1)} collective-permute-done((f32[4,2,4,16,128]{4,3,2,1,0:T(8,128)S(1)}, f32[4,2,4,16,128]{4,3,2,1,0:T(8,128)S(1)}, u32[]{:S(2)}, u32[]{:S(2)}) %collective-permute-start.10) | collective-permute-done | bytes 262176 | tf_op jit(solution)/shard_map/ppermute | solution.py:359
  122.1 2.5 %collective-permute-done.11.above = f32[4,2,4,16,128]{4,3,2,1,0:T(8,128)S(1)} collective-permute-done((f32[4,2,4,16,128]{4,3,2,1,0:T(8,128)S(1)}, f32[4,2,4,16,128]{4,3,2,1,0:T(8,128)S(1)}, u32[]{:S(2)}, u32[]{:S(2)}) %collective-permute-start.11) | collective-permute-done | bytes 262176 | tf_op jit(solution)/shard_map/ppermute | solution.py:359
  124.5 1.7 shard_map.86
  126.3 0.5 collective-permute-start.13
  126.8 2.8 %collective-permute-done.12.below = f32[4,2,4,16,128]{4,3,2,1,0:T(8,128)S(1)} collective-permute-done((f32[4,2,4,16,128]{4,3,2,1,0:T(8,128)S(1)}, f32[4,2,4,16,128]{4,3,2,1,0:T(8,128)S(1)}, u32[]{:S(2)}, u32[]{:S(2)}) %collective-permute-start.12) | collective-permute-done | bytes 262176 | tf_op jit(solution)/shard_map/ppermute | solution.py:359
  129.6 2.8 %collective-permute-done.13.above = f32[4,2,4,16,128]{4,3,2,1,0:T(8,128)S(1)} collective-permute-done((f32[4,2,4,16,128]{4,3,2,1,0:T(8,128)S(1)}, f32[4,2,4,16,128]{4,3,2,1,0:T(8,128)S(1)}, u32[]{:S(2)}, u32[]{:S(2)}) %collective-permute-start.13) | collective-permute-done | bytes 262176 | tf_op jit(solution)/shard_map/ppermute | solution.py:359
  132.4 1.9 shard_map.87
  134.3 3.5 %shard_map.88 = f32[64,16,8,128]{3,2,1,0:T(8,128)S(1)} custom-call(f32[4,4,2,4,16,128]{5,4,3,2,1,0:T(8,128)S(1)} %get-tuple-element.42.start.early, f32[4,4,2,4,16,128]{5,4,3,2,1,0:T(8,128)S(1)} %get-tuple-element.45.late, f32[4,2,4,16,128]{4,3,2,1,0:T(8,128)S(1)} %shard_map.82.first, f32[5,4,2,4,16,128]{5,4,3,2,1,0:T(8,128)S(1)} %get-tuple-element.31.r_early, ...), custom_call_target="tpu_custom_call" | custom-call | bytes 8650752 | tf_op jit(solution)/shard_map/pallas_call | solution.py:48
  137.8 56.8 %all_to_all.11.recv = f32[64,16,8,128]{3,2,1,0:T(8,128)S(1)} all-to-all(f32[64,16,8,128]{3,2,1,0:T(8,128)S(1)} %shard_map.88), channel_id=1, replica_groups=mesh['xh'=2,'y'=4,'space'=16] {'y','space'}, dimensions={0} | all-to-all | bytes 8388608 | tf_op jit(solution)/shard_map/all_to_all | solution.py:434
  194.6 2.9 %shard_map.89 = (f32[2,2,256,512]{3,2,1,0:T(8,128)}, f32[2,2,256,512]{3,2,1,0:T(8,128)}) custom-call(s32[2]{0:T(128)S(1)} %copy-done.1, f32[64,16,8,128]{3,2,1,0:T(8,128)S(1)} %all_to_all.11.recv, f32[2,2,256,512]{3,2,1,0:T(8,128)S(1)} %copy-done), custom_call_target="tpu_custom_call" | custom-call | tf_op jit(solution)/shard_map/pallas_call | solution.py:436
  (20 shorter events, 0.5 us)
Async XLA Ops:
  53.9 22.2 %copy-start.2 = (f32[3,8]{1,0:T(4,128)S(1)}, f32[3,8]{1,0:T(4,128)}, u32[]{:S(2)}) copy-start(f32[3,8]{1,0:T(4,128)} %drift.1) | copy-start | bytes 292
  53.9 22.2 %copy-start.3 = (f32[8]{0:T(128)S(1)}, f32[8]{0:T(128)}, u32[]{:S(2)}) copy-start(f32[8]{0:T(128)} %diffusion.1) | copy-start | bytes 100
  54.5 21.6 %collective-permute-start.1 = (f32[26,2,4,16,128]{4,3,2,1,0:T(8,128)S(1)}, f32[26,2,4,16,128]{4,3,2,1,0:T(8,128)S(1)}, u32[]{:S(2)}, u32[]{:S(2)}) collective-permute-start(f32[26,2,4,16,128]{4,3,2,1,0:T(8,128)S(1)} %get-tuple-element.27), channel_id=1, source_target_pairs={{1,0},{16,1},{17,16},{32,17},{33,32},{48,33},{49,48},{52,49},{53,5... | collective-permute-start | bytes 5111816 | tf_op jit(solution)/shard_map/ppermute | solution.py:359
  55.1 21.0 %collective-permute-start = (f32[26,2,4,16,128]{4,3,2,1,0:T(8,128)S(1)}, f32[26,2,4,16,128]{4,3,2,1,0:T(8,128)S(1)}, u32[]{:S(2)}, u32[]{:S(2)}) collective-permute-start(f32[26,2,4,16,128]{4,3,2,1,0:T(8,128)S(1)} %get-tuple-element.26.up), channel_id=1, source_target_pairs={{0,1},{1,16},{16,17},{17,32},{32,33},{33,48},{48,49},{49,52},{52,5... | collective-permute-start | bytes 5111816 | tf_op jit(solution)/shard_map/ppermute | solution.py:359
  56.3 32.9 %collective-permute-start.3 = (f32[4,4,2,4,16,128]{5,4,3,2,1,0:T(8,128)S(1)}, f32[4,4,2,4,16,128]{5,4,3,2,1,0:T(8,128)S(1)}, u32[]{:S(2)}, u32[]{:S(2)}) collective-permute-start(f32[4,4,2,4,16,128]{5,4,3,2,1,0:T(8,128)S(1)} %get-tuple-element.28.second), channel_id=1, source_target_pairs={{1,0},{16,1},{17,16},{32,17},{33,32},{48,33},{49,48},{52,49},{53,5... | collective-permute-start | bytes 3145736 | tf_op jit(solution)/shard_map/ppermute | solution.py:359
  56.3 32.9 %collective-permute-start.2 = (f32[4,4,2,4,16,128]{5,4,3,2,1,0:T(8,128)S(1)}, f32[4,4,2,4,16,128]{5,4,3,2,1,0:T(8,128)S(1)}, u32[]{:S(2)}, u32[]{:S(2)}) collective-permute-start(f32[4,4,2,4,16,128]{5,4,3,2,1,0:T(8,128)S(1)} %get-tuple-element.28.second), channel_id=1, source_target_pairs={{0,1},{1,16},{16,17},{17,32},{32,33},{33,48},{48,49},{49,52},{52,5... | collective-permute-start | bytes 3145736 | tf_op jit(solution)/shard_map/ppermute | solution.py:359
  87.7 7.8 %collective-permute-start.5 = (f32[3,2,4,16,128]{4,3,2,1,0:T(8,128)S(1)}, f32[3,2,4,16,128]{4,3,2,1,0:T(8,128)S(1)}, u32[]{:S(2)}, u32[]{:S(2)}) collective-permute-start(f32[3,2,4,16,128]{4,3,2,1,0:T(8,128)S(1)} %get-tuple-element.35), channel_id=1, source_target_pairs={{0,1},{1,16},{16,17},{17,32},{32,33},{33,48},{48,49},{49,52},{52,5... | collective-permute-start | bytes 589832 | tf_op jit(solution)/shard_map/ppermute | solution.py:359
  89.2 6.3 %collective-permute-start.6 = (f32[3,2,4,16,128]{4,3,2,1,0:T(8,128)S(1)}, f32[3,2,4,16,128]{4,3,2,1,0:T(8,128)S(1)}, u32[]{:S(2)}, u32[]{:S(2)}) collective-permute-start(f32[3,2,4,16,128]{4,3,2,1,0:T(8,128)S(1)} %get-tuple-element.32.order), channel_id=1, source_target_pairs={{1,0},{16,1},{17,16},{32,17},{33,32},{48,33},{49,48},{52,49},{53,5... | collective-permute-start | bytes 589832 | tf_op jit(solution)/shard_map/ppermute | solution.py:359
  96.8 5.1 %collective-permute-start.7 = (f32[4,2,4,16,128]{4,3,2,1,0:T(8,128)S(1)}, f32[4,2,4,16,128]{4,3,2,1,0:T(8,128)S(1)}, u32[]{:S(2)}, u32[]{:S(2)}) collective-permute-start(f32[4,2,4,16,128]{4,3,2,1,0:T(8,128)S(1)} %get-tuple-element.37), channel_id=1, source_target_pairs={{0,1},{1,16},{16,17},{17,32},{32,33},{33,48},{48,49},{49,52},{52,5... | collective-permute-start | bytes 786440 | tf_op jit(solution)/shard_map/ppermute | solution.py:359
  98.6 6.1 %collective-permute-start.8 = (f32[4,2,4,16,128]{4,3,2,1,0:T(8,128)S(1)}, f32[4,2,4,16,128]{4,3,2,1,0:T(8,128)S(1)}, u32[]{:S(2)}, u32[]{:S(2)}) collective-permute-start(f32[4,2,4,16,128]{4,3,2,1,0:T(8,128)S(1)} %get-tuple-element.38), channel_id=1, source_target_pairs={{1,0},{16,1},{17,16},{32,17},{33,32},{48,33},{49,48},{52,49},{53,5... | collective-permute-start | bytes 786440 | tf_op jit(solution)/shard_map/ppermute | solution.py:359
  98.6 9.5 %collective-permute-start.4 = (f32[4,2,4,16,128]{4,3,2,1,0:T(8,128)S(1)}, f32[4,2,4,16,128]{4,3,2,1,0:T(8,128)S(1)}, u32[]{:S(2)}, u32[]{:S(2)}) collective-permute-start(f32[4,2,4,16,128]{4,3,2,1,0:T(8,128)S(1)} %get-tuple-element.33), channel_id=1, source_target_pairs={{0,66},{1,67},{2,64},{3,65},{4,70},{5,71},{6,68},{7,69},{8,74},{9,... | collective-permute-start | bytes 786440 | tf_op jit(solution)/shard_map/ppermute | solution.py:429
  104.7 3.4 %copy-start.1 = (s32[2]{0:T(128)S(1)}, s32[2]{0:T(128)}, u32[]{:S(2)}) copy-start(s32[2]{0:T(128)} %pad_add_fusion.at_ref) | copy-start | bytes 28
  106.8 8.9 %collective-permute-start.9 = (f32[4,2,4,16,128]{4,3,2,1,0:T(8,128)S(1)}, f32[4,2,4,16,128]{4,3,2,1,0:T(8,128)S(1)}, u32[]{:S(2)}, u32[]{:S(2)}) collective-permute-start(f32[4,2,4,16,128]{4,3,2,1,0:T(8,128)S(1)} %get-tuple-element.39), channel_id=1, source_target_pairs={{0,66},{1,67},{2,64},{3,65},{4,70},{5,71},{6,68},{7,69},{8,74},{9,... | collective-permute-start | bytes 786440 | tf_op jit(solution)/shard_map/ppermute | solution.py:430
  116.3 5.7 %collective-permute-start.10 = (f32[4,2,4,16,128]{4,3,2,1,0:T(8,128)S(1)}, f32[4,2,4,16,128]{4,3,2,1,0:T(8,128)S(1)}, u32[]{:S(2)}, u32[]{:S(2)}) collective-permute-start(f32[4,2,4,16,128]{4,3,2,1,0:T(8,128)S(1)} %get-tuple-element.40), channel_id=1, source_target_pairs={{0,1},{1,16},{16,17},{17,32},{32,33},{33,48},{48,49},{49,52},{52,5... | collective-permute-start | bytes 786440 | tf_op jit(solution)/shard_map/ppermute | solution.py:359
  118.8 5.8 %collective-permute-start.11 = (f32[4,2,4,16,128]{4,3,2,1,0:T(8,128)S(1)}, f32[4,2,4,16,128]{4,3,2,1,0:T(8,128)S(1)}, u32[]{:S(2)}, u32[]{:S(2)}) collective-permute-start(f32[4,2,4,16,128]{4,3,2,1,0:T(8,128)S(1)} %get-tuple-element.41), channel_id=1, source_target_pairs={{1,0},{16,1},{17,16},{32,17},{33,32},{48,33},{49,48},{52,49},{53,5... | collective-permute-start | bytes 786440 | tf_op jit(solution)/shard_map/ppermute | solution.py:359
  126.2 3.4 %collective-permute-start.12 = (f32[4,2,4,16,128]{4,3,2,1,0:T(8,128)S(1)}, f32[4,2,4,16,128]{4,3,2,1,0:T(8,128)S(1)}, u32[]{:S(2)}, u32[]{:S(2)}) collective-permute-start(f32[4,2,4,16,128]{4,3,2,1,0:T(8,128)S(1)} %get-tuple-element.43), channel_id=1, source_target_pairs={{0,1},{1,16},{16,17},{17,32},{32,33},{33,48},{48,49},{49,52},{52,5... | collective-permute-start | bytes 786440 | tf_op jit(solution)/shard_map/ppermute | solution.py:359
  126.3 6.1 %collective-permute-start.13 = (f32[4,2,4,16,128]{4,3,2,1,0:T(8,128)S(1)}, f32[4,2,4,16,128]{4,3,2,1,0:T(8,128)S(1)}, u32[]{:S(2)}, u32[]{:S(2)}) collective-permute-start(f32[4,2,4,16,128]{4,3,2,1,0:T(8,128)S(1)} %get-tuple-element.44), channel_id=1, source_target_pairs={{1,0},{16,1},{17,16},{32,17},{33,32},{48,33},{49,48},{52,49},{53,5... | collective-permute-start | bytes 786440 | tf_op jit(solution)/shard_map/ppermute | solution.py:359
  137.8 56.9 %copy-start = (f32[2,2,256,512]{3,2,1,0:T(8,128)S(1)}, f32[2,2,256,512]{3,2,1,0:T(8,128)}, u32[]{:S(2)}) copy-start(f32[2,2,256,512]{3,2,1,0:T(8,128)} %field.1) | copy-start | bytes 6291460

commit v2 on v1

--- a/solution.py
+++ b/solution.py
@@ -86,11 +86,12 @@
                 send[to, 2 * XC + n - 1, spread, :] = held[n][(*i, rows, mine)].astype(jnp.float32)
 
 
-EARLY, LATE = 5, 4
-EDGE = EARLY * ROWS
-
-
-def unpack_kernel(recv, up, down, second, label, force):
+MESSAGES = ((0, 1, 2), (3, 4), (5, 6), (7, 8))
+OTHER = (1, 2, 3, 0)
+
+
+def unpack_kernel(recv, *refs):
+    messages, (label, force, low, high) = refs[:4], refs[4:]
     flat = recv.reshape(GROUP * PARCEL * 8, 128)
 
     def piece(y, n, row, par):
@@ -100,39 +101,60 @@
         for row in range(ROWS):
             for par in range(2):
                 for tt in range(2):
-                    k = 2 * y + tt
-                    for c in range(XC):
-                        part = piece(y, tt * XC + c, row, par)
-                        if k < EARLY - 1:
-                            up[(k + 1) * ROWS + row, par, c] = part
-                            down[(k + 1) * ROWS + row, par, c] = part
-                        else:
-                            second[k - EARLY + 1, row, par, c] = part
-                part = piece(y, 2 * XC, row, par)
-                up[row, par, y] = part
-                down[row, par, y] = part
+                    for ref, starts in zip(messages, MESSAGES):
+                        if 2 * y + tt + 1 in starts:
+                            for c in range(XC):
+                                ref[starts.index(2 * y + tt + 1), row, par, c] = piece(y, tt * XC + c, row, par)
+                messages[0][0, row, par, y] = piece(y, 2 * XC, row, par)
                 for n, ref in enumerate((force, label)):
                     part = piece(y, 2 * XC + 1 + n, row, par)
                     ref[row, par, y] = part
-                    first = EDGE + (1 - n) * HALO
                     if row < HALO:
-                        down[first + row, par, y] = part
+                        low[n, row, par, y] = part
                     if row >= ROWS - HALO:
-                        up[first + row - ROWS + HALO, par, y] = part
-
-
-def return_pack_kernel(early, late, first, r_early, r_late, send):
-    flat = send.reshape(GROUP * 4 * XC * 8, 128)
-    r = residual_rows(first, r_early, r_late)
+                        high[n, row - ROWS + HALO, par, y] = part
+
+
+def hold_kernel(source, order, out):
+    out[...] = source[...]
+
+
+def return_pack_kernel(n, rows, back, scratch, done):
+    flat = scratch.reshape(GROUP * 2 * XC * 8, 128)
+    copies = []
     for y in range(Y):
         for tt in range(2):
-            k = 2 * y + tt
             for row in range(ROWS):
-                for n, rows in enumerate((pair((early, late)[k // 4], k % 4, row), r(k, row))):
-                    for par in range(2):
-                        for c in range(XC):
-                            at = ((y * SPACE * 2 + n) * 2 + tt) * XC + c
-                            flat[pl.ds(at * 8 + row * 2 + par, SPACE, stride=4 * XC * 8), :] = rows[par][c]
+                for par, part in enumerate(rows(2 * y + tt, row)):
+                    for c in range(XC):
+                        at = (y * SPACE * 2 + tt) * XC + c
+                        flat[pl.ds(at * 8 + row * 2 + par, SPACE, stride=2 * XC * 8), :] = part[c]
+        some = pl.ds(y * SPACE, SPACE)
+        copies.append(pltpu.make_async_copy(scratch.at[some], back.at[some, pl.ds(n * 2 * XC, 2 * XC)], done.at[y]))
+        copies[-1].start()
+    for copy in copies:
+        copy.wait()
+
+
+def residual_pack_kernel(times, order, *refs):
+    return_pack_kernel(1, residual_rows(times, refs), *refs[-3:])
+
+
+def error_pack_kernel(early, late, given, *refs):
+    return_pack_kernel(0, lambda k, i: pair((early, late)[k // 4], k % 4, i), *refs)
+
+
+def pack_call(kernel, alias, *args):
+    return pl.pallas_call(
+        kernel,
+        out_shape=f32(GROUP, 4 * XC, 8, 128),
+        in_specs=[VMEM] * (len(args) - alias) + [pl.BlockSpec(memory_space=pl.ANY)] * alias,
+        out_specs=pl.BlockSpec(memory_space=pl.ANY),
+        scratch_shapes=[pltpu.VMEM((GROUP, 2 * XC, 8, 128), jnp.float32), pltpu.SemaphoreType.DMA((Y,))],
+        input_output_aliases={len(args) - 1: 0} if alias else {},
+        compiler_params=pltpu.CompilerParams(vmem_limit_bytes=16 << 20),
+        cost_estimate=pl.CostEstimate(flops=1_500_000_000, bytes_accessed=1 << 22, transcendentals=0),
+    )(*args)
 
 
 def return_kernel(at_ref, recv, field, updated, residual, new, rest, done):
@@ -154,7 +176,7 @@
         copy.wait()
 
 
-def fill_coefficients(diffusion, drift, label, below, above, coef):
+def coefficient_kernel(diffusion, drift, label, below, above, coef):
     lane = lax.broadcasted_iota(jnp.int32, (SPACE, 128), 1)
     tables = [jnp.zeros((SPACE, 128), jnp.float32)] * 8
     for n in range(diffusion.shape[0]):
@@ -163,10 +185,10 @@
         values = [1.0 - 6.0 * a, a - bz, a + bz, a - by, a + by, a - bx, a + bx, 1.0 - 6.0 * (a * COARSEN)]
         tables = [jnp.where(lane == n, value, table) for value, table in zip(values, tables)]
     for i in range(-HALO, ROWS + HALO):
-        ref, at = (below, EDGE + HALO + i) if i < 0 else (above, EDGE + i - ROWS) if i >= ROWS else (label, i)
+        ref, at = (below, (1, HALO + i)) if i < 0 else (above, (1, i - ROWS)) if i >= ROWS else (label, (i,))
         for par in range(2):
             for c in range(XC):
-                index = ref[at, par, c].astype(jnp.int32)
+                index = ref[(*at, par, c)].astype(jnp.int32)
                 for t in range(8):
                     coef[t, HALO + i, par, c] = jnp.take_along_axis(tables[t], index, axis=1, mode="promise_in_bounds")
 
@@ -231,63 +253,33 @@
     return [[rows[i] for i in range(ROWS)] for rows in all_rows]
 
 
-def forcing_rows(own, below, above):
-    first = EDGE + HALO
-
-    def at(i):
-        return pair(below, first + HALO + i) if i < 0 else pair(above, first + i - ROWS) if i >= ROWS else pair(own, i)
-
-    return at
-
-
 def minus(a, b):
     return [x - y for x, y in zip(a, b)]
 
 
-def fine_early_kernel(diffusion, drift, label, force, up, below, above, second, coef, r, first):
-    fill_coefficients(diffusion, drift, label, below, above, coef)
-    extra = forcing_rows(force, below, above)
-
-    def results(*times):
-        return fine_times(coef, extra, [[lambda i, ref=ref, k=k: pair(ref, k * ROWS + i) for ref in (up, below, above)] for k in times])
-
-    @pl.loop(0, EARLY // 2)
-    def _(n):
-        for k, rows in zip((2 * n, 2 * n + 1), results(2 * n, 2 * n + 1)):
-            for i in range(ROWS):
-                put(r, (k, i), minus(rows[i], pair(up, (k + 1) * ROWS + i)))
-
-    for i in range(ROWS):
-        put(first, (i,), pair(r, 0, i))
-    (rows,) = results(EARLY - 1)
-    for i in range(ROWS):
-        put(r, (EARLY - 1, i), minus(rows[i], pair(second, 0, i)))
-
-
-def fine_late_kernel(coef, force, edge_below, edge_above, second, below, above, order, r, beyond):
-    extra = forcing_rows(force, edge_below, edge_above)
-
-    def results(*times):
-        return fine_times(coef, extra, [[lambda i, ref=ref, k=k: pair(ref, k, i) for ref in (second, below, above)] for k in times])
-
-    @pl.loop(0, LATE // 2)
-    def _(n):
-        even, odd = results(2 * n, 2 * n + 1)
+def fine_kernel(n, coef, force, edge_below, edge_above, starts, below, above, *refs):
+    ks = MESSAGES[n]
+    other, results = refs[0], refs[-1 - (8 in ks) :]
+
+    def extra(i):
+        return pair(edge_below, 0, i + HALO) if i < 0 else pair(edge_above, 0, i - ROWS) if i >= ROWS else pair(force, i)
+
+    made = fine_times(
+        coef, extra, [[lambda i, ref=ref, m=m: pair(ref, m, i) for ref in (starts, below, above)] for m in range(len(ks))]
+    )
+    for m, (k, rows) in enumerate(zip(ks, made)):
         for i in range(ROWS):
-            put(r, (2 * n, i), minus(even[i], pair(second, 2 * n + 1, i)))
-
-            @pl.when(n == 0)
-            def _():
-                put(r, (1, i), minus(odd[i], pair(second, 2, i)))
-
-            @pl.when(n == 1)
-            def _():
-                put(beyond, (i,), odd[i])
-
-
-def residual_rows(first, early, late):
+            if k == 8:
+                put(results[1], (0, i), rows[i])
+            else:
+                ref, holder = (starts, ks) if k + 1 in ks else (other, MESSAGES[OTHER[n]])
+                put(results[0], (m, i), minus(rows[i], pair(ref, holder.index(k + 1), i)))
+
+
+def residual_rows(times, refs):
     def at(k, i):
-        return pair(first, i) if k == 0 else pair(early, k, i) if k < EARLY else pair(late, k - EARLY, i)
+        n = next(n for n, ks in enumerate(times) if k in ks)
+        return pair(refs[n], times[n].index(k), i)
 
     return at
 
@@ -337,62 +329,66 @@
     return [pair(ref, *at, i) for i in range(ROWS)]
 
 
-def start_kernel(time, width, coef, first, r_early, start, low, high):
-    r = residual_rows(first, r_early, None)
-    trajectory(coef, r, time, width, block(start), low, high)
-
-
-def middle_kernel(time, width, then, coef, first, r_early, r_late, start, below, above, errors, low, high):
-    r = residual_rows(first, r_early, r_late)
-    rows = advance(coef, r, time, width, block(start), below, above, errors)
+def start_kernel(times, time, width, coef, start, *refs):
+    low, high = refs[-2:]
+    trajectory(coef, residual_rows(times, refs), time, width, block(start, 0), low, high)
+
+
+def middle_kernel(times, time, width, then, coef, start, below, above, *refs):
+    errors, low, high = refs[-3:]
+    r = residual_rows(times, refs)
+    rows = advance(coef, r, time, width, block(start, 0), below, above, errors)
     trajectory(coef, r, time + width, then, rows, low, high)
 
 
-def end_kernel(time, width, coef, first, r_early, r_late, start, below, above, errors, last):
-    r = residual_rows(first, r_early, r_late)
-    rows = advance(coef, r, time, width, block(start, start.shape[0] - 1), below, above, errors)
+def end_kernel(times, time, width, coef, start, below, above, *refs):
+    errors, last = refs[-2:]
+    rows = advance(coef, residual_rows(times, refs), time, width, block(start, start.shape[0] - 1), below, above, errors)
     for i in range(ROWS):
-        put(last, (i,), rows[i])
+        put(last, (0, i), rows[i])
 
 
 def exchange(low, high):
     return lax.ppermute(high, ALL, UP), lax.ppermute(low, ALL, DOWN)
 
 
-def coarse(coef, first, r_early, r_late, start, time):
+def coarse(coef, r, start, time, behind=None):
     a, b = 4 - time, 4
-    low, high = call(
-        functools.partial(start_kernel, time, a), [f32(a, *ROW)] * 2, coef, first, r_early, start, flops=500_000_000
-    )
+    r = list(r)
+
+    def step(kernel, outs, flops, *args):
+        times, arrays = [ks for ks, _ in r], [array for _, array in r]
+        return call(functools.partial(kernel, times), outs, coef, *args, *arrays, flops=flops)
+
+    low, high = step(lambda ks, *refs: start_kernel(ks, time, a, *refs), [f32(a, *ROW)] * 2, 500_000_000, start)
     below, above = exchange(low, high)
-    if callable(r_late):
-        r_late = r_late(low)
-    given = coef, first, r_early, r_late
-    early, low, high = call(
-        functools.partial(middle_kernel, time, a, b), [f32(a, ROWS, *ROW)] + [f32(b, *ROW)] * 2,
-        *given, start, below, above, flops=1_000_000_000,
+    if behind:
+        r += behind[0](low)
+    early, low, high = step(
+        lambda ks, *refs: middle_kernel(ks, time, a, b, *refs), [f32(a, ROWS, *ROW)] + [f32(b, *ROW)] * 2, 1_000_000_000,
+        start, below, above,
     )
     below, above = exchange(low, high)
-    late, last = call(
-        functools.partial(end_kernel, 4, b), [f32(b, ROWS, *ROW), f32(ROWS, *ROW)],
-        *given, early, below, above, flops=500_000_000,
+    if behind:
+        r += behind[1](low)
+    late, last = step(
+        lambda ks, *refs: end_kernel(ks, 4, b, *refs), [f32(b, ROWS, *ROW), f32(1, ROWS, *ROW)], 500_000_000, early, below, above
     )
     return early, late, last
 
 
-def choose_kernel(at_ref, first, beyond, up, out):
+def choose_kernel(at_ref, first, beyond, starts, out):
     @pl.when(at_ref[0] == 0)
     def _():
-        out[...] = first[...]
+        out[0] = first[0]
 
     @pl.when(at_ref[0] == 1)
     def _():
-        out[...] = beyond[...] - up[ROWS : 2 * ROWS]
+        out[0] = beyond[0] - starts[1]
 
 
 def shards(initial, c_values, forcing, classes, diffusion, drift):
-    xh = lax.axis_index("xh")
-    at = jnp.stack([xh, lax.axis_index("y")])
+    at = jnp.stack([lax.axis_index("xh"), lax.axis_index("y")])
     one = f32(ROWS, *ROW)
 
     inputs = (c_values, initial, forcing, classes)
@@ -405,32 +401,50 @@
         compiler_params=pltpu.CompilerParams(vmem_limit_bytes=56 << 20),
     )(at, *inputs)
     recv = lax.all_to_all(send, RING, 0, 0, tiled=True)
-    message = f32(EDGE + 2 * HALO, *ROW)
-    up, down, second, label, force = call(unpack_kernel, [message, message, f32(LATE, ROWS, *ROW), one, one], recv)
-    edge_below, edge_above = exchange(down, up)
-    below, above = exchange(second, second)
-    coef, r_early, first = call(
-        fine_early_kernel, [f32(8, ROWS + 2 * HALO, *ROW), f32(EARLY, ROWS, *ROW), one],
-        diffusion, drift, label, force, up, edge_below, edge_above, second, flops=10_000_000_000, scalars=2,
-    )
+    outs = [f32(len(ks), ROWS, *ROW) for ks in MESSAGES] + [one, one] + [f32(2, HALO, *ROW)] * 2
+    *starts, label, force, low, high = call(unpack_kernel, outs, recv)
+
+    edges = exchange(low, high)
+    halos = [exchange(message, message) for message in starts[:3]]
+    coef = call(
+        coefficient_kernel, f32(8, ROWS + 2 * HALO, *ROW), diffusion, drift, label, *edges, flops=30_000_000_000, scalars=2
+    )
+
+    def fine(n, halo, *order):
+        ks = [k for k in MESSAGES[n] if k < 8]
+        results = [f32(len(ks), ROWS, *ROW)] + [f32(1, ROWS, *ROW)] * (8 in MESSAGES[n])
+        work = 1_500_000_000 * len(MESSAGES[n])
+        kernel = functools.partial(fine_kernel, n)
+        return call(kernel, results, coef, force, *edges, starts[n], *halo, starts[OTHER[n]], *order, flops=work)
+
+    r = [(MESSAGES[0], fine(0, halos[0])[0])]
     made = []
 
-    def make_late(order):
-        made.extend(
-            call(
-                fine_late_kernel, [f32(LATE - 1, ROWS, *ROW), one],
-                coef, force, edge_below, edge_above, second, below, above, order, flops=5_000_000_000,
-            )
-        )
-        return made[0]
-
-    early, late, last = coarse(coef, first, r_early, make_late, first, 1)
-    r_late, beyond = made
-    beyond = lax.ppermute(beyond, ALL, ACROSS)
+    def first_behind(order):
+        made.extend((MESSAGES[n], fine(n, halos[n], order)[0]) for n in (1, 2))
+        held = call(hold_kernel, f32(*starts[3].shape), starts[3], order)
+        halos.append(exchange(held, held))
+        return made[:2]
+
+    def second_behind(order):
+        residual, beyond = fine(3, halos[3], order)
+        made.extend([beyond, ((7,), residual)])
+        return made[3:]
+
+    early, late, last = coarse(coef, r, r[0][1], 1, (first_behind, second_behind))
+    beyond = lax.ppermute(made[2], ALL, ACROSS)
     start = lax.ppermute(last, ALL, ACROSS)
-    first = call(choose_kernel, one, at, first, beyond, up, scalars=1)
-    early, late, last = coarse(coef, first, r_early, r_late, start, 0)
-    back = call(return_pack_kernel, f32(GROUP, 4 * XC, 8, 128), early, late, first, r_early, r_late)
+    first = call(choose_kernel, f32(1, ROWS, *ROW), at, r[0][1], beyond, starts[0], scalars=1)
+    r = [((0,), first), r[0], *made[:2], made[3]]
+    back = []
+
+    def pack_residual(order):
+        kernel = functools.partial(residual_pack_kernel, [ks for ks, _ in r])
+        back.append(pack_call(kernel, 0, order, *[array for _, array in r]))
+        return []
+
+    early, late, last = coarse(coef, r, start, 0, (pack_residual, lambda order: []))
+    back = pack_call(error_pack_kernel, 1, early, late, back[0])
     got = lax.all_to_all(back, RING, 0, 0, tiled=True)
     return tuple(
         pl.pallas_call(

time: 198 us -> 189 us (0.955)
  waiting for transfers between devices: 41.3 us -> 26 us
  starting transfers between devices: 12.4 us -> 21.2 us
  Pallas kernels: 37.7 us -> 34.7 us
    ppermute x12 -> x18, waiting for transfers between devices: 34.2 us -> 17.6 us  [exchange(): return (lax.ppermute(high, ALL, UP), lax.ppermute(low, ALL, DOWN))]
    ppermute x12 -> x18, starting transfers between devices: 9.86 us -> 18.6 us  [exchange(): return (lax.ppermute(high, ALL, UP), lax.ppermute(low, ALL, DOWN))]
    pallas_call x11 -> x14, Pallas kernels: 30 us -> 23.3 us  [call(): pl.pallas_call(kernel, out_shape=outs, in_specs=[SMEM] * scalars + [VMEM]...]
    pallas_call x0 -> x2, Pallas kernels: none -> 3.69 us  [pack_call(): pl.pallas_call(kernel, out_shape=f32(GROUP, 4 * XC, 8, 128), in_specs=[VM...]
  transfers between devices with their start and end apart: 14 -> 20, of which waited for: 8 -> 13; matrix products, arithmetic and copies ran while one was open for 0% -> 0% of each run, Pallas kernels for 10% -> 11%
where the time goes in v2:
time: 189 us
  blocking collectives  106 us (56%)
  Pallas kernels  34.7 us (18%)
  waiting for transfers between devices  26 us (14%)
  starting transfers between devices  21.2 us (11%)
    all_to_all x1, blocking collectives, shards(): got = lax.all_to_all(back, RING, 0, 0, tiled=True)  57.7 us
    all_to_all x1, blocking collectives, shards(): recv = lax.all_to_all(send, RING, 0, 0, tiled=True)  47.8 us
    pallas_call x14, Pallas kernels, call(): pl.pallas_call(kernel, out_shape=outs, in_specs=[SMEM] * scalars + [VMEM]...  23.3 us
    ppermute x18, starting transfers between devices, exchange(): return (lax.ppermute(high, ALL, UP), lax.ppermute(low, ALL, DOWN))  18.6 us
    ppermute x18, waiting for transfers between devices, exchange(): return (lax.ppermute(high, ALL, UP), lax.ppermute(low, ALL, DOWN))  17.6 us
    ppermute x1, waiting for transfers between devices, shards(): start = lax.ppermute(last, ALL, ACROSS)  6.47 us
    pallas_call x1, Pallas kernels, shards(): pl.pallas_call(pack_kernel, out_shape=f32(GROUP, PARCEL, 8, 128), in_spec...  4.88 us
  transfers between devices with their start and end apart: 20, of which 13 were waited for; matrix products, arithmetic and copies ran while one was open for 0% of the time, Pallas kernels for 11%

profile of v2, /device:TPU:5, one launch (start us, length us, event | category | flops | bytes accessed | tf_op | source)
XLA Modules:
  0.0 189.1 jit_solution(2293332929060850851)
XLA Ops:
  1.2 4.9 %shard_map.77 = f32[64,11,8,128]{3,2,1,0:T(8,128)} custom-call(s32[2]{0:T(128)} %pad_add_fusion.at_ref, f32[2,2,256,512]{3,2,1,0:T(8,128)} %field.1, f32[2,256,512]{2,1,0:T(8,128)} %refs_1_.1, f32[2,256,512]{2,1,0:T(8,128)} %refs_2_.1, s32[2,256,512]{2,1,0:T(8,128)} %refs_3_.1), custom_call_target="tpu_custom_call" | custom-call | tf_op jit(solution)/shard_map/pallas_call | solution.py:395
  6.1 47.8 %all_to_all.10.recv = f32[64,11,8,128]{3,2,1,0:T(8,128)S(1)} all-to-all(f32[64,11,8,128]{3,2,1,0:T(8,128)} %shard_map.77), channel_id=1, replica_groups=mesh['xh'=2,'y'=4,'space'=16] {'y','space'}, dimensions={0} | all-to-all | bytes 5767168 | tf_op jit(solution)/shard_map/all_to_all | solution.py:403
  55.2 1.6 collective-permute-start.2
  56.8 1.7 collective-permute-start.6
  59.7 2.6 %collective-permute-start.7 = (f32[2,4,2,4,16,128]{5,4,3,2,1,0:T(8,128)S(1)}, f32[2,4,2,4,16,128]{5,4,3,2,1,0:T(8,128)S(1)}, u32[]{:S(2)}, u32[]{:S(2)}) collective-permute-start(f32[2,4,2,4,16,128]{5,4,3,2,1,0:T(8,128)S(1)} %get-tuple-element.29.refs_0_.starts), channel_id=1, source_target_pairs={{1,0},{16,1},{17,16},{32,17},{33,32},{48,33},{49,48},{52,49},{53,5... | collective-permute-start | bytes 1572872 | tf_op jit(solution)/shard_map/ppermute | solution.py:352
  62.5 3.4 %shard_map.79.coef.refs_0_ = f32[8,10,2,4,16,128]{5,4,3,2,1,0:T(8,128)S(1)} custom-call(f32[8]{0:T(128)S(1)} %copy-done.3, f32[3,8]{1,0:T(4,128)S(1)} %copy-done.2, f32[4,2,4,16,128]{4,3,2,1,0:T(8,128)S(1)} %get-tuple-element.24.label, f32[2,3,2,4,16,128]{5,4,3,2,1,0:T(8,128)S(1)} %collective-permute-done.below.edge_below, ...), custom_call_target="tpu_custom_call" | custom-call | flops 30000001024 | bytes 6291584 | tf_op jit(solution)/shard_map/pallas_call | solution.py:48
  65.9 2.2 %collective-permute-done.2.below = f32[3,4,2,4,16,128]{5,4,3,2,1,0:T(8,128)S(1)} collective-permute-done((f32[3,4,2,4,16,128]{5,4,3,2,1,0:T(8,128)S(1)}, f32[3,4,2,4,16,128]{5,4,3,2,1,0:T(8,128)S(1)}, u32[]{:S(2)}, u32[]{:S(2)}) %collective-permute-start.2) | collective-permute-done | bytes 786464 | tf_op jit(solution)/shard_map/ppermute | solution.py:352
  68.1 2.6 %collective-permute-start.9 = (f32[2,4,2,4,16,128]{5,4,3,2,1,0:T(8,128)S(1)}, f32[2,4,2,4,16,128]{5,4,3,2,1,0:T(8,128)S(1)}, u32[]{:S(2)}, u32[]{:S(2)}) collective-permute-start(f32[2,4,2,4,16,128]{5,4,3,2,1,0:T(8,128)S(1)} %get-tuple-element.32.refs_0_.starts), channel_id=1, source_target_pairs={{1,0},{16,1},{17,16},{32,17},{33,32},{48,33},{49,48},{52,49},{53,5... | collective-permute-start | bytes 1572872 | tf_op jit(solution)/shard_map/ppermute | solution.py:352
  70.9 4.0 %shard_map.80.refs_1_.refs_2_.refs_4_.first.refs_3_.refs_5_ = f32[3,4,2,4,16,128]{5,4,3,2,1,0:T(8,128)S(1)} custom-call(f32[8,10,2,4,16,128]{5,4,3,2,1,0:T(8,128)S(1)} %shard_map.79.coef.refs_0_, f32[4,2,4,16,128]{4,3,2,1,0:T(8,128)S(1)} %get-tuple-element.27.force, f32[2,3,2,4,16,128]{5,4,3,2,1,0:T(8,128)S(1)} %collective-permute-done.below.edge_below, ...), custom_call_target="tpu_custom_call" | custom-call | flops 4499999744 | bytes 9961472 | tf_op jit(solution)/shard_map/pallas_call | solution.py:48
  75.4 1.8 collective-permute-start.12
  77.3 2.7 %shard_map.82.refs_5_.refs_4_.refs_6_.refs_2_ = f32[2,4,2,4,16,128]{5,4,3,2,1,0:T(8,128)S(1)} custom-call(f32[8,10,2,4,16,128]{5,4,3,2,1,0:T(8,128)S(1)} %shard_map.79.coef.refs_0_, f32[4,2,4,16,128]{4,3,2,1,0:T(8,128)S(1)} %get-tuple-element.27.force, f32[2,3,2,4,16,128]{5,4,3,2,1,0:T(8,128)S(1)} %collective-permute-done.below.edge_below, ...), custom_call_target="tpu_custom_call" | custom-call | flops 3000000000 | bytes 9109504 | tf_op jit(solution)/shard_map/pallas_call | solution.py:48
  80.0 1.9 collective-permute-start.4
  82.1 2.7 %shard_map.83.refs_6_.refs_5_.refs_7_.refs_3_ = f32[2,4,2,4,16,128]{5,4,3,2,1,0:T(8,128)S(1)} custom-call(f32[8,10,2,4,16,128]{5,4,3,2,1,0:T(8,128)S(1)} %shard_map.79.coef.refs_0_, f32[4,2,4,16,128]{4,3,2,1,0:T(8,128)S(1)} %get-tuple-element.27.force, f32[2,3,2,4,16,128]{5,4,3,2,1,0:T(8,128)S(1)} %collective-permute-done.below.edge_below, ...), custom_call_target="tpu_custom_call" | custom-call | flops 3000000000 | bytes 9109504 | tf_op jit(solution)/shard_map/pallas_call | solution.py:48
  84.8 2.3 %collective-permute-done.4.refs_2_ = f32[3,2,4,16,128]{4,3,2,1,0:T(8,128)S(1)} collective-permute-done((f32[3,2,4,16,128]{4,3,2,1,0:T(8,128)S(1)}, f32[3,2,4,16,128]{4,3,2,1,0:T(8,128)S(1)}, u32[]{:S(2)}, u32[]{:S(2)}) %collective-permute-start.4) | collective-permute-done | bytes 196640 | tf_op jit(solution)/shard_map/ppermute | solution.py:352
  88.2 2.5 %collective-permute-start.10 = (f32[4,2,4,16,128]{4,3,2,1,0:T(8,128)S(1)}, f32[4,2,4,16,128]{4,3,2,1,0:T(8,128)S(1)}, u32[]{:S(2)}, u32[]{:S(2)}) collective-permute-start(f32[4,2,4,16,128]{4,3,2,1,0:T(8,128)S(1)} %get-tuple-element.35), channel_id=1, source_target_pairs={{0,1},{1,16},{16,17},{17,32},{32,33},{33,48},{48,49},{49,52},{52,5... | collective-permute-start | bytes 786440 | tf_op jit(solution)/shard_map/ppermute | solution.py:352
  90.9 2.7 %shard_map.86 = (f32[1,4,2,4,16,128]{5,4,3,2,1,0:T(8,128)S(1)}, f32[1,4,2,4,16,128]{5,4,3,2,1,0:T(8,128)S(1)}) custom-call(f32[8,10,2,4,16,128]{5,4,3,2,1,0:T(8,128)S(1)} %shard_map.79.coef.refs_0_, f32[4,2,4,16,128]{4,3,2,1,0:T(8,128)S(1)} %get-tuple-element.27.force, f32[2,3,2,4,16,128]{5,4,3,2,1,0:T(8,128)S(1)} %collective-permute-done.below.edge_below, ...), custom_call_target="tpu_custom_call" | custom-call | flops 3000000000 | bytes 9437184 | tf_op jit(solution)/shard_map/pallas_call | solution.py:48
  93.6 1.3 collective-permute-start.15
  94.9 1.6 collective-permute-done.11.refs_3_
  96.5 1.9 shard_map.87
  98.4 1.3 collective-permute-start.14
  99.7 1.9 %collective-permute-done.15.beyond = f32[1,4,2,4,16,128]{5,4,3,2,1,0:T(8,128)S(1)} collective-permute-done((f32[1,4,2,4,16,128]{5,4,3,2,1,0:T(8,128)S(1)}, f32[1,4,2,4,16,128]{5,4,3,2,1,0:T(8,128)S(1)}, u32[]{:S(2)}, u32[]{:S(2)}) %collective-permute-start.15) | collective-permute-done | bytes 262176 | tf_op jit(solution)/shard_map/ppermute | solution.py:435
  102.2 6.5 %collective-permute-done.14.refs_1_ = f32[1,4,2,4,16,128]{5,4,3,2,1,0:T(8,128)S(1)} collective-permute-done((f32[1,4,2,4,16,128]{5,4,3,2,1,0:T(8,128)S(1)}, f32[1,4,2,4,16,128]{5,4,3,2,1,0:T(8,128)S(1)}, u32[]{:S(2)}, u32[]{:S(2)}) %collective-permute-start.14) | collective-permute-done | bytes 262176 | tf_op jit(solution)/shard_map/ppermute | solution.py:436
  109.2 2.3 %collective-permute-start.16 = (f32[4,2,4,16,128]{4,3,2,1,0:T(8,128)S(1)}, f32[4,2,4,16,128]{4,3,2,1,0:T(8,128)S(1)}, u32[]{:S(2)}, u32[]{:S(2)}) collective-permute-start(f32[4,2,4,16,128]{4,3,2,1,0:T(8,128)S(1)} %get-tuple-element.40), channel_id=1, source_target_pairs={{0,1},{1,16},{16,17},{17,32},{32,33},{33,48},{48,49},{49,52},{52,5... | collective-permute-start | bytes 786440 | tf_op jit(solution)/shard_map/ppermute | solution.py:352
  111.5 3.3 %collective-permute-done.16.refs_2_ = f32[4,2,4,16,128]{4,3,2,1,0:T(8,128)S(1)} collective-permute-done((f32[4,2,4,16,128]{4,3,2,1,0:T(8,128)S(1)}, f32[4,2,4,16,128]{4,3,2,1,0:T(8,128)S(1)}, u32[]{:S(2)}, u32[]{:S(2)}) %collective-permute-start.16) | collective-permute-done | bytes 262176 | tf_op jit(solution)/shard_map/ppermute | solution.py:352
  114.8 2.5 %collective-permute-done.17.refs_3_ = f32[4,2,4,16,128]{4,3,2,1,0:T(8,128)S(1)} collective-permute-done((f32[4,2,4,16,128]{4,3,2,1,0:T(8,128)S(1)}, f32[4,2,4,16,128]{4,3,2,1,0:T(8,128)S(1)}, u32[]{:S(2)}, u32[]{:S(2)}) %collective-permute-start.17) | collective-permute-done | bytes 262176 | tf_op jit(solution)/shard_map/ppermute | solution.py:352
  117.3 1.4 shard_map.90
  119.2 1.8 shard_map.92.given
  122.1 2.8 %collective-permute-done.19.refs_3_ = f32[4,2,4,16,128]{4,3,2,1,0:T(8,128)S(1)} collective-permute-done((f32[4,2,4,16,128]{4,3,2,1,0:T(8,128)S(1)}, f32[4,2,4,16,128]{4,3,2,1,0:T(8,128)S(1)}, u32[]{:S(2)}, u32[]{:S(2)}) %collective-permute-start.19) | collective-permute-done | bytes 262176 | tf_op jit(solution)/shard_map/ppermute | solution.py:352
  124.9 1.6 shard_map.91
  126.5 1.8 shard_map.93
  128.3 57.7 %all_to_all.11.recv = f32[64,16,8,128]{3,2,1,0:T(8,128)S(1)} all-to-all(f32[64,16,8,128]{3,2,1,0:T(8,128)S(1)} %shard_map.93), channel_id=1, replica_groups=mesh['xh'=2,'y'=4,'space'=16] {'y','space'}, dimensions={0} | all-to-all | bytes 8388608 | tf_op jit(solution)/shard_map/all_to_all | solution.py:448
  186.0 2.9 %shard_map.94 = (f32[2,2,256,512]{3,2,1,0:T(8,128)}, f32[2,2,256,512]{3,2,1,0:T(8,128)}) custom-call(s32[2]{0:T(128)S(1)} %copy-done.1, f32[64,16,8,128]{3,2,1,0:T(8,128)S(1)} %all_to_all.11.recv, f32[2,2,256,512]{3,2,1,0:T(8,128)S(1)} %copy-done), custom_call_target="tpu_custom_call" | custom-call | tf_op jit(solution)/shard_map/pallas_call | solution.py:450
  (37 shorter events, 8.2 us)
Async XLA Ops:
  54.0 8.5 %copy-start.2 = (f32[3,8]{1,0:T(4,128)S(1)}, f32[3,8]{1,0:T(4,128)}, u32[]{:S(2)}) copy-start(f32[3,8]{1,0:T(4,128)} %drift.1) | copy-start | bytes 292
  54.0 8.5 %copy-start.3 = (f32[8]{0:T(128)S(1)}, f32[8]{0:T(128)}, u32[]{:S(2)}) copy-start(f32[8]{0:T(128)} %diffusion.1) | copy-start | bytes 100
  54.5 5.2 %collective-permute-start = (f32[2,3,2,4,16,128]{5,4,3,2,1,0:T(8,128)S(1)}, f32[2,3,2,4,16,128]{5,4,3,2,1,0:T(8,128)S(1)}, u32[]{:S(2)}, u32[]{:S(2)}) collective-permute-start(f32[2,3,2,4,16,128]{5,4,3,2,1,0:T(8,128)S(1)} %get-tuple-element.25), channel_id=1, source_target_pairs={{0,1},{1,16},{16,17},{17,32},{32,33},{33,48},{48,49},{49,52},{52,5... | collective-permute-start | bytes 1179656 | tf_op jit(solution)/shard_map/ppermute | solution.py:352
  55.0 7.5 %collective-permute-start.1 = (f32[2,3,2,4,16,128]{5,4,3,2,1,0:T(8,128)S(1)}, f32[2,3,2,4,16,128]{5,4,3,2,1,0:T(8,128)S(1)}, u32[]{:S(2)}, u32[]{:S(2)}) collective-permute-start(f32[2,3,2,4,16,128]{5,4,3,2,1,0:T(8,128)S(1)} %get-tuple-element.26), channel_id=1, source_target_pairs={{1,0},{16,1},{17,16},{32,17},{33,32},{48,33},{49,48},{52,49},{53,5... | collective-permute-start | bytes 1179656 | tf_op jit(solution)/shard_map/ppermute | solution.py:352
  55.2 13.0 %collective-permute-start.2 = (f32[3,4,2,4,16,128]{5,4,3,2,1,0:T(8,128)S(1)}, f32[3,4,2,4,16,128]{5,4,3,2,1,0:T(8,128)S(1)}, u32[]{:S(2)}, u32[]{:S(2)}) collective-permute-start(f32[3,4,2,4,16,128]{5,4,3,2,1,0:T(8,128)S(1)} %get-tuple-element.28.starts.refs_0_), channel_id=1, source_target_pairs={{0,1},{1,16},{16,17},{17,32},{32,33},{33,48},{48,49},{49,52},{52,5... | collective-permute-start | bytes 2359304 | tf_op jit(solution)/shard_map/ppermute | solution.py:352
  56.7 14.2 %collective-permute-start.3 = (f32[3,4,2,4,16,128]{5,4,3,2,1,0:T(8,128)S(1)}, f32[3,4,2,4,16,128]{5,4,3,2,1,0:T(8,128)S(1)}, u32[]{:S(2)}, u32[]{:S(2)}) collective-permute-start(f32[3,4,2,4,16,128]{5,4,3,2,1,0:T(8,128)S(1)} %get-tuple-element.28.starts.refs_0_), channel_id=1, source_target_pairs={{1,0},{16,1},{17,16},{32,17},{33,32},{48,33},{49,48},{52,49},{53,5... | collective-permute-start | bytes 2359304 | tf_op jit(solution)/shard_map/ppermute | solution.py:352
  56.8 18.5 %collective-permute-start.6 = (f32[2,4,2,4,16,128]{5,4,3,2,1,0:T(8,128)S(1)}, f32[2,4,2,4,16,128]{5,4,3,2,1,0:T(8,128)S(1)}, u32[]{:S(2)}, u32[]{:S(2)}) collective-permute-start(f32[2,4,2,4,16,128]{5,4,3,2,1,0:T(8,128)S(1)} %get-tuple-element.29.refs_0_.starts), channel_id=1, source_target_pairs={{0,1},{1,16},{16,17},{17,32},{32,33},{33,48},{48,49},{49,52},{52,5... | collective-permute-start | bytes 1572872 | tf_op jit(solution)/shard_map/ppermute | solution.py:352
  59.7 17.5 %collective-permute-start.7 = (f32[2,4,2,4,16,128]{5,4,3,2,1,0:T(8,128)S(1)}, f32[2,4,2,4,16,128]{5,4,3,2,1,0:T(8,128)S(1)}, u32[]{:S(2)}, u32[]{:S(2)}) collective-permute-start(f32[2,4,2,4,16,128]{5,4,3,2,1,0:T(8,128)S(1)} %get-tuple-element.29.refs_0_.starts), channel_id=1, source_target_pairs={{1,0},{16,1},{17,16},{32,17},{33,32},{48,33},{49,48},{52,49},{53,5... | collective-permute-start | bytes 1572872 | tf_op jit(solution)/shard_map/ppermute | solution.py:352
  62.5 17.6 %collective-permute-start.8 = (f32[2,4,2,4,16,128]{5,4,3,2,1,0:T(8,128)S(1)}, f32[2,4,2,4,16,128]{5,4,3,2,1,0:T(8,128)S(1)}, u32[]{:S(2)}, u32[]{:S(2)}) collective-permute-start(f32[2,4,2,4,16,128]{5,4,3,2,1,0:T(8,128)S(1)} %get-tuple-element.32.refs_0_.starts), channel_id=1, source_target_pairs={{0,1},{1,16},{16,17},{17,32},{32,33},{33,48},{48,49},{49,52},{52,5... | collective-permute-start | bytes 1572872 | tf_op jit(solution)/shard_map/ppermute | solution.py:352
  68.1 14.0 %collective-permute-start.9 = (f32[2,4,2,4,16,128]{5,4,3,2,1,0:T(8,128)S(1)}, f32[2,4,2,4,16,128]{5,4,3,2,1,0:T(8,128)S(1)}, u32[]{:S(2)}, u32[]{:S(2)}) collective-permute-start(f32[2,4,2,4,16,128]{5,4,3,2,1,0:T(8,128)S(1)} %get-tuple-element.32.refs_0_.starts), channel_id=1, source_target_pairs={{1,0},{16,1},{17,16},{32,17},{33,32},{48,33},{49,48},{52,49},{53,5... | collective-permute-start | bytes 1572872 | tf_op jit(solution)/shard_map/ppermute | solution.py:352
  75.2 11.9 %collective-permute-start.5 = (f32[3,2,4,16,128]{4,3,2,1,0:T(8,128)S(1)}, f32[3,2,4,16,128]{4,3,2,1,0:T(8,128)S(1)}, u32[]{:S(2)}, u32[]{:S(2)}) collective-permute-start(f32[3,2,4,16,128]{4,3,2,1,0:T(8,128)S(1)} %get-tuple-element.31.refs_1_.order), channel_id=1, source_target_pairs={{1,0},{16,1},{17,16},{32,17},{33,32},{48,33},{49,48},{52,49},{53,5... | collective-permute-start | bytes 589832 | tf_op jit(solution)/shard_map/ppermute | solution.py:352
  75.4 15.5 %collective-permute-start.12 = (f32[2,4,2,4,16,128]{5,4,3,2,1,0:T(8,128)S(1)}, f32[2,4,2,4,16,128]{5,4,3,2,1,0:T(8,128)S(1)}, u32[]{:S(2)}, u32[]{:S(2)}) collective-permute-start(f32[2,4,2,4,16,128]{5,4,3,2,1,0:T(8,128)S(1)} %shard_map.85), channel_id=1, source_target_pairs={{0,1},{1,16},{16,17},{17,32},{32,33},{33,48},{48,49},{49,52},{52,5... | collective-permute-start | bytes 1572872 | tf_op jit(solution)/shard_map/ppermute | solution.py:352
  77.2 13.7 %collective-permute-start.13 = (f32[2,4,2,4,16,128]{5,4,3,2,1,0:T(8,128)S(1)}, f32[2,4,2,4,16,128]{5,4,3,2,1,0:T(8,128)S(1)}, u32[]{:S(2)}, u32[]{:S(2)}) collective-permute-start(f32[2,4,2,4,16,128]{5,4,3,2,1,0:T(8,128)S(1)} %shard_map.85), channel_id=1, source_target_pairs={{1,0},{16,1},{17,16},{32,17},{33,32},{48,33},{49,48},{52,49},{53,5... | collective-permute-start | bytes 1572872 | tf_op jit(solution)/shard_map/ppermute | solution.py:352
  80.0 7.0 %collective-permute-start.4 = (f32[3,2,4,16,128]{4,3,2,1,0:T(8,128)S(1)}, f32[3,2,4,16,128]{4,3,2,1,0:T(8,128)S(1)}, u32[]{:S(2)}, u32[]{:S(2)}) collective-permute-start(f32[3,2,4,16,128]{4,3,2,1,0:T(8,128)S(1)} %get-tuple-element.30), channel_id=1, source_target_pairs={{0,1},{1,16},{16,17},{17,32},{32,33},{33,48},{48,49},{49,52},{52,5... | collective-permute-start | bytes 589832 | tf_op jit(solution)/shard_map/ppermute | solution.py:352
  88.2 6.7 %collective-permute-start.10 = (f32[4,2,4,16,128]{4,3,2,1,0:T(8,128)S(1)}, f32[4,2,4,16,128]{4,3,2,1,0:T(8,128)S(1)}, u32[]{:S(2)}, u32[]{:S(2)}) collective-permute-start(f32[4,2,4,16,128]{4,3,2,1,0:T(8,128)S(1)} %get-tuple-element.35), channel_id=1, source_target_pairs={{0,1},{1,16},{16,17},{17,32},{32,33},{33,48},{48,49},{49,52},{52,5... | collective-permute-start | bytes 786440 | tf_op jit(solution)/shard_map/ppermute | solution.py:352
  90.7 5.8 %collective-permute-start.11 = (f32[4,2,4,16,128]{4,3,2,1,0:T(8,128)S(1)}, f32[4,2,4,16,128]{4,3,2,1,0:T(8,128)S(1)}, u32[]{:S(2)}, u32[]{:S(2)}) collective-permute-start(f32[4,2,4,16,128]{4,3,2,1,0:T(8,128)S(1)} %get-tuple-element.36.refs_1_), channel_id=1, source_target_pairs={{1,0},{16,1},{17,16},{32,17},{33,32},{48,33},{49,48},{52,49},{53,5... | collective-permute-start | bytes 786440 | tf_op jit(solution)/shard_map/ppermute | solution.py:352
  93.6 8.0 %collective-permute-start.15 = (f32[1,4,2,4,16,128]{5,4,3,2,1,0:T(8,128)S(1)}, f32[1,4,2,4,16,128]{5,4,3,2,1,0:T(8,128)S(1)}, u32[]{:S(2)}, u32[]{:S(2)}) collective-permute-start(f32[1,4,2,4,16,128]{5,4,3,2,1,0:T(8,128)S(1)} %get-tuple-element.39), channel_id=1, source_target_pairs={{0,66},{1,67},{2,64},{3,65},{4,70},{5,71},{6,68},{7,69},{8,74},{9,... | collective-permute-start | bytes 786440 | tf_op jit(solution)/shard_map/ppermute | solution.py:435
  96.5 5.1 %copy-start.1 = (s32[2]{0:T(128)S(1)}, s32[2]{0:T(128)}, u32[]{:S(2)}) copy-start(s32[2]{0:T(128)} %pad_add_fusion.at_ref) | copy-start | bytes 28
  98.4 10.3 %collective-permute-start.14 = (f32[1,4,2,4,16,128]{5,4,3,2,1,0:T(8,128)S(1)}, f32[1,4,2,4,16,128]{5,4,3,2,1,0:T(8,128)S(1)}, u32[]{:S(2)}, u32[]{:S(2)}) collective-permute-start(f32[1,4,2,4,16,128]{5,4,3,2,1,0:T(8,128)S(1)} %get-tuple-element.38), channel_id=1, source_target_pairs={{0,66},{1,67},{2,64},{3,65},{4,70},{5,71},{6,68},{7,69},{8,74},{9,... | collective-permute-start | bytes 786440 | tf_op jit(solution)/shard_map/ppermute | solution.py:436
  109.2 5.6 %collective-permute-start.16 = (f32[4,2,4,16,128]{4,3,2,1,0:T(8,128)S(1)}, f32[4,2,4,16,128]{4,3,2,1,0:T(8,128)S(1)}, u32[]{:S(2)}, u32[]{:S(2)}) collective-permute-start(f32[4,2,4,16,128]{4,3,2,1,0:T(8,128)S(1)} %get-tuple-element.40), channel_id=1, source_target_pairs={{0,1},{1,16},{16,17},{17,32},{32,33},{33,48},{48,49},{49,52},{52,5... | collective-permute-start | bytes 786440 | tf_op jit(solution)/shard_map/ppermute | solution.py:352
  111.5 5.8 %collective-permute-start.17 = (f32[4,2,4,16,128]{4,3,2,1,0:T(8,128)S(1)}, f32[4,2,4,16,128]{4,3,2,1,0:T(8,128)S(1)}, u32[]{:S(2)}, u32[]{:S(2)}) collective-permute-start(f32[4,2,4,16,128]{4,3,2,1,0:T(8,128)S(1)} %get-tuple-element.41.order), channel_id=1, source_target_pairs={{1,0},{16,1},{17,16},{32,17},{33,32},{48,33},{49,48},{52,49},{53,5... | collective-permute-start | bytes 786440 | tf_op jit(solution)/shard_map/ppermute | solution.py:352
  118.7 3.4 %collective-permute-start.18 = (f32[4,2,4,16,128]{4,3,2,1,0:T(8,128)S(1)}, f32[4,2,4,16,128]{4,3,2,1,0:T(8,128)S(1)}, u32[]{:S(2)}, u32[]{:S(2)}) collective-permute-start(f32[4,2,4,16,128]{4,3,2,1,0:T(8,128)S(1)} %get-tuple-element.43), channel_id=1, source_target_pairs={{0,1},{1,16},{16,17},{17,32},{32,33},{33,48},{48,49},{49,52},{52,5... | collective-permute-start | bytes 786440 | tf_op jit(solution)/shard_map/ppermute | solution.py:352
  118.7 6.1 %collective-permute-start.19 = (f32[4,2,4,16,128]{4,3,2,1,0:T(8,128)S(1)}, f32[4,2,4,16,128]{4,3,2,1,0:T(8,128)S(1)}, u32[]{:S(2)}, u32[]{:S(2)}) collective-permute-start(f32[4,2,4,16,128]{4,3,2,1,0:T(8,128)S(1)} %get-tuple-element.44), channel_id=1, source_target_pairs={{1,0},{16,1},{17,16},{32,17},{33,32},{48,33},{49,48},{52,49},{53,5... | collective-permute-start | bytes 786440 | tf_op jit(solution)/shard_map/ppermute | solution.py:352
  128.3 57.7 %copy-start = (f32[2,2,256,512]{3,2,1,0:T(8,128)S(1)}, f32[2,2,256,512]{3,2,1,0:T(8,128)}, u32[]{:S(2)}) copy-start(f32[2,2,256,512]{3,2,1,0:T(8,128)} %field.1) | copy-start | bytes 6291460

commit v3 on v2

--- a/solution.py
+++ b/solution.py
@@ -51,7 +51,7 @@
         in_specs=[SMEM] * scalars + [VMEM] * (len(args) - scalars),
         out_specs=VMEM if single else [VMEM] * len(out_list),
         compiler_params=pltpu.CompilerParams(vmem_limit_bytes=16 << 20),
-        cost_estimate=pl.CostEstimate(flops=flops, bytes_accessed=size, transcendentals=0),
+        cost_estimate=pl.CostEstimate(flops=flops, bytes_accessed=1024, transcendentals=0),
     )(*args)
 
 
@@ -119,41 +119,47 @@
     out[...] = source[...]
 
 
-def return_pack_kernel(n, rows, back, scratch, done):
-    flat = scratch.reshape(GROUP * 2 * XC * 8, 128)
+def pack_parcels(n, ys, rows, back, scratch, done):
+    flat = scratch.reshape(len(ys) * SPACE * 2 * XC * 8, 128)
     copies = []
-    for y in range(Y):
+    for m, y in enumerate(ys):
         for tt in range(2):
             for row in range(ROWS):
                 for par, part in enumerate(rows(2 * y + tt, row)):
                     for c in range(XC):
-                        at = (y * SPACE * 2 + tt) * XC + c
+                        at = (m * SPACE * 2 + tt) * XC + c
                         flat[pl.ds(at * 8 + row * 2 + par, SPACE, stride=2 * XC * 8), :] = part[c]
-        some = pl.ds(y * SPACE, SPACE)
-        copies.append(pltpu.make_async_copy(scratch.at[some], back.at[some, pl.ds(n * 2 * XC, 2 * XC)], done.at[y]))
+        to = back.at[pl.ds(y * SPACE, SPACE), pl.ds(n * 2 * XC, 2 * XC)]
+        copies.append(pltpu.make_async_copy(scratch.at[pl.ds(m * SPACE, SPACE)], to, done.at[m]))
         copies[-1].start()
     for copy in copies:
         copy.wait()
 
 
 def residual_pack_kernel(times, order, *refs):
-    return_pack_kernel(1, residual_rows(times, refs), *refs[-3:])
-
-
-def error_pack_kernel(early, late, given, *refs):
-    return_pack_kernel(0, lambda k, i: pair((early, late)[k // 4], k % 4, i), *refs)
-
-
-def pack_call(kernel, alias, *args):
+    pack_parcels(1, range(Y), residual_rows(times, refs), *refs[-3:])
+
+
+def early_pack_kernel(early, given, *refs):
+    pack_parcels(0, range(Y // 2), lambda k, i: pair(early, k, i), *refs)
+
+
+def finish_kernel(times, coef, start, below, above, *refs):
+    back, errors, scratch, done = refs[-4:]
+    advance(coef, residual_rows(times, refs), 4, 4, block(start, start.shape[0] - 1), below, above, errors)
+    pack_parcels(0, range(Y // 2, Y), lambda k, i: pair(errors, k - 4, i), back, scratch, done)
+
+
+def pack_call(kernel, alias, count, *args, more=()):
     return pl.pallas_call(
         kernel,
         out_shape=f32(GROUP, 4 * XC, 8, 128),
         in_specs=[VMEM] * (len(args) - alias) + [pl.BlockSpec(memory_space=pl.ANY)] * alias,
         out_specs=pl.BlockSpec(memory_space=pl.ANY),
-        scratch_shapes=[pltpu.VMEM((GROUP, 2 * XC, 8, 128), jnp.float32), pltpu.SemaphoreType.DMA((Y,))],
+        scratch_shapes=[*more, pltpu.VMEM((count * SPACE, 2 * XC, 8, 128), jnp.float32), pltpu.SemaphoreType.DMA((count,))],
         input_output_aliases={len(args) - 1: 0} if alias else {},
         compiler_params=pltpu.CompilerParams(vmem_limit_bytes=16 << 20),
-        cost_estimate=pl.CostEstimate(flops=1_500_000_000, bytes_accessed=1 << 22, transcendentals=0),
+        cost_estimate=pl.CostEstimate(flops=0, bytes_accessed=1024, transcendentals=0),
     )(*args)
 
 
@@ -320,8 +326,9 @@
                 new_high[i] = [COARSEN * coef[4, HALO + ROWS - 1 + i, p] * source_high[p] for p in range(2)]
         rows = [sweep_row(coef, i, padded[i + 1], padded[i + 2], padded[i], r(first + j, i), True) for i in range(ROWS)]
         dev_low, dev_high = new_low, new_high
-        for i in range(ROWS):
-            put(store, (j, i), rows[i])
+        if store is not None:
+            for i in range(ROWS):
+                put(store, (j, i), rows[i])
     return rows
 
 
@@ -334,25 +341,27 @@
     trajectory(coef, residual_rows(times, refs), time, width, block(start, 0), low, high)
 
 
-def middle_kernel(times, time, width, then, coef, start, below, above, *refs):
+def middle_kernel(times, time, width, then, whole, coef, start, below, above, *refs):
     errors, low, high = refs[-3:]
     r = residual_rows(times, refs)
-    rows = advance(coef, r, time, width, block(start, 0), below, above, errors)
+    rows = advance(coef, r, time, width, block(start, 0), below, above, errors if whole else None)
+    if not whole:
+        for i in range(ROWS):
+            put(errors, (0, i), rows[i])
     trajectory(coef, r, time + width, then, rows, low, high)
 
 
-def end_kernel(times, time, width, coef, start, below, above, *refs):
-    errors, last = refs[-2:]
-    rows = advance(coef, residual_rows(times, refs), time, width, block(start, start.shape[0] - 1), below, above, errors)
+def end_kernel(times, coef, start, below, above, *refs):
+    rows = advance(coef, residual_rows(times, refs), 4, 4, block(start, 0), below, above, None)
     for i in range(ROWS):
-        put(last, (0, i), rows[i])
+        put(refs[-1], (0, i), rows[i])
 
 
 def exchange(low, high):
     return lax.ppermute(high, ALL, UP), lax.ppermute(low, ALL, DOWN)
 
 
-def coarse(coef, r, start, time, behind=None):
+def coarse(coef, r, start, time, behind, whole):
     a, b = 4 - time, 4
     r = list(r)
 
@@ -362,19 +371,14 @@
 
     low, high = step(lambda ks, *refs: start_kernel(ks, time, a, *refs), [f32(a, *ROW)] * 2, 500_000_000, start)
     below, above = exchange(low, high)
-    if behind:
-        r += behind[0](low)
+    r += behind[0](low)
     early, low, high = step(
-        lambda ks, *refs: middle_kernel(ks, time, a, b, *refs), [f32(a, ROWS, *ROW)] + [f32(b, *ROW)] * 2, 1_000_000_000,
-        start, below, above,
+        lambda ks, *refs: middle_kernel(ks, time, a, b, whole, *refs),
+        [f32(a if whole else 1, ROWS, *ROW)] + [f32(b, *ROW)] * 2, 1_000_000_000, start, below, above,
     )
     below, above = exchange(low, high)
-    if behind:
-        r += behind[1](low)
-    late, last = step(
-        lambda ks, *refs: end_kernel(ks, 4, b, *refs), [f32(b, ROWS, *ROW), f32(1, ROWS, *ROW)], 500_000_000, early, below, above
-    )
-    return early, late, last
+    r += behind[1](low, early)
+    return early, below, above, r
 
 
 def choose_kernel(at_ref, first, beyond, starts, out):
@@ -407,7 +411,7 @@
     edges = exchange(low, high)
     halos = [exchange(message, message) for message in starts[:3]]
     coef = call(
-        coefficient_kernel, f32(8, ROWS + 2 * HALO, *ROW), diffusion, drift, label, *edges, flops=30_000_000_000, scalars=2
+        coefficient_kernel, f32(8, ROWS + 2 * HALO, *ROW), diffusion, drift, label, *edges, flops=3_000_000_000, scalars=2
     )
 
     def fine(n, halo, *order):
@@ -415,7 +419,7 @@
         results = [f32(len(ks), ROWS, *ROW)] + [f32(1, ROWS, *ROW)] * (8 in MESSAGES[n])
         work = 1_500_000_000 * len(MESSAGES[n])
         kernel = functools.partial(fine_kernel, n)
-        return call(kernel, results, coef, force, *edges, starts[n], *halo, starts[OTHER[n]], *order, flops=work)
+        return call(kernel, results, coef, force, *edges, starts[n], *halo, starts[OTHER[n]], *order, flops=0)
 
     r = [(MESSAGES[0], fine(0, halos[0])[0])]
     made = []
@@ -426,25 +430,33 @@
         halos.append(exchange(held, held))
         return made[:2]
 
-    def second_behind(order):
+    def second_behind(order, early):
         residual, beyond = fine(3, halos[3], order)
         made.extend([beyond, ((7,), residual)])
         return made[3:]
 
-    early, late, last = coarse(coef, r, r[0][1], 1, (first_behind, second_behind))
+    *given, r_all = coarse(coef, r, r[0][1], 1, (first_behind, second_behind), False)
+    kernel = functools.partial(end_kernel, [ks for ks, _ in r_all])
+    last = call(kernel, f32(1, ROWS, *ROW), coef, *given, *[array for _, array in r_all], flops=0)
     beyond = lax.ppermute(made[2], ALL, ACROSS)
     start = lax.ppermute(last, ALL, ACROSS)
     first = call(choose_kernel, f32(1, ROWS, *ROW), at, r[0][1], beyond, starts[0], scalars=1)
     r = [((0,), first), r[0], *made[:2], made[3]]
+    times, arrays = [ks for ks, _ in r], [array for _, array in r]
     back = []
 
     def pack_residual(order):
-        kernel = functools.partial(residual_pack_kernel, [ks for ks, _ in r])
-        back.append(pack_call(kernel, 0, order, *[array for _, array in r]))
+        back.append(pack_call(functools.partial(residual_pack_kernel, times), 0, Y, order, *arrays))
         return []
 
-    early, late, last = coarse(coef, r, start, 0, (pack_residual, lambda order: []))
-    back = pack_call(error_pack_kernel, 1, early, late, back[0])
+    def pack_early(order, early):
+        back.append(pack_call(early_pack_kernel, 1, Y // 2, early, back[0]))
+        return []
+
+    *given, _ = coarse(coef, r, start, 0, (pack_residual, pack_early), True)
+    errors = [pltpu.VMEM((4, ROWS, *ROW), jnp.float32)]
+    kernel = functools.partial(finish_kernel, times)
+    back = pack_call(kernel, 1, Y // 2, coef, *given, *arrays, back[1], more=errors)
     got = lax.all_to_all(back, RING, 0, 0, tiled=True)
     return tuple(
         pl.pallas_call(

time: 189 us -> 187 us (0.989)
  starting transfers between devices: 21.2 us -> 14.8 us
  waiting for transfers between devices: 26 us -> 32.2 us
    ppermute x18, starting transfers between devices: 18.6 us -> 12.2 us  [exchange(): return (lax.ppermute(high, ALL, UP), lax.ppermute(low, ALL, DOWN))]
    ppermute x1, waiting for transfers between devices: 1.93 us -> 6.55 us  [shards(): beyond = lax.ppermute(made[2], ALL, ACROSS)]
    ppermute x18, waiting for transfers between devices: 17.6 us -> 20.7 us  [exchange(): return (lax.ppermute(high, ALL, UP), lax.ppermute(low, ALL, DOWN))]
    pallas_call x14 -> x13, Pallas kernels: 23.3 us -> 20.6 us  [call(): pl.pallas_call(kernel, out_shape=outs, in_specs=[SMEM] * scalars + [VMEM]...]
    pallas_call x2 -> x3, Pallas kernels: 3.69 us -> 4.52 us  [pack_call(): pl.pallas_call(kernel, out_shape=f32(GROUP, 4 * XC, 8, 128), in_specs=[VM...]
  transfers between devices with their start and end apart: 20 -> 20, of which waited for: 13 -> 9; matrix products, arithmetic and copies ran while one was open for 0% -> 0% of each run, Pallas kernels for 11% -> 11%
where the time goes in v3:
time: 187 us
  blocking collectives  105 us (56%)
  Pallas kernels  32.9 us (18%)
  waiting for transfers between devices  32.2 us (17%)
  starting transfers between devices  14.8 us (8%)
    all_to_all x1, blocking collectives, shards(): got = lax.all_to_all(back, RING, 0, 0, tiled=True)  57.4 us
    all_to_all x1, blocking collectives, shards(): recv = lax.all_to_all(send, RING, 0, 0, tiled=True)  47.8 us
    ppermute x18, waiting for transfers between devices, exchange(): return (lax.ppermute(high, ALL, UP), lax.ppermute(low, ALL, DOWN))  20.7 us
    pallas_call x13, Pallas kernels, call(): pl.pallas_call(kernel, out_shape=outs, in_specs=[SMEM] * scalars + [VMEM]...  20.6 us
    ppermute x18, starting transfers between devices, exchange(): return (lax.ppermute(high, ALL, UP), lax.ppermute(low, ALL, DOWN))  12.2 us
    ppermute x1, waiting for transfers between devices, shards(): beyond = lax.ppermute(made[2], ALL, ACROSS)  6.55 us
    ppermute x1, waiting for transfers between devices, shards(): start = lax.ppermute(last, ALL, ACROSS)  5.03 us
    pallas_call x1, Pallas kernels, shards(): pl.pallas_call(pack_kernel, out_shape=f32(GROUP, PARCEL, 8, 128), in_spec...  4.87 us
  transfers between devices with their start and end apart: 20, of which 9 were waited for; matrix products, arithmetic and copies ran while one was open for 0% of the time, Pallas kernels for 11%

profile of v3, /device:TPU:5, one launch (start us, length us, event | category | flops | bytes accessed | tf_op | source)
XLA Modules:
  0.0 186.9 jit_solution(2626148522351864938)
XLA Ops:
  1.2 4.9 %shard_map.77 = f32[64,11,8,128]{3,2,1,0:T(8,128)} custom-call(s32[2]{0:T(128)} %pad_add_fusion.at_ref, f32[2,2,256,512]{3,2,1,0:T(8,128)} %field.1, f32[2,256,512]{2,1,0:T(8,128)} %refs_1_.1, f32[2,256,512]{2,1,0:T(8,128)} %refs_2_.1, s32[2,256,512]{2,1,0:T(8,128)} %refs_3_.1), custom_call_target="tpu_custom_call" | custom-call | tf_op jit(solution)/shard_map/pallas_call | solution.py:399
  6.1 47.8 %all_to_all.10.recv = f32[64,11,8,128]{3,2,1,0:T(8,128)S(1)} all-to-all(f32[64,11,8,128]{3,2,1,0:T(8,128)} %shard_map.77), channel_id=1, replica_groups=mesh['xh'=2,'y'=4,'space'=16] {'y','space'}, dimensions={0} | all-to-all | bytes 5767168 | tf_op jit(solution)/shard_map/all_to_all | solution.py:407
  55.1 1.2 collective-permute-start
  56.3 1.7 collective-permute-start.2
  58.1 3.0 %collective-permute-done.below.edge_below = f32[2,3,2,4,16,128]{5,4,3,2,1,0:T(8,128)S(1)} collective-permute-done((f32[2,3,2,4,16,128]{5,4,3,2,1,0:T(8,128)S(1)}, f32[2,3,2,4,16,128]{5,4,3,2,1,0:T(8,128)S(1)}, u32[]{:S(2)}, u32[]{:S(2)}) %collective-permute-start) | collective-permute-done | bytes 393248 | tf_op jit(solution)/shard_map/ppermute | solution.py:361
  61.1 2.5 %collective-permute-start.6 = (f32[2,4,2,4,16,128]{5,4,3,2,1,0:T(8,128)S(1)}, f32[2,4,2,4,16,128]{5,4,3,2,1,0:T(8,128)S(1)}, u32[]{:S(2)}, u32[]{:S(2)}) collective-permute-start(f32[2,4,2,4,16,128]{5,4,3,2,1,0:T(8,128)S(1)} %get-tuple-element.27.refs_0_.starts), channel_id=1, source_target_pairs={{0,1},{1,16},{16,17},{17,32},{32,33},{33,48},{48,49},{49,52},{52,5... | collective-permute-start | bytes 1572872 | tf_op jit(solution)/shard_map/ppermute | solution.py:361
  63.5 7.0 %collective-permute-done.1.above.edge_above = f32[2,3,2,4,16,128]{5,4,3,2,1,0:T(8,128)S(1)} collective-permute-done((f32[2,3,2,4,16,128]{5,4,3,2,1,0:T(8,128)S(1)}, f32[2,3,2,4,16,128]{5,4,3,2,1,0:T(8,128)S(1)}, u32[]{:S(2)}, u32[]{:S(2)}) %collective-permute-start.1) | collective-permute-done | bytes 393248 | tf_op jit(solution)/shard_map/ppermute | solution.py:361
  70.5 1.7 collective-permute-start.8
  72.3 3.4 %shard_map.79.coef.refs_0_ = f32[8,10,2,4,16,128]{5,4,3,2,1,0:T(8,128)S(1)} custom-call(f32[8]{0:T(128)S(1)} %copy-done.3, f32[3,8]{1,0:T(4,128)S(1)} %copy-done.2, f32[4,2,4,16,128]{4,3,2,1,0:T(8,128)S(1)} %get-tuple-element.22.label, f32[2,3,2,4,16,128]{5,4,3,2,1,0:T(8,128)S(1)} %collective-permute-done.below.edge_below, ...), custom_call_target="tpu_custom_call" | custom-call | flops 3000000000 | bytes 1024 | tf_op jit(solution)/shard_map/pallas_call | solution.py:48
  75.7 4.0 %shard_map.80.refs_1_.refs_2_.refs_4_.refs_0_.first.refs_3_.refs_5_ = f32[3,4,2,4,16,128]{5,4,3,2,1,0:T(8,128)S(1)} custom-call(f32[8,10,2,4,16,128]{5,4,3,2,1,0:T(8,128)S(1)} %shard_map.79.coef.refs_0_, f32[4,2,4,16,128]{4,3,2,1,0:T(8,128)S(1)} %get-tuple-element.25.force, f32[2,3,2,4,16,128]{5,4,3,2,1,0:T(8,128)S(1)} %collective-permute-done.below.edge_below, ...), custom_call_target="tpu_custom_call" | custom-call | bytes 1024 | tf_op jit(solution)/shard_map/pallas_call | solution.py:48
  80.8 0.9 collective-permute-done.9.above
  81.7 0.7 collective-permute-start.12
  82.4 2.7 %shard_map.82.refs_5_.refs_1_.refs_4_.refs_6_.refs_2_ = f32[2,4,2,4,16,128]{5,4,3,2,1,0:T(8,128)S(1)} custom-call(f32[8,10,2,4,16,128]{5,4,3,2,1,0:T(8,128)S(1)} %shard_map.79.coef.refs_0_, f32[4,2,4,16,128]{4,3,2,1,0:T(8,128)S(1)} %get-tuple-element.25.force, f32[2,3,2,4,16,128]{5,4,3,2,1,0:T(8,128)S(1)} %collective-permute-done.below.edge_below, ...), custom_call_target="tpu_custom_call" | custom-call | bytes 1024 | tf_op jit(solution)/shard_map/pallas_call | solution.py:48
  85.1 2.7 %shard_map.83.refs_6_.refs_2_.refs_5_.refs_7_.refs_3_ = f32[2,4,2,4,16,128]{5,4,3,2,1,0:T(8,128)S(1)} custom-call(f32[8,10,2,4,16,128]{5,4,3,2,1,0:T(8,128)S(1)} %shard_map.79.coef.refs_0_, f32[4,2,4,16,128]{4,3,2,1,0:T(8,128)S(1)} %get-tuple-element.25.force, f32[2,3,2,4,16,128]{5,4,3,2,1,0:T(8,128)S(1)} %collective-permute-done.below.edge_below, ...), custom_call_target="tpu_custom_call" | custom-call | bytes 1024 | tf_op jit(solution)/shard_map/pallas_call | solution.py:48
  87.8 1.1 shard_map.84
  89.5 1.4 collective-permute-done.13.above
  90.9 2.7 %shard_map.86 = (f32[1,4,2,4,16,128]{5,4,3,2,1,0:T(8,128)S(1)}, f32[1,4,2,4,16,128]{5,4,3,2,1,0:T(8,128)S(1)}) custom-call(f32[8,10,2,4,16,128]{5,4,3,2,1,0:T(8,128)S(1)} %shard_map.79.coef.refs_0_, f32[4,2,4,16,128]{4,3,2,1,0:T(8,128)S(1)} %get-tuple-element.25.force, f32[2,3,2,4,16,128]{5,4,3,2,1,0:T(8,128)S(1)} %collective-permute-done.below.edge_below, ...), custom_call_target="tpu_custom_call" | custom-call | bytes 1024 | tf_op jit(solution)/shard_map/pallas_call | solution.py:48
  93.5 1.3 collective-permute-start.15
  94.9 0.9 shard_map.87
  95.8 1.3 collective-permute-start.14
  97.1 6.6 %collective-permute-done.15.beyond = f32[1,4,2,4,16,128]{5,4,3,2,1,0:T(8,128)S(1)} collective-permute-done((f32[1,4,2,4,16,128]{5,4,3,2,1,0:T(8,128)S(1)}, f32[1,4,2,4,16,128]{5,4,3,2,1,0:T(8,128)S(1)}, u32[]{:S(2)}, u32[]{:S(2)}) %collective-permute-start.15) | collective-permute-done | bytes 262176 | tf_op jit(solution)/shard_map/ppermute | solution.py:441
  104.2 5.0 %collective-permute-done.14.refs_1_ = f32[1,4,2,4,16,128]{5,4,3,2,1,0:T(8,128)S(1)} collective-permute-done((f32[1,4,2,4,16,128]{5,4,3,2,1,0:T(8,128)S(1)}, f32[1,4,2,4,16,128]{5,4,3,2,1,0:T(8,128)S(1)}, u32[]{:S(2)}, u32[]{:S(2)}) %collective-permute-start.14) | collective-permute-done | bytes 262176 | tf_op jit(solution)/shard_map/ppermute | solution.py:442
  109.7 1.8 collective-permute-start.16
  111.6 3.3 %collective-permute-done.16.refs_2_ = f32[4,2,4,16,128]{4,3,2,1,0:T(8,128)S(1)} collective-permute-done((f32[4,2,4,16,128]{4,3,2,1,0:T(8,128)S(1)}, f32[4,2,4,16,128]{4,3,2,1,0:T(8,128)S(1)}, u32[]{:S(2)}, u32[]{:S(2)}) %collective-permute-start.16) | collective-permute-done | bytes 262176 | tf_op jit(solution)/shard_map/ppermute | solution.py:361
  114.9 2.5 %collective-permute-done.17.refs_3_ = f32[4,2,4,16,128]{4,3,2,1,0:T(8,128)S(1)} collective-permute-done((f32[4,2,4,16,128]{4,3,2,1,0:T(8,128)S(1)}, f32[4,2,4,16,128]{4,3,2,1,0:T(8,128)S(1)}, u32[]{:S(2)}, u32[]{:S(2)}) %collective-permute-start.17) | collective-permute-done | bytes 262176 | tf_op jit(solution)/shard_map/ppermute | solution.py:361
  117.4 1.3 shard_map.90
  119.3 1.8 shard_map.91.given
  121.1 0.9 shard_map.92.refs_5_
  122.1 2.6 %collective-permute-done.19.above = f32[4,2,4,16,128]{4,3,2,1,0:T(8,128)S(1)} collective-permute-done((f32[4,2,4,16,128]{4,3,2,1,0:T(8,128)S(1)}, f32[4,2,4,16,128]{4,3,2,1,0:T(8,128)S(1)}, u32[]{:S(2)}, u32[]{:S(2)}) %collective-permute-start.19) | collective-permute-done | bytes 262176 | tf_op jit(solution)/shard_map/ppermute | solution.py:361
  124.7 1.7 shard_map.93
  126.4 57.4 %all_to_all.11.recv = f32[64,16,8,128]{3,2,1,0:T(8,128)S(1)} all-to-all(f32[64,16,8,128]{3,2,1,0:T(8,128)S(1)} %shard_map.93), channel_id=1, replica_groups=mesh['xh'=2,'y'=4,'space'=16] {'y','space'}, dimensions={0} | all-to-all | bytes 8388608 | tf_op jit(solution)/shard_map/all_to_all | solution.py:460
  183.8 2.9 %shard_map.94 = (f32[2,2,256,512]{3,2,1,0:T(8,128)}, f32[2,2,256,512]{3,2,1,0:T(8,128)}) custom-call(s32[2]{0:T(128)S(1)} %copy-done.1, f32[64,16,8,128]{3,2,1,0:T(8,128)S(1)} %all_to_all.11.recv, f32[2,2,256,512]{3,2,1,0:T(8,128)S(1)} %copy-done), custom_call_target="tpu_custom_call" | custom-call | tf_op jit(solution)/shard_map/pallas_call | solution.py:462
  (37 shorter events, 5.1 us)
Async XLA Ops:
  6.1 66.2 %copy-start.2 = (f32[3,8]{1,0:T(4,128)S(1)}, f32[3,8]{1,0:T(4,128)}, u32[]{:S(2)}) copy-start(f32[3,8]{1,0:T(4,128)} %drift.1) | copy-start | bytes 292
  6.1 66.1 %copy-start.3 = (f32[8]{0:T(128)S(1)}, f32[8]{0:T(128)}, u32[]{:S(2)}) copy-start(f32[8]{0:T(128)} %diffusion.1) | copy-start | bytes 100
  54.5 16.0 %collective-permute-start.3 = (f32[3,4,2,4,16,128]{5,4,3,2,1,0:T(8,128)S(1)}, f32[3,4,2,4,16,128]{5,4,3,2,1,0:T(8,128)S(1)}, u32[]{:S(2)}, u32[]{:S(2)}) collective-permute-start(f32[3,4,2,4,16,128]{5,4,3,2,1,0:T(8,128)S(1)} %get-tuple-element.26.starts.refs_0_), channel_id=1, source_target_pairs={{1,0},{16,1},{17,16},{32,17},{33,32},{48,33},{49,48},{52,49},{53,5... | collective-permute-start | bytes 2359304 | tf_op jit(solution)/shard_map/ppermute | solution.py:361
  55.1 6.0 %collective-permute-start = (f32[2,3,2,4,16,128]{5,4,3,2,1,0:T(8,128)S(1)}, f32[2,3,2,4,16,128]{5,4,3,2,1,0:T(8,128)S(1)}, u32[]{:S(2)}, u32[]{:S(2)}) collective-permute-start(f32[2,3,2,4,16,128]{5,4,3,2,1,0:T(8,128)S(1)} %get-tuple-element.23), channel_id=1, source_target_pairs={{0,1},{1,16},{16,17},{17,32},{32,33},{33,48},{48,49},{49,52},{52,5... | collective-permute-start | bytes 1179656 | tf_op jit(solution)/shard_map/ppermute | solution.py:361
  56.3 14.2 %collective-permute-start.1 = (f32[2,3,2,4,16,128]{5,4,3,2,1,0:T(8,128)S(1)}, f32[2,3,2,4,16,128]{5,4,3,2,1,0:T(8,128)S(1)}, u32[]{:S(2)}, u32[]{:S(2)}) collective-permute-start(f32[2,3,2,4,16,128]{5,4,3,2,1,0:T(8,128)S(1)} %get-tuple-element.24), channel_id=1, source_target_pairs={{1,0},{16,1},{17,16},{32,17},{33,32},{48,33},{49,48},{52,49},{53,5... | collective-permute-start | bytes 1179656 | tf_op jit(solution)/shard_map/ppermute | solution.py:361
  56.3 19.4 %collective-permute-start.2 = (f32[3,4,2,4,16,128]{5,4,3,2,1,0:T(8,128)S(1)}, f32[3,4,2,4,16,128]{5,4,3,2,1,0:T(8,128)S(1)}, u32[]{:S(2)}, u32[]{:S(2)}) collective-permute-start(f32[3,4,2,4,16,128]{5,4,3,2,1,0:T(8,128)S(1)} %get-tuple-element.26.starts.refs_0_), channel_id=1, source_target_pairs={{0,1},{1,16},{16,17},{17,32},{32,33},{33,48},{48,49},{49,52},{52,5... | collective-permute-start | bytes 2359304 | tf_op jit(solution)/shard_map/ppermute | solution.py:361
  58.1 22.0 %collective-permute-start.7 = (f32[2,4,2,4,16,128]{5,4,3,2,1,0:T(8,128)S(1)}, f32[2,4,2,4,16,128]{5,4,3,2,1,0:T(8,128)S(1)}, u32[]{:S(2)}, u32[]{:S(2)}) collective-permute-start(f32[2,4,2,4,16,128]{5,4,3,2,1,0:T(8,128)S(1)} %get-tuple-element.27.refs_0_.starts), channel_id=1, source_target_pairs={{1,0},{16,1},{17,16},{32,17},{33,32},{48,33},{49,48},{52,49},{53,5... | collective-permute-start | bytes 1572872 | tf_op jit(solution)/shard_map/ppermute | solution.py:361
  61.1 19.6 %collective-permute-start.6 = (f32[2,4,2,4,16,128]{5,4,3,2,1,0:T(8,128)S(1)}, f32[2,4,2,4,16,128]{5,4,3,2,1,0:T(8,128)S(1)}, u32[]{:S(2)}, u32[]{:S(2)}) collective-permute-start(f32[2,4,2,4,16,128]{5,4,3,2,1,0:T(8,128)S(1)} %get-tuple-element.27.refs_0_.starts), channel_id=1, source_target_pairs={{0,1},{1,16},{16,17},{17,32},{32,33},{33,48},{48,49},{49,52},{52,5... | collective-permute-start | bytes 1572872 | tf_op jit(solution)/shard_map/ppermute | solution.py:361
  70.5 11.2 %collective-permute-start.9 = (f32[2,4,2,4,16,128]{5,4,3,2,1,0:T(8,128)S(1)}, f32[2,4,2,4,16,128]{5,4,3,2,1,0:T(8,128)S(1)}, u32[]{:S(2)}, u32[]{:S(2)}) collective-permute-start(f32[2,4,2,4,16,128]{5,4,3,2,1,0:T(8,128)S(1)} %get-tuple-element.30.refs_0_.starts), channel_id=1, source_target_pairs={{1,0},{16,1},{17,16},{32,17},{33,32},{48,33},{49,48},{52,49},{53,5... | collective-permute-start | bytes 1572872 | tf_op jit(solution)/shard_map/ppermute | solution.py:361
  70.5 14.6 %collective-permute-start.8 = (f32[2,4,2,4,16,128]{5,4,3,2,1,0:T(8,128)S(1)}, f32[2,4,2,4,16,128]{5,4,3,2,1,0:T(8,128)S(1)}, u32[]{:S(2)}, u32[]{:S(2)}) collective-permute-start(f32[2,4,2,4,16,128]{5,4,3,2,1,0:T(8,128)S(1)} %get-tuple-element.30.refs_0_.starts), channel_id=1, source_target_pairs={{0,1},{1,16},{16,17},{17,32},{32,33},{33,48},{48,49},{49,52},{52,5... | collective-permute-start | bytes 1572872 | tf_op jit(solution)/shard_map/ppermute | solution.py:361
  80.0 7.8 %collective-permute-start.4 = (f32[3,2,4,16,128]{4,3,2,1,0:T(8,128)S(1)}, f32[3,2,4,16,128]{4,3,2,1,0:T(8,128)S(1)}, u32[]{:S(2)}, u32[]{:S(2)}) collective-permute-start(f32[3,2,4,16,128]{4,3,2,1,0:T(8,128)S(1)} %get-tuple-element.28), channel_id=1, source_target_pairs={{0,1},{1,16},{16,17},{17,32},{32,33},{33,48},{48,49},{49,52},{52,5... | collective-permute-start | bytes 589832 | tf_op jit(solution)/shard_map/ppermute | solution.py:361
  80.1 7.7 %collective-permute-start.5 = (f32[3,2,4,16,128]{4,3,2,1,0:T(8,128)S(1)}, f32[3,2,4,16,128]{4,3,2,1,0:T(8,128)S(1)}, u32[]{:S(2)}, u32[]{:S(2)}) collective-permute-start(f32[3,2,4,16,128]{4,3,2,1,0:T(8,128)S(1)} %get-tuple-element.29.refs_1_.order), channel_id=1, source_target_pairs={{1,0},{16,1},{17,16},{32,17},{33,32},{48,33},{49,48},{52,49},{53,5... | collective-permute-start | bytes 589832 | tf_op jit(solution)/shard_map/ppermute | solution.py:361
  80.6 10.2 %collective-permute-start.13 = (f32[2,4,2,4,16,128]{5,4,3,2,1,0:T(8,128)S(1)}, f32[2,4,2,4,16,128]{5,4,3,2,1,0:T(8,128)S(1)}, u32[]{:S(2)}, u32[]{:S(2)}) collective-permute-start(f32[2,4,2,4,16,128]{5,4,3,2,1,0:T(8,128)S(1)} %shard_map.85), channel_id=1, source_target_pairs={{1,0},{16,1},{17,16},{32,17},{33,32},{48,33},{49,48},{52,49},{53,5... | collective-permute-start | bytes 1572872 | tf_op jit(solution)/shard_map/ppermute | solution.py:361
  81.7 9.1 %collective-permute-start.12 = (f32[2,4,2,4,16,128]{5,4,3,2,1,0:T(8,128)S(1)}, f32[2,4,2,4,16,128]{5,4,3,2,1,0:T(8,128)S(1)}, u32[]{:S(2)}, u32[]{:S(2)}) collective-permute-start(f32[2,4,2,4,16,128]{5,4,3,2,1,0:T(8,128)S(1)} %shard_map.85), channel_id=1, source_target_pairs={{0,1},{1,16},{16,17},{17,32},{32,33},{33,48},{48,49},{49,52},{52,5... | collective-permute-start | bytes 1572872 | tf_op jit(solution)/shard_map/ppermute | solution.py:361
  88.9 6.0 %collective-permute-start.10 = (f32[4,2,4,16,128]{4,3,2,1,0:T(8,128)S(1)}, f32[4,2,4,16,128]{4,3,2,1,0:T(8,128)S(1)}, u32[]{:S(2)}, u32[]{:S(2)}) collective-permute-start(f32[4,2,4,16,128]{4,3,2,1,0:T(8,128)S(1)} %get-tuple-element.33), channel_id=1, source_target_pairs={{0,1},{1,16},{16,17},{17,32},{32,33},{33,48},{48,49},{49,52},{52,5... | collective-permute-start | bytes 786440 | tf_op jit(solution)/shard_map/ppermute | solution.py:361
  89.1 5.8 %collective-permute-start.11 = (f32[4,2,4,16,128]{4,3,2,1,0:T(8,128)S(1)}, f32[4,2,4,16,128]{4,3,2,1,0:T(8,128)S(1)}, u32[]{:S(2)}, u32[]{:S(2)}) collective-permute-start(f32[4,2,4,16,128]{4,3,2,1,0:T(8,128)S(1)} %get-tuple-element.34.refs_1_), channel_id=1, source_target_pairs={{1,0},{16,1},{17,16},{32,17},{33,32},{48,33},{49,48},{52,49},{53,5... | collective-permute-start | bytes 786440 | tf_op jit(solution)/shard_map/ppermute | solution.py:361
  93.5 10.1 %collective-permute-start.15 = (f32[1,4,2,4,16,128]{5,4,3,2,1,0:T(8,128)S(1)}, f32[1,4,2,4,16,128]{5,4,3,2,1,0:T(8,128)S(1)}, u32[]{:S(2)}, u32[]{:S(2)}) collective-permute-start(f32[1,4,2,4,16,128]{5,4,3,2,1,0:T(8,128)S(1)} %get-tuple-element.36), channel_id=1, source_target_pairs={{0,66},{1,67},{2,64},{3,65},{4,70},{5,71},{6,68},{7,69},{8,74},{9,... | collective-permute-start | bytes 786440 | tf_op jit(solution)/shard_map/ppermute | solution.py:441
  94.9 8.8 %copy-start.1 = (s32[2]{0:T(128)S(1)}, s32[2]{0:T(128)}, u32[]{:S(2)}) copy-start(s32[2]{0:T(128)} %pad_add_fusion.at_ref) | copy-start | bytes 28
  95.8 13.5 %collective-permute-start.14 = (f32[1,4,2,4,16,128]{5,4,3,2,1,0:T(8,128)S(1)}, f32[1,4,2,4,16,128]{5,4,3,2,1,0:T(8,128)S(1)}, u32[]{:S(2)}, u32[]{:S(2)}) collective-permute-start(f32[1,4,2,4,16,128]{5,4,3,2,1,0:T(8,128)S(1)} %shard_map.87), channel_id=1, source_target_pairs={{0,66},{1,67},{2,64},{3,65},{4,70},{5,71},{6,68},{7,69},{8,74},{9,... | collective-permute-start | bytes 786440 | tf_op jit(solution)/shard_map/ppermute | solution.py:442
  109.7 5.2 %collective-permute-start.16 = (f32[4,2,4,16,128]{4,3,2,1,0:T(8,128)S(1)}, f32[4,2,4,16,128]{4,3,2,1,0:T(8,128)S(1)}, u32[]{:S(2)}, u32[]{:S(2)}) collective-permute-start(f32[4,2,4,16,128]{4,3,2,1,0:T(8,128)S(1)} %get-tuple-element.37), channel_id=1, source_target_pairs={{0,1},{1,16},{16,17},{17,32},{32,33},{33,48},{48,49},{49,52},{52,5... | collective-permute-start | bytes 786440 | tf_op jit(solution)/shard_map/ppermute | solution.py:361
  111.6 5.8 %collective-permute-start.17 = (f32[4,2,4,16,128]{4,3,2,1,0:T(8,128)S(1)}, f32[4,2,4,16,128]{4,3,2,1,0:T(8,128)S(1)}, u32[]{:S(2)}, u32[]{:S(2)}) collective-permute-start(f32[4,2,4,16,128]{4,3,2,1,0:T(8,128)S(1)} %get-tuple-element.38.order), channel_id=1, source_target_pairs={{1,0},{16,1},{17,16},{32,17},{33,32},{48,33},{49,48},{52,49},{53,5... | collective-permute-start | bytes 786440 | tf_op jit(solution)/shard_map/ppermute | solution.py:361
  118.7 3.4 %collective-permute-start.18 = (f32[4,2,4,16,128]{4,3,2,1,0:T(8,128)S(1)}, f32[4,2,4,16,128]{4,3,2,1,0:T(8,128)S(1)}, u32[]{:S(2)}, u32[]{:S(2)}) collective-permute-start(f32[4,2,4,16,128]{4,3,2,1,0:T(8,128)S(1)} %get-tuple-element.40), channel_id=1, source_target_pairs={{0,1},{1,16},{16,17},{17,32},{32,33},{33,48},{48,49},{49,52},{52,5... | collective-permute-start | bytes 786440 | tf_op jit(solution)/shard_map/ppermute | solution.py:361
  118.8 5.9 %collective-permute-start.19 = (f32[4,2,4,16,128]{4,3,2,1,0:T(8,128)S(1)}, f32[4,2,4,16,128]{4,3,2,1,0:T(8,128)S(1)}, u32[]{:S(2)}, u32[]{:S(2)}) collective-permute-start(f32[4,2,4,16,128]{4,3,2,1,0:T(8,128)S(1)} %get-tuple-element.41), channel_id=1, source_target_pairs={{1,0},{16,1},{17,16},{32,17},{33,32},{48,33},{49,48},{52,49},{53,5... | collective-permute-start | bytes 786440 | tf_op jit(solution)/shard_map/ppermute | solution.py:361
  126.4 57.4 %copy-start = (f32[2,2,256,512]{3,2,1,0:T(8,128)S(1)}, f32[2,2,256,512]{3,2,1,0:T(8,128)}, u32[]{:S(2)}) copy-start(f32[2,2,256,512]{3,2,1,0:T(8,128)} %field.1) | copy-start | bytes 6291460

commit v4 on v3

--- a/solution.py
+++ b/solution.py
@@ -90,13 +90,27 @@
 OTHER = (1, 2, 3, 0)
 
 
-def unpack_kernel(recv, *refs):
-    messages, (label, force, low, high) = refs[:4], refs[4:]
+def parcel_piece(recv):
     flat = recv.reshape(GROUP * PARCEL * 8, 128)
-
-    def piece(y, n, row, par):
-        return flat[pl.ds((y * SPACE * PARCEL + n) * 8 + row * 2 + par, SPACE, stride=PARCEL * 8), :]
-
+    return lambda y, n, row, par: flat[pl.ds((y * SPACE * PARCEL + n) * 8 + row * 2 + par, SPACE, stride=PARCEL * 8), :]
+
+
+def unpack_shared_kernel(recv, label, force, low, high):
+    piece = parcel_piece(recv)
+    for y in range(Y):
+        for row in range(ROWS):
+            for par in range(2):
+                for n, ref in enumerate((force, label)):
+                    part = piece(y, 2 * XC + 1 + n, row, par)
+                    ref[row, par, y] = part
+                    if row < HALO:
+                        low[n, row, par, y] = part
+                    if row >= ROWS - HALO:
+                        high[n, row - ROWS + HALO, par, y] = part
+
+
+def unpack_kernel(recv, order, *messages):
+    piece = parcel_piece(recv)
     for y in range(Y):
         for row in range(ROWS):
             for par in range(2):
@@ -106,13 +120,6 @@
                             for c in range(XC):
                                 ref[starts.index(2 * y + tt + 1), row, par, c] = piece(y, tt * XC + c, row, par)
                 messages[0][0, row, par, y] = piece(y, 2 * XC, row, par)
-                for n, ref in enumerate((force, label)):
-                    part = piece(y, 2 * XC + 1 + n, row, par)
-                    ref[row, par, y] = part
-                    if row < HALO:
-                        low[n, row, par, y] = part
-                    if row >= ROWS - HALO:
-                        high[n, row - ROWS + HALO, par, y] = part
 
 
 def hold_kernel(source, order, out):
@@ -405,11 +412,10 @@
         compiler_params=pltpu.CompilerParams(vmem_limit_bytes=56 << 20),
     )(at, *inputs)
     recv = lax.all_to_all(send, RING, 0, 0, tiled=True)
-    outs = [f32(len(ks), ROWS, *ROW) for ks in MESSAGES] + [one, one] + [f32(2, HALO, *ROW)] * 2
-    *starts, label, force, low, high = call(unpack_kernel, outs, recv)
-
+    label, force, low, high = call(unpack_shared_kernel, [one, one] + [f32(2, HALO, *ROW)] * 2, recv)
     edges = exchange(low, high)
-    halos = [exchange(message, message) for message in starts[:3]]
+    starts = call(unpack_kernel, [f32(len(ks), ROWS, *ROW) for ks in MESSAGES], recv, low)
+    halos = [exchange(message, message) for message in starts[:2]]
     coef = call(
         coefficient_kernel, f32(8, ROWS + 2 * HALO, *ROW), diffusion, drift, label, *edges, flops=3_000_000_000, scalars=2
     )
@@ -422,6 +428,8 @@
         return call(kernel, results, coef, force, *edges, starts[n], *halo, starts[OTHER[n]], *order, flops=0)
 
     r = [(MESSAGES[0], fine(0, halos[0])[0])]
+    third = call(hold_kernel, f32(*starts[2].shape), starts[2], coef)
+    halos.append(exchange(third, third))
     made = []
 
     def first_behind(order):

time: 187 us -> 186 us (level)
    ppermute x1, waiting for transfers between devices: 6.55 us -> 4.16 us  [shards(): beyond = lax.ppermute(made[2], ALL, ACROSS)]
    pallas_call x13 -> x15, Pallas kernels: 20.6 us -> 20.8 us  [call(): pl.pallas_call(kernel, out_shape=outs, in_specs=[SMEM] * scalars + [VMEM]...]
  transfers between devices with their start and end apart: 20 -> 20, of which waited for: 9 -> 12; matrix products, arithmetic and copies ran while one was open for 0% -> 0% of each run, Pallas kernels for 11% -> 12%
where the time goes in v4:
time: 186 us
  blocking collectives  105 us (56%)
  Pallas kernels  33 us (18%)
  waiting for transfers between devices  30.7 us (17%)
  starting transfers between devices  14.9 us (8%)
    all_to_all x1, blocking collectives, shards(): got = lax.all_to_all(back, RING, 0, 0, tiled=True)  57.4 us
    all_to_all x1, blocking collectives, shards(): recv = lax.all_to_all(send, RING, 0, 0, tiled=True)  47.8 us
    ppermute x18, waiting for transfers between devices, exchange(): return (lax.ppermute(high, ALL, UP), lax.ppermute(low, ALL, DOWN))  21.5 us
    pallas_call x15, Pallas kernels, call(): pl.pallas_call(kernel, out_shape=outs, in_specs=[SMEM] * scalars + [VMEM]...  20.8 us
    ppermute x18, starting transfers between devices, exchange(): return (lax.ppermute(high, ALL, UP), lax.ppermute(low, ALL, DOWN))  12.3 us
    ppermute x1, waiting for transfers between devices, shards(): start = lax.ppermute(last, ALL, ACROSS)  5.03 us
    pallas_call x1, Pallas kernels, shards(): pl.pallas_call(pack_kernel, out_shape=f32(GROUP, PARCEL, 8, 128), in_spec...  4.87 us
    pallas_call x3, Pallas kernels, pack_call(): pl.pallas_call(kernel, out_shape=f32(GROUP, 4 * XC, 8, 128), in_specs=[VM...  4.52 us
  transfers between devices with their start and end apart: 20, of which 12 were waited for; matrix products, arithmetic and copies ran while one was open for 0% of the time, Pallas kernels for 12%

profile of v4, /device:TPU:5, one launch (start us, length us, event | category | flops | bytes accessed | tf_op | source)
XLA Modules:
  0.0 185.5 jit_solution(5945329739176577825)
XLA Ops:
  0.6 0.6 pad_add_fusion.at_ref
  1.3 4.9 %shard_map.77 = f32[64,11,8,128]{3,2,1,0:T(8,128)} custom-call(s32[2]{0:T(128)} %pad_add_fusion.at_ref, f32[2,2,256,512]{3,2,1,0:T(8,128)} %field.1, f32[2,256,512]{2,1,0:T(8,128)} %refs_1_.1, f32[2,256,512]{2,1,0:T(8,128)} %refs_2_.1, s32[2,256,512]{2,1,0:T(8,128)} %refs_3_.1), custom_call_target="tpu_custom_call" | custom-call | tf_op jit(solution)/shard_map/pallas_call | solution.py:406
  6.1 47.8 %all_to_all.10.recv = f32[64,11,8,128]{3,2,1,0:T(8,128)S(1)} all-to-all(f32[64,11,8,128]{3,2,1,0:T(8,128)} %shard_map.77), channel_id=1, replica_groups=mesh['xh'=2,'y'=4,'space'=16] {'y','space'}, dimensions={0} | all-to-all | bytes 5767168 | tf_op jit(solution)/shard_map/all_to_all | solution.py:414
  55.2 1.7 collective-permute-start.3
  57.4 1.9 %collective-permute-done.below.edge_below = f32[2,3,2,4,16,128]{5,4,3,2,1,0:T(8,128)S(1)} collective-permute-done((f32[2,3,2,4,16,128]{5,4,3,2,1,0:T(8,128)S(1)}, f32[2,3,2,4,16,128]{5,4,3,2,1,0:T(8,128)S(1)}, u32[]{:S(2)}, u32[]{:S(2)}) %collective-permute-start) | collective-permute-done | bytes 393248 | tf_op jit(solution)/shard_map/ppermute | solution.py:368
  59.3 2.5 %collective-permute-start.6 = (f32[2,4,2,4,16,128]{5,4,3,2,1,0:T(8,128)S(1)}, f32[2,4,2,4,16,128]{5,4,3,2,1,0:T(8,128)S(1)}, u32[]{:S(2)}, u32[]{:S(2)}) collective-permute-start(f32[2,4,2,4,16,128]{5,4,3,2,1,0:T(8,128)S(1)} %get-tuple-element.27.refs_0_.starts), channel_id=1, source_target_pairs={{0,1},{1,16},{16,17},{17,32},{32,33},{33,48},{48,49},{49,52},{52,5... | collective-permute-start | bytes 1572872 | tf_op jit(solution)/shard_map/ppermute | solution.py:368
  62.1 3.4 %shard_map.79.coef.refs_0_.order = f32[8,10,2,4,16,128]{5,4,3,2,1,0:T(8,128)S(1)} custom-call(f32[8]{0:T(128)S(1)} %copy-done.3, f32[3,8]{1,0:T(4,128)S(1)} %copy-done.2, f32[4,2,4,16,128]{4,3,2,1,0:T(8,128)S(1)} %get-tuple-element.22.label, f32[2,3,2,4,16,128]{5,4,3,2,1,0:T(8,128)S(1)} %collective-permute-done.below.edge_below, ...), custom_call_target="tpu_custom_call" | custom-call | flops 3000000000 | bytes 1024 | tf_op jit(solution)/shard_map/pallas_call | solution.py:48
  65.7 4.9 %collective-permute-done.3.above = f32[3,4,2,4,16,128]{5,4,3,2,1,0:T(8,128)S(1)} collective-permute-done((f32[3,4,2,4,16,128]{5,4,3,2,1,0:T(8,128)S(1)}, f32[3,4,2,4,16,128]{5,4,3,2,1,0:T(8,128)S(1)}, u32[]{:S(2)}, u32[]{:S(2)}) %collective-permute-start.3) | collective-permute-done | bytes 786464 | tf_op jit(solution)/shard_map/ppermute | solution.py:368
  70.6 4.0 %shard_map.81.refs_1_.refs_2_.refs_4_.refs_0_.first.refs_3_.refs_5_ = f32[3,4,2,4,16,128]{5,4,3,2,1,0:T(8,128)S(1)} custom-call(f32[8,10,2,4,16,128]{5,4,3,2,1,0:T(8,128)S(1)} %shard_map.79.coef.refs_0_.order, f32[4,2,4,16,128]{4,3,2,1,0:T(8,128)S(1)} %get-tuple-element.25.force, f32[2,3,2,4,16,128]{5,4,3,2,1,0:T(8,128)S(1)} %collective-permute-done.below.edge_below, ...), custom_call_target="tpu_custom_call" | custom-call | bytes 1024 | tf_op jit(solution)/shard_map/pallas_call | solution.py:48
  75.3 0.8 collective-permute-done.7.above
  76.2 1.9 %collective-permute-start.13 = (f32[2,4,2,4,16,128]{5,4,3,2,1,0:T(8,128)S(1)}, f32[2,4,2,4,16,128]{5,4,3,2,1,0:T(8,128)S(1)}, u32[]{:S(2)}, u32[]{:S(2)}) collective-permute-start(f32[2,4,2,4,16,128]{5,4,3,2,1,0:T(8,128)S(1)} %shard_map.87), channel_id=1, source_target_pairs={{1,0},{16,1},{17,16},{32,17},{33,32},{48,33},{49,48},{52,49},{53,5... | collective-permute-start | bytes 1572872 | tf_op jit(solution)/shard_map/ppermute | solution.py:368
  78.1 3.7 %collective-permute-done.9.above = f32[2,4,2,4,16,128]{5,4,3,2,1,0:T(8,128)S(1)} collective-permute-done((f32[2,4,2,4,16,128]{5,4,3,2,1,0:T(8,128)S(1)}, f32[2,4,2,4,16,128]{5,4,3,2,1,0:T(8,128)S(1)}, u32[]{:S(2)}, u32[]{:S(2)}) %collective-permute-start.9) | collective-permute-done | bytes 524320 | tf_op jit(solution)/shard_map/ppermute | solution.py:368
  81.8 2.7 %shard_map.83.refs_5_.refs_1_.refs_4_.refs_6_.refs_2_ = f32[2,4,2,4,16,128]{5,4,3,2,1,0:T(8,128)S(1)} custom-call(f32[8,10,2,4,16,128]{5,4,3,2,1,0:T(8,128)S(1)} %shard_map.79.coef.refs_0_.order, f32[4,2,4,16,128]{4,3,2,1,0:T(8,128)S(1)} %get-tuple-element.25.force, f32[2,3,2,4,16,128]{5,4,3,2,1,0:T(8,128)S(1)} %collective-permute-done.below.edge_below, ...), custom_call_target="tpu_custom_call" | custom-call | bytes 1024 | tf_op jit(solution)/shard_map/pallas_call | solution.py:48
  84.5 2.7 %shard_map.85.refs_6_.refs_2_.refs_5_.refs_7_.refs_3_ = f32[2,4,2,4,16,128]{5,4,3,2,1,0:T(8,128)S(1)} custom-call(f32[8,10,2,4,16,128]{5,4,3,2,1,0:T(8,128)S(1)} %shard_map.79.coef.refs_0_.order, f32[4,2,4,16,128]{4,3,2,1,0:T(8,128)S(1)} %get-tuple-element.25.force, f32[2,3,2,4,16,128]{5,4,3,2,1,0:T(8,128)S(1)} %collective-permute-done.below.edge_below, ...), custom_call_target="tpu_custom_call" | custom-call | bytes 1024 | tf_op jit(solution)/shard_map/pallas_call | solution.py:48
  87.2 1.1 shard_map.86
  89.5 2.7 %shard_map.88 = (f32[1,4,2,4,16,128]{5,4,3,2,1,0:T(8,128)S(1)}, f32[1,4,2,4,16,128]{5,4,3,2,1,0:T(8,128)S(1)}) custom-call(f32[8,10,2,4,16,128]{5,4,3,2,1,0:T(8,128)S(1)} %shard_map.79.coef.refs_0_.order, f32[4,2,4,16,128]{4,3,2,1,0:T(8,128)S(1)} %get-tuple-element.25.force, f32[2,3,2,4,16,128]{5,4,3,2,1,0:T(8,128)S(1)} %collective-permute-done.below.edge_below, ...), custom_call_target="tpu_custom_call" | custom-call | bytes 1024 | tf_op jit(solution)/shard_map/pallas_call | solution.py:48
  92.2 1.3 collective-permute-start.15
  93.5 0.9 collective-permute-done.11.above
  94.4 0.9 shard_map.89
  95.4 1.3 collective-permute-start.14
  96.7 4.2 %collective-permute-done.15.beyond = f32[1,4,2,4,16,128]{5,4,3,2,1,0:T(8,128)S(1)} collective-permute-done((f32[1,4,2,4,16,128]{5,4,3,2,1,0:T(8,128)S(1)}, f32[1,4,2,4,16,128]{5,4,3,2,1,0:T(8,128)S(1)}, u32[]{:S(2)}, u32[]{:S(2)}) %collective-permute-start.15) | collective-permute-done | bytes 262176 | tf_op jit(solution)/shard_map/ppermute | solution.py:449
  101.4 5.0 %collective-permute-done.14.refs_1_ = f32[1,4,2,4,16,128]{5,4,3,2,1,0:T(8,128)S(1)} collective-permute-done((f32[1,4,2,4,16,128]{5,4,3,2,1,0:T(8,128)S(1)}, f32[1,4,2,4,16,128]{5,4,3,2,1,0:T(8,128)S(1)}, u32[]{:S(2)}, u32[]{:S(2)}) %collective-permute-start.14) | collective-permute-done | bytes 262176 | tf_op jit(solution)/shard_map/ppermute | solution.py:450
  106.9 3.3 %collective-permute-start.16 = (f32[4,2,4,16,128]{4,3,2,1,0:T(8,128)S(1)}, f32[4,2,4,16,128]{4,3,2,1,0:T(8,128)S(1)}, u32[]{:S(2)}, u32[]{:S(2)}) collective-permute-start(f32[4,2,4,16,128]{4,3,2,1,0:T(8,128)S(1)} %get-tuple-element.37), channel_id=1, source_target_pairs={{0,1},{1,16},{16,17},{17,32},{32,33},{33,48},{48,49},{49,52},{52,5... | collective-permute-start | bytes 786440 | tf_op jit(solution)/shard_map/ppermute | solution.py:368
  110.3 3.3 %collective-permute-done.16.refs_2_ = f32[4,2,4,16,128]{4,3,2,1,0:T(8,128)S(1)} collective-permute-done((f32[4,2,4,16,128]{4,3,2,1,0:T(8,128)S(1)}, f32[4,2,4,16,128]{4,3,2,1,0:T(8,128)S(1)}, u32[]{:S(2)}, u32[]{:S(2)}) %collective-permute-start.16) | collective-permute-done | bytes 262176 | tf_op jit(solution)/shard_map/ppermute | solution.py:368
  113.6 2.5 %collective-permute-done.17.refs_3_ = f32[4,2,4,16,128]{4,3,2,1,0:T(8,128)S(1)} collective-permute-done((f32[4,2,4,16,128]{4,3,2,1,0:T(8,128)S(1)}, f32[4,2,4,16,128]{4,3,2,1,0:T(8,128)S(1)}, u32[]{:S(2)}, u32[]{:S(2)}) %collective-permute-start.17) | collective-permute-done | bytes 262176 | tf_op jit(solution)/shard_map/ppermute | solution.py:368
  116.0 1.3 shard_map.92
  118.0 1.8 shard_map.93.given
  119.8 0.9 shard_map.94.refs_5_
  120.8 2.6 %collective-permute-done.19.above = f32[4,2,4,16,128]{4,3,2,1,0:T(8,128)S(1)} collective-permute-done((f32[4,2,4,16,128]{4,3,2,1,0:T(8,128)S(1)}, f32[4,2,4,16,128]{4,3,2,1,0:T(8,128)S(1)}, u32[]{:S(2)}, u32[]{:S(2)}) %collective-permute-start.19) | collective-permute-done | bytes 262176 | tf_op jit(solution)/shard_map/ppermute | solution.py:368
  123.3 1.7 shard_map.95
  125.1 57.4 %all_to_all.11.recv = f32[64,16,8,128]{3,2,1,0:T(8,128)S(1)} all-to-all(f32[64,16,8,128]{3,2,1,0:T(8,128)S(1)} %shard_map.95), channel_id=1, replica_groups=mesh['xh'=2,'y'=4,'space'=16] {'y','space'}, dimensions={0} | all-to-all | bytes 8388608 | tf_op jit(solution)/shard_map/all_to_all | solution.py:468
  182.5 2.9 %shard_map.96 = (f32[2,2,256,512]{3,2,1,0:T(8,128)}, f32[2,2,256,512]{3,2,1,0:T(8,128)}) custom-call(s32[2]{0:T(128)S(1)} %copy-done.1, f32[64,16,8,128]{3,2,1,0:T(8,128)S(1)} %all_to_all.11.recv, f32[2,2,256,512]{3,2,1,0:T(8,128)S(1)} %copy-done), custom_call_target="tpu_custom_call" | custom-call | tf_op jit(solution)/shard_map/pallas_call | solution.py:470
  (39 shorter events, 5.8 us)
Async XLA Ops:
  54.0 8.1 %copy-start.2 = (f32[3,8]{1,0:T(4,128)S(1)}, f32[3,8]{1,0:T(4,128)}, u32[]{:S(2)}) copy-start(f32[3,8]{1,0:T(4,128)} %drift.1) | copy-start | bytes 292
  54.0 8.1 %copy-start.3 = (f32[8]{0:T(128)S(1)}, f32[8]{0:T(128)}, u32[]{:S(2)}) copy-start(f32[8]{0:T(128)} %diffusion.1) | copy-start | bytes 100
  54.1 5.2 %collective-permute-start = (f32[2,3,2,4,16,128]{5,4,3,2,1,0:T(8,128)S(1)}, f32[2,3,2,4,16,128]{5,4,3,2,1,0:T(8,128)S(1)}, u32[]{:S(2)}, u32[]{:S(2)}) collective-permute-start(f32[2,3,2,4,16,128]{5,4,3,2,1,0:T(8,128)S(1)} %get-tuple-element.23), channel_id=1, source_target_pairs={{0,1},{1,16},{16,17},{17,32},{32,33},{33,48},{48,49},{49,52},{52,5... | collective-permute-start | bytes 1179656 | tf_op jit(solution)/shard_map/ppermute | solution.py:368
  54.6 7.5 %collective-permute-start.1 = (f32[2,3,2,4,16,128]{5,4,3,2,1,0:T(8,128)S(1)}, f32[2,3,2,4,16,128]{5,4,3,2,1,0:T(8,128)S(1)}, u32[]{:S(2)}, u32[]{:S(2)}) collective-permute-start(f32[2,3,2,4,16,128]{5,4,3,2,1,0:T(8,128)S(1)} %get-tuple-element.24.order), channel_id=1, source_target_pairs={{1,0},{16,1},{17,16},{32,17},{33,32},{48,33},{49,48},{52,49},{53,5... | collective-permute-start | bytes 1179656 | tf_op jit(solution)/shard_map/ppermute | solution.py:368
  55.2 15.3 %collective-permute-start.3 = (f32[3,4,2,4,16,128]{5,4,3,2,1,0:T(8,128)S(1)}, f32[3,4,2,4,16,128]{5,4,3,2,1,0:T(8,128)S(1)}, u32[]{:S(2)}, u32[]{:S(2)}) collective-permute-start(f32[3,4,2,4,16,128]{5,4,3,2,1,0:T(8,128)S(1)} %get-tuple-element.26.starts.refs_0_), channel_id=1, source_target_pairs={{1,0},{16,1},{17,16},{32,17},{33,32},{48,33},{49,48},{52,49},{53,5... | collective-permute-start | bytes 2359304 | tf_op jit(solution)/shard_map/ppermute | solution.py:368
  56.9 13.6 %collective-permute-start.2 = (f32[3,4,2,4,16,128]{5,4,3,2,1,0:T(8,128)S(1)}, f32[3,4,2,4,16,128]{5,4,3,2,1,0:T(8,128)S(1)}, u32[]{:S(2)}, u32[]{:S(2)}) collective-permute-start(f32[3,4,2,4,16,128]{5,4,3,2,1,0:T(8,128)S(1)} %get-tuple-element.26.starts.refs_0_), channel_id=1, source_target_pairs={{0,1},{1,16},{16,17},{17,32},{32,33},{33,48},{48,49},{49,52},{52,5... | collective-permute-start | bytes 2359304 | tf_op jit(solution)/shard_map/ppermute | solution.py:368
  57.0 19.1 %collective-permute-start.7 = (f32[2,4,2,4,16,128]{5,4,3,2,1,0:T(8,128)S(1)}, f32[2,4,2,4,16,128]{5,4,3,2,1,0:T(8,128)S(1)}, u32[]{:S(2)}, u32[]{:S(2)}) collective-permute-start(f32[2,4,2,4,16,128]{5,4,3,2,1,0:T(8,128)S(1)} %get-tuple-element.27.refs_0_.starts), channel_id=1, source_target_pairs={{1,0},{16,1},{17,16},{32,17},{33,32},{48,33},{49,48},{52,49},{53,5... | collective-permute-start | bytes 1572872 | tf_op jit(solution)/shard_map/ppermute | solution.py:368
  59.3 16.9 %collective-permute-start.6 = (f32[2,4,2,4,16,128]{5,4,3,2,1,0:T(8,128)S(1)}, f32[2,4,2,4,16,128]{5,4,3,2,1,0:T(8,128)S(1)}, u32[]{:S(2)}, u32[]{:S(2)}) collective-permute-start(f32[2,4,2,4,16,128]{5,4,3,2,1,0:T(8,128)S(1)} %get-tuple-element.27.refs_0_.starts), channel_id=1, source_target_pairs={{0,1},{1,16},{16,17},{17,32},{32,33},{33,48},{48,49},{49,52},{52,5... | collective-permute-start | bytes 1572872 | tf_op jit(solution)/shard_map/ppermute | solution.py:368
  65.6 16.2 %collective-permute-start.9 = (f32[2,4,2,4,16,128]{5,4,3,2,1,0:T(8,128)S(1)}, f32[2,4,2,4,16,128]{5,4,3,2,1,0:T(8,128)S(1)}, u32[]{:S(2)}, u32[]{:S(2)}) collective-permute-start(f32[2,4,2,4,16,128]{5,4,3,2,1,0:T(8,128)S(1)} %shard_map.84), channel_id=1, source_target_pairs={{1,0},{16,1},{17,16},{32,17},{33,32},{48,33},{49,48},{52,49},{53,5... | collective-permute-start | bytes 1572872 | tf_op jit(solution)/shard_map/ppermute | solution.py:368
  70.5 13.9 %collective-permute-start.8 = (f32[2,4,2,4,16,128]{5,4,3,2,1,0:T(8,128)S(1)}, f32[2,4,2,4,16,128]{5,4,3,2,1,0:T(8,128)S(1)}, u32[]{:S(2)}, u32[]{:S(2)}) collective-permute-start(f32[2,4,2,4,16,128]{5,4,3,2,1,0:T(8,128)S(1)} %shard_map.84), channel_id=1, source_target_pairs={{0,1},{1,16},{16,17},{17,32},{32,33},{33,48},{48,49},{49,52},{52,5... | collective-permute-start | bytes 1572872 | tf_op jit(solution)/shard_map/ppermute | solution.py:368
  74.9 12.2 %collective-permute-start.4 = (f32[3,2,4,16,128]{4,3,2,1,0:T(8,128)S(1)}, f32[3,2,4,16,128]{4,3,2,1,0:T(8,128)S(1)}, u32[]{:S(2)}, u32[]{:S(2)}) collective-permute-start(f32[3,2,4,16,128]{4,3,2,1,0:T(8,128)S(1)} %get-tuple-element.28), channel_id=1, source_target_pairs={{0,1},{1,16},{16,17},{17,32},{32,33},{33,48},{48,49},{49,52},{52,5... | collective-permute-start | bytes 589832 | tf_op jit(solution)/shard_map/ppermute | solution.py:368
  76.2 11.0 %collective-permute-start.5 = (f32[3,2,4,16,128]{4,3,2,1,0:T(8,128)S(1)}, f32[3,2,4,16,128]{4,3,2,1,0:T(8,128)S(1)}, u32[]{:S(2)}, u32[]{:S(2)}) collective-permute-start(f32[3,2,4,16,128]{4,3,2,1,0:T(8,128)S(1)} %get-tuple-element.29.refs_1_.order), channel_id=1, source_target_pairs={{1,0},{16,1},{17,16},{32,17},{33,32},{48,33},{49,48},{52,49},{53,5... | collective-permute-start | bytes 589832 | tf_op jit(solution)/shard_map/ppermute | solution.py:368
  76.2 13.3 %collective-permute-start.13 = (f32[2,4,2,4,16,128]{5,4,3,2,1,0:T(8,128)S(1)}, f32[2,4,2,4,16,128]{5,4,3,2,1,0:T(8,128)S(1)}, u32[]{:S(2)}, u32[]{:S(2)}) collective-permute-start(f32[2,4,2,4,16,128]{5,4,3,2,1,0:T(8,128)S(1)} %shard_map.87), channel_id=1, source_target_pairs={{1,0},{16,1},{17,16},{32,17},{33,32},{48,33},{49,48},{52,49},{53,5... | collective-permute-start | bytes 1572872 | tf_op jit(solution)/shard_map/ppermute | solution.py:368
  81.8 7.7 %collective-permute-start.12 = (f32[2,4,2,4,16,128]{5,4,3,2,1,0:T(8,128)S(1)}, f32[2,4,2,4,16,128]{5,4,3,2,1,0:T(8,128)S(1)}, u32[]{:S(2)}, u32[]{:S(2)}) collective-permute-start(f32[2,4,2,4,16,128]{5,4,3,2,1,0:T(8,128)S(1)} %shard_map.87), channel_id=1, source_target_pairs={{0,1},{1,16},{16,17},{17,32},{32,33},{33,48},{48,49},{49,52},{52,5... | collective-permute-start | bytes 1572872 | tf_op jit(solution)/shard_map/ppermute | solution.py:368
  88.2 5.2 %collective-permute-start.10 = (f32[4,2,4,16,128]{4,3,2,1,0:T(8,128)S(1)}, f32[4,2,4,16,128]{4,3,2,1,0:T(8,128)S(1)}, u32[]{:S(2)}, u32[]{:S(2)}) collective-permute-start(f32[4,2,4,16,128]{4,3,2,1,0:T(8,128)S(1)} %get-tuple-element.33), channel_id=1, source_target_pairs={{0,1},{1,16},{16,17},{17,32},{32,33},{33,48},{48,49},{49,52},{52,5... | collective-permute-start | bytes 786440 | tf_op jit(solution)/shard_map/ppermute | solution.py:368
  88.6 5.8 %collective-permute-start.11 = (f32[4,2,4,16,128]{4,3,2,1,0:T(8,128)S(1)}, f32[4,2,4,16,128]{4,3,2,1,0:T(8,128)S(1)}, u32[]{:S(2)}, u32[]{:S(2)}) collective-permute-start(f32[4,2,4,16,128]{4,3,2,1,0:T(8,128)S(1)} %get-tuple-element.34.refs_1_), channel_id=1, source_target_pairs={{1,0},{16,1},{17,16},{32,17},{33,32},{48,33},{49,48},{52,49},{53,5... | collective-permute-start | bytes 786440 | tf_op jit(solution)/shard_map/ppermute | solution.py:368
  92.2 8.6 %collective-permute-start.15 = (f32[1,4,2,4,16,128]{5,4,3,2,1,0:T(8,128)S(1)}, f32[1,4,2,4,16,128]{5,4,3,2,1,0:T(8,128)S(1)}, u32[]{:S(2)}, u32[]{:S(2)}) collective-permute-start(f32[1,4,2,4,16,128]{5,4,3,2,1,0:T(8,128)S(1)} %get-tuple-element.36), channel_id=1, source_target_pairs={{0,66},{1,67},{2,64},{3,65},{4,70},{5,71},{6,68},{7,69},{8,74},{9,... | collective-permute-start | bytes 786440 | tf_op jit(solution)/shard_map/ppermute | solution.py:449
  94.4 6.4 %copy-start.1 = (s32[2]{0:T(128)S(1)}, s32[2]{0:T(128)}, u32[]{:S(2)}) copy-start(s32[2]{0:T(128)} %pad_add_fusion.at_ref) | copy-start | bytes 28
  95.4 11.1 %collective-permute-start.14 = (f32[1,4,2,4,16,128]{5,4,3,2,1,0:T(8,128)S(1)}, f32[1,4,2,4,16,128]{5,4,3,2,1,0:T(8,128)S(1)}, u32[]{:S(2)}, u32[]{:S(2)}) collective-permute-start(f32[1,4,2,4,16,128]{5,4,3,2,1,0:T(8,128)S(1)} %shard_map.89), channel_id=1, source_target_pairs={{0,66},{1,67},{2,64},{3,65},{4,70},{5,71},{6,68},{7,69},{8,74},{9,... | collective-permute-start | bytes 786440 | tf_op jit(solution)/shard_map/ppermute | solution.py:450
  106.9 6.7 %collective-permute-start.16 = (f32[4,2,4,16,128]{4,3,2,1,0:T(8,128)S(1)}, f32[4,2,4,16,128]{4,3,2,1,0:T(8,128)S(1)}, u32[]{:S(2)}, u32[]{:S(2)}) collective-permute-start(f32[4,2,4,16,128]{4,3,2,1,0:T(8,128)S(1)} %get-tuple-element.37), channel_id=1, source_target_pairs={{0,1},{1,16},{16,17},{17,32},{32,33},{33,48},{48,49},{49,52},{52,5... | collective-permute-start | bytes 786440 | tf_op jit(solution)/shard_map/ppermute | solution.py:368
  110.3 5.8 %collective-permute-start.17 = (f32[4,2,4,16,128]{4,3,2,1,0:T(8,128)S(1)}, f32[4,2,4,16,128]{4,3,2,1,0:T(8,128)S(1)}, u32[]{:S(2)}, u32[]{:S(2)}) collective-permute-start(f32[4,2,4,16,128]{4,3,2,1,0:T(8,128)S(1)} %get-tuple-element.38.order), channel_id=1, source_target_pairs={{1,0},{16,1},{17,16},{32,17},{33,32},{48,33},{49,48},{52,49},{53,5... | collective-permute-start | bytes 786440 | tf_op jit(solution)/shard_map/ppermute | solution.py:368
  117.4 3.4 %collective-permute-start.18 = (f32[4,2,4,16,128]{4,3,2,1,0:T(8,128)S(1)}, f32[4,2,4,16,128]{4,3,2,1,0:T(8,128)S(1)}, u32[]{:S(2)}, u32[]{:S(2)}) collective-permute-start(f32[4,2,4,16,128]{4,3,2,1,0:T(8,128)S(1)} %get-tuple-element.40), channel_id=1, source_target_pairs={{0,1},{1,16},{16,17},{17,32},{32,33},{33,48},{48,49},{49,52},{52,5... | collective-permute-start | bytes 786440 | tf_op jit(solution)/shard_map/ppermute | solution.py:368
  117.5 5.9 %collective-permute-start.19 = (f32[4,2,4,16,128]{4,3,2,1,0:T(8,128)S(1)}, f32[4,2,4,16,128]{4,3,2,1,0:T(8,128)S(1)}, u32[]{:S(2)}, u32[]{:S(2)}) collective-permute-start(f32[4,2,4,16,128]{4,3,2,1,0:T(8,128)S(1)} %get-tuple-element.41), channel_id=1, source_target_pairs={{1,0},{16,1},{17,16},{32,17},{33,32},{48,33},{49,48},{52,49},{53,5... | collective-permute-start | bytes 786440 | tf_op jit(solution)/shard_map/ppermute | solution.py:368
  125.1 57.4 %copy-start = (f32[2,2,256,512]{3,2,1,0:T(8,128)S(1)}, f32[2,2,256,512]{3,2,1,0:T(8,128)}, u32[]{:S(2)}) copy-start(f32[2,2,256,512]{3,2,1,0:T(8,128)} %field.1) | copy-start | bytes 6291460
